TPU v7x, 32 devices: a whole 2x2x4 slice. The times are simulated.
32 devices in a mesh: dp: 4 (over x, core), atom: 8 (over z, y).
Axes of the slice: x: 2, y: 2, z: 4, core: 2. Of those that a mesh axis runs over, the one named last changes fastest.
Arguments:
- frac: float32 [3, 4096], P(None, ('dp', 'atom')), may hold values from 0 to 1, as said below
- species: int32 [4096], P(('dp', 'atom')), may hold values from 0 to 95
- neighbours: int32 [32, 4096], P(None, ('dp', 'atom')), may hold values from 0 to 191, as said below
- counts: int32 [4096], P(('dp', 'atom')), may hold values from 8 to 32, as said below
- shifts: int32 [3, 32, 4096], P(None, None, ('dp', 'atom')), may hold values from -1 to 1, as said below
- cell: float32 [4, 3, 3], P('dp'), may hold values from -0.4 to 211.2, as said below
- energy_ref: float32 [4], P('dp'), may hold values from -4 to 4
- embedding: float32 [96, 128], replicated, may hold values from -6 to 6
- radial_in: float32 [2, 64, 128], replicated, may hold values from -1.5 to 1.5
- radial_out: float32 [2, 128, 384], replicated, may hold values from -0.5 to 0.5
- scalar_mix: float32 [2, 128, 128], replicated, may hold values from -0.5 to 0.5
- vector_mix: float32 [2, 128, 128], replicated, may hold values from -0.5 to 0.5
- vector_gate: float32 [2, 128, 128], replicated, may hold values from -0.5 to 0.5
- readout_mid: float32 [128, 128], replicated, may hold values from -0.5 to 0.5
- readout_out: float32 [128], replicated, may hold values from -0.5 to 0.5
Outputs:
- energy: float32 [4], P('dp')
- forces: float32 [3, 4096], P(None, ('dp', 'atom'))
- stress: float32 [4, 3, 3], P('dp')
- embedding_grad: float32 [96, 128], replicated
- radial_in_grad: float32 [2, 64, 128], replicated
- radial_out_grad: float32 [2, 128, 384], replicated
- scalar_mix_grad: float32 [2, 128, 128], replicated
- vector_mix_grad: float32 [2, 128, 128], replicated
- vector_gate_grad: float32 [2, 128, 128], replicated
- readout_mid_grad: float32 [128, 128], replicated
- readout_out_grad: float32 [128], replicated
Inputs may be any that keep to these rules, and one draw needn't show every extreme that they name: `frac`: each fractional coordinate of slab p's atoms along the first lattice vector lies in [p / 8, (p + 1) / 8); the other two lie in [0, 1). `neighbours`: A window row; atom i (local index within its slab) names rows i to i + 64 only. In every slab, slot 0 of the first atom names row 0 and slot 0 of the last atom names row 191. `counts`: in every slab the first atom has 32 used slots and the second 32 // 4. `shifts`: the first component is -1 exactly where slab 0 names a row below 32, +1 exactly where the last slab names a row from 160 on, else 0. `cell`: diagonal entries near 24 * 8, 12 and 12; off-diagonal entries small against them, so the determinant is positive.
All inputs are finite; a program needn't handle non-finite values.
Results may differ from a plain program's by a relative error of at most 0.0003.
Values sent between devices are 32-bit elements; how exact they have to be, the bound alone decides.
No kernel may reach another device: no remote copies, remote signals or barrier semaphores. Data moves between devices by JAX's collectives and lax.ppermute only.
A program may use at most 64 MiB of HBM per device.

v0:
```python
import jax
import jax.numpy as jnp
from jax import lax
from jax.sharding import PartitionSpec as P

BLOCK = 32


HIGH = lax.Precision.HIGHEST


def shifted(block, axis, distance):
    devices = range(lax.axis_size(axis))
    route = [((i - distance) % len(devices), i) for i in devices]
    return lax.ppermute(block, axis, route)


def extended_2(x, sides, width):
    for axis, dim in sides:
        size, length = (lax.axis_size(axis), x.shape[dim])
        up = [(i, (i + 1) % size) for i in range(size)]
        down = [(j, i) for i, j in up]
        last = lax.slice_in_dim(x, length - width, length, axis=dim)
        initial = lax.slice_in_dim(x, 0, width, axis=dim)
        before = lax.ppermute(last, axis, up)
        after = lax.ppermute(initial, axis, down)
        x = jnp.concatenate([before, x, after], axis=dim)
    return x


def edge_geometry(window_pos, neighbour_rows, image_shifts, lattice):
    atom_count = neighbour_rows.shape[1]
    halo_rows = (window_pos.shape[1] - atom_count) // 2
    far_end = jnp.take(window_pos, neighbour_rows, axis=1)
    near_end = window_pos[:, halo_rows : halo_rows + atom_count]
    image = jnp.einsum("akb,ac->ckb", image_shifts, lattice, precision=HIGH)
    return far_end - near_end[:, None, :] + image


def interact(layer_set, wide_rows, edge_set, neighbour_rows, slot_mask):
    radial_in, radial_out, scalar_mix, vector_mix, vector_gate = layer_set
    slot_count, atom_count = neighbour_rows.shape
    halo_rows = (wide_rows.shape[0] - atom_count) // 2
    block_count = atom_count // BLOCK
    width = wide_rows.shape[2]
    own_rows = wide_rows[halo_rows : halo_rows + atom_count]
    block_inputs = (
        neighbour_rows.reshape(slot_count, block_count, BLOCK).transpose(1, 0, 2),
        edge_set.reshape(3, slot_count, block_count, BLOCK).transpose(2, 0, 1, 3),
        slot_mask.reshape(slot_count, block_count, BLOCK).transpose(1, 0, 2),
        own_rows.reshape(block_count, BLOCK, own_rows.shape[1], width),
    )
    scale = slot_count ** (-0.5)
    basis_count = radial_in.shape[0]
    centres = 8.0 * jnp.arange(basis_count, dtype=jnp.float32) / (basis_count - 1)
    sharpness = 0.5 * ((basis_count - 1) / 8.0) ** 2

    def one_block(inputs):
        rows, vectors, block_mask, own = inputs
        distance = jnp.sqrt(jnp.sum(vectors * vectors, axis=0) + 1.0)
        direction = vectors / distance
        radial_basis = jnp.exp(-sharpness * (distance[..., None] - centres) ** 2)
        hidden = jax.nn.silu(jnp.einsum("kbn,nc->kbc", radial_basis, radial_in, precision=HIGH))
        filters = (
            jnp.einsum("kbc,cd->kbd", hidden, radial_out, precision=HIGH) * block_mask[..., None]
        )
        filter_scalar = filters[..., :width]
        filter_vector = filters[..., width : 2 * width]
        filter_direction = filters[..., 2 * width :]
        gathered = jnp.take(wide_rows, rows, axis=0)
        neighbour_scalar = gathered[:, :, 0, :]
        summed_scalar = jnp.sum(filter_scalar * neighbour_scalar, axis=0) * scale
        message = (filter_direction * neighbour_scalar)[:, :, None, :] * direction.transpose(
            1, 2, 0
        )[..., None]
        if gathered.shape[2] > 1:
            message = message + filter_vector[:, :, None, :] * gathered[:, :, 1:, :]
        summed_vector = jnp.sum(message, axis=0) * scale
        mixed_vector = jnp.einsum("bjc,cd->bjd", summed_vector, vector_mix, precision=HIGH)
        magnitude = jnp.sqrt(jnp.sum(mixed_vector * mixed_vector, axis=1) + 1.0) - 1.0
        new_scalar = own[:, 0, :] + jax.nn.silu(
            jnp.dot(summed_scalar, scalar_mix, precision=HIGH) + magnitude
        )
        gate = jax.nn.sigmoid(jnp.dot(summed_scalar, vector_gate, precision=HIGH))
        if own.shape[1] > 1:
            old_vector = own[:, 1:, :]
        else:
            old_vector = jnp.zeros(mixed_vector.shape, jnp.float32)
        new_vector = old_vector + mixed_vector * gate[:, None, :]
        return jnp.concatenate([new_scalar[:, None, :], new_vector], axis=1)

    result = lax.map(jax.checkpoint(one_block), block_inputs)
    return result.reshape(atom_count, 4, width)


def readout(readout_mid, readout_out, features):
    hidden = jax.nn.silu(jnp.dot(features[:, 0, :], readout_mid, precision=HIGH))
    return jnp.sum(jnp.dot(hidden, readout_out, precision=HIGH))


def determinant(lattice):
    return (
        lattice[0, 0] * (lattice[1, 1] * lattice[2, 2] - lattice[1, 2] * lattice[2, 1])
        - lattice[0, 1] * (lattice[1, 0] * lattice[2, 2] - lattice[1, 2] * lattice[2, 0])
        + lattice[0, 2] * (lattice[1, 0] * lattice[2, 1] - lattice[1, 1] * lattice[2, 0])
    )


def send_back(cotangent, axis, halo_rows):
    size = cotangent.shape[axis]
    atom_count = size - 2 * halo_rows
    lower_rows = lax.slice_in_dim(cotangent, 0, halo_rows, axis=axis)
    upper_rows = lax.slice_in_dim(cotangent, size - halo_rows, size, axis=axis)
    middle = lax.slice_in_dim(cotangent, halo_rows, halo_rows + atom_count, axis=axis)
    from_above = shifted(lower_rows, "atom", -1)
    from_below = shifted(upper_rows, "atom", 1)
    head = lax.slice_in_dim(middle, 0, halo_rows, axis=axis) + from_below
    centre = lax.slice_in_dim(middle, halo_rows, atom_count - halo_rows, axis=axis)
    tail = lax.slice_in_dim(middle, atom_count - halo_rows, atom_count, axis=axis) + from_above
    return jnp.concatenate([head, centre, tail], axis=axis)


def local(
    frac,
    species,
    neighbours,
    counts,
    shifts,
    cell,
    energy_ref,
    embedding,
    radial_in,
    radial_out,
    scalar_mix,
    vector_mix,
    vector_gate,
    readout_mid,
    readout_out,
):
    atom_count = frac.shape[1]
    halo_rows = atom_count // 4
    slot_count = neighbours.shape[0]
    lattice = cell[0]
    positions = jnp.dot(lattice.T, frac, precision=HIGH)
    window_pos = extended_2(positions, (("atom", 1),), halo_rows)
    image_shifts = shifts.astype(jnp.float32)
    edge_set, pull_edges = jax.vjp(
        lambda place: edge_geometry(place, neighbours, image_shifts, lattice), window_pos
    )
    slot_mask = (
        lax.broadcasted_iota(jnp.int32, (slot_count, atom_count), 0) < counts[None, :]
    ).astype(jnp.float32)
    one_hot = (
        species[:, None] == lax.broadcasted_iota(jnp.int32, (1, embedding.shape[0]), 1)
    ).astype(jnp.float32)
    features = jnp.dot(one_hot, embedding, precision=HIGH)[:, None, :]
    pulls = []
    for layer_index in range(radial_in.shape[0]):
        extended = extended_2(features, (("atom", 0),), halo_rows)
        layer_set = (
            radial_in[layer_index],
            radial_out[layer_index],
            scalar_mix[layer_index],
            vector_mix[layer_index],
            vector_gate[layer_index],
        )
        features, pull_back = jax.vjp(
            lambda weight_group, wide_rows, edge_group: interact(
                weight_group, wide_rows, edge_group, neighbours, slot_mask
            ),
            layer_set,
            extended,
            edge_set,
        )
        pulls.append(pull_back)
    energy_part, pull_out = jax.vjp(readout, readout_mid, readout_out, features)
    grad_mid, grad_out, cotangent = pull_out(jnp.ones((), jnp.float32))
    edge_cotangent = jnp.zeros(edge_set.shape, jnp.float32)
    layer_grads = []
    for pull_back in reversed(pulls):
        grad_layer, wide_cotangent, edge_part = pull_back(cotangent)
        edge_cotangent = edge_cotangent + edge_part
        cotangent = send_back(wide_cotangent, 0, halo_rows)
        layer_grads.insert(0, grad_layer)
    grad_embedding = jnp.dot(one_hot.T, cotangent[:, 0, :], precision=HIGH)
    window_cotangent = pull_edges(edge_cotangent)[0]
    forces = -send_back(window_cotangent, 1, halo_rows)
    virial = jnp.einsum("akb,ckb->ac", edge_set, edge_cotangent, precision=HIGH)
    energy_total, virial_total = lax.psum((energy_part, virial), "atom")
    stress = (virial_total / determinant(lattice))[None]
    cell_atoms = atom_count * lax.axis_size("atom")
    loss_scale = 2.0 * (energy_total / cell_atoms - energy_ref[0]) / cell_atoms
    stacked = tuple((jnp.stack([g[kind] for g in layer_grads]) for kind in range(5)))
    local_grads = (grad_embedding,) + stacked + (grad_mid, grad_out)
    scaled = tuple((g * loss_scale for g in local_grads))
    summed = lax.psum(
        (scaled[0], scaled[1], scaled[2], scaled[3], scaled[4], scaled[5], scaled[6], scaled[7]),
        ("dp", "atom"),
    )
    return (
        energy_total.reshape(1),
        forces,
        stress,
        summed[0],
        summed[1],
        summed[2],
        summed[3],
        summed[4],
        summed[5],
        summed[6],
        summed[7],
    )


def solution(mesh):
    return jax.shard_map(
        local,
        mesh=mesh,
        in_specs=(
            P(None, ("dp", "atom")),
            P(("dp", "atom")),
            P(None, ("dp", "atom")),
            P(("dp", "atom")),
            P(None, None, ("dp", "atom")),
            P("dp", None, None),
            P("dp"),
            P(),
            P(),
            P(),
            P(),
            P(),
            P(),
            P(),
            P(),
        ),
        out_specs=(
            P("dp"),
            P(None, ("dp", "atom")),
            P("dp", None, None),
            P(),
            P(),
            P(),
            P(),
            P(),
            P(),
            P(),
            P(),
        ),
        check_vma=False,
    )
```

profile of v0, /device:TPU:0, one launch (start us, length us, event | category | flops | bytes accessed | tf_op | source)
XLA Modules:
  0.0 715.9 jit_solution(5302295964521520347)
XLA Ops:
  8.3 3.0 collective-permute-start
  11.3 3.1 collective-permute-start.1
  15.5 4.7 collective-permute-start.3
  27.0 10.8 %gather_fusion.4 = f32[4096,3]{1,0:T(8,128)S(1)} fusion(f32[3,192]{0,1:T(8,128)S(1)} %copy.120, s32[4096]{0:T(1024)S(1)} %broadcast_clamp_fusion.4), kind=kCustom, calls=%fused_computation.4 | custom fusion | bytes 114688 | tf_op jit(solution)/shard_map/jvp(jit(_take))/gather | solution.py:34
  40.6 32.2 %while.84 = (s32[]{:T(128)}, f32[4,32,4,128]{3,1,2,0:T(8,128)}, f32[4,32,1,128]{3,1,2,0:T(8,128)S(1)}, f32[4,3,32,32]{3,2,1,0:T(8,128)S(1)}, f32[64,128]{1,0:T(8...) while((s32[]{:T(128)}, f32[4,32,4,128]{3,1,2,0:T(8,128)}, ...), condition=%wide.region_5.6_spmd.clone, body=%wide.region_0.5_spmd.clone.sunk | while | flops 738774080 | bytes 7810197 | solution.py:92
  43.9 2.8 gather_fusion
  51.9 2.8 gather_fusion
  59.9 2.8 gather_fusion
  68.0 2.8 gather_fusion
  74.0 4.7 collective-permute-start.5
  81.8 36.9 %while.85 = (s32[]{:T(128)}, f32[4,32,4,128]{3,1,0,2:T(8,128)}, f32[4,32,4,128]{3,1,2,0:T(8,128)}, f32[4,3,32,32]{3,2,1,0:T(8,128)S(1)}, f32[64,128]{1,0:T(8,128...) while((s32[]{:T(128)}, f32[4,32,4,128]{3,1,0,2:T(8,128)}, ...), condition=%wide.region_11.12_spmd.clone, body=%wide.region_6.11_spmd.clone.sunk | while | flops 739834944 | bytes 22908080 | solution.py:92
  81.9 3.6 gather_fusion.1
  91.1 3.6 gather_fusion.1
  100.4 3.6 gather_fusion.1
  109.6 3.6 gather_fusion.1
  122.2 249.8 %while.86 = (s32[]{:T(128)}, f32[64,128]{1,0:T(8,128)}, f32[128,384]{1,0:T(8,128)}, f32[192,4,128]{2,1,0:T(4,128)S(1)}, f32[128,128]{1,0:T(8,128)}, /*index=5*/f...) while((s32[]{:T(128)}, f32[64,128]{1,0:T(8,128)}, ...), condition=%wide.region_26.27_spmd.clone, body=%wide.region_14.26_spmd.clone.sunk | while | flops 2221451264 | bytes 69594376 | solution.py:92
  124.2 3.6 gather_fusion.2
  145.5 33.0 %scatter_fusion = f32[192,4,128]{2,1,0:T(4,128)S(1)} fusion(f32[192,4,128]{2,1,0:T(4,128)S(1)} %get-tuple-element.2437, s32[1024]{0:T(1024)S(1)} %copy-done.29, f32[1024,4,128]{2,1,0:T(4,128)S(1)} %copy.199), kind=kCustom, calls=%fused_computation.5.clone.clone.1 | custom fusion | flops 524288 | bytes 6295552 | tf_op jit(solution)/shard_map/transpose(jvp())/while/body/eval_jaxpr/checkpoint/jit(_take)/scatter-add | solution.py:70
  178.6 3.7 fusion.456
  186.1 3.6 gather_fusion.2
  207.9 33.0 %scatter_fusion = f32[192,4,128]{2,1,0:T(4,128)S(1)} fusion(f32[192,4,128]{2,1,0:T(4,128)S(1)} %get-tuple-element.2437, s32[1024]{0:T(1024)S(1)} %copy-done.29, f32[1024,4,128]{2,1,0:T(4,128)S(1)} %copy.199), kind=kCustom, calls=%fused_computation.5.clone.clone.1 | custom fusion | flops 524288 | bytes 6295552 | tf_op jit(solution)/shard_map/transpose(jvp())/while/body/eval_jaxpr/checkpoint/jit(_take)/scatter-add | solution.py:70
  241.0 3.8 fusion.456
  248.6 3.6 gather_fusion.2
  270.3 33.0 %scatter_fusion = f32[192,4,128]{2,1,0:T(4,128)S(1)} fusion(f32[192,4,128]{2,1,0:T(4,128)S(1)} %get-tuple-element.2437, s32[1024]{0:T(1024)S(1)} %copy-done.29, f32[1024,4,128]{2,1,0:T(4,128)S(1)} %copy.199), kind=kCustom, calls=%fused_computation.5.clone.clone.1 | custom fusion | flops 524288 | bytes 6295552 | tf_op jit(solution)/shard_map/transpose(jvp())/while/body/eval_jaxpr/checkpoint/jit(_take)/scatter-add | solution.py:70
  303.5 3.8 fusion.456
  311.1 3.6 gather_fusion.2
  332.8 33.0 %scatter_fusion = f32[192,4,128]{2,1,0:T(4,128)S(1)} fusion(f32[192,4,128]{2,1,0:T(4,128)S(1)} %get-tuple-element.2437, s32[1024]{0:T(1024)S(1)} %copy-done.29, f32[1024,4,128]{2,1,0:T(4,128)S(1)} %copy.199), kind=kCustom, calls=%fused_computation.5.clone.clone.1 | custom fusion | flops 524288 | bytes 6295552 | tf_op jit(solution)/shard_map/transpose(jvp())/while/body/eval_jaxpr/checkpoint/jit(_take)/scatter-add | solution.py:70
  366.0 3.8 fusion.456
  385.6 4.8 collective-permute-start.7
  393.8 114.6 %while.87 = (s32[]{:T(128)}, f32[64,128]{1,0:T(8,128)}, f32[128,384]{1,0:T(8,128)}, f32[192,1,128]{2,0,1:T(8,128)S(1)}, f32[128,128]{1,0:T(8,128)S(1)}, /*index=...) while((s32[]{:T(128)}, f32[64,128]{1,0:T(8,128)}, ...), condition=%wide.region_38.39_spmd.clone, body=%wide.region_27.38_spmd.clone.sunk | while | flops 2217748480 | bytes 36684576 | solution.py:92
  399.8 2.8 gather_fusion.3
  411.7 2.7 fusion.490
  415.6 6.1 scatter_fusion.1
  428.4 2.8 gather_fusion.3
  440.3 2.7 fusion.490
  444.2 6.1 scatter_fusion.1
  457.0 2.8 gather_fusion.3
  468.9 2.7 fusion.490
  472.8 6.1 scatter_fusion.1
  485.6 2.8 gather_fusion.3
  497.5 2.7 fusion.490
  501.4 6.1 scatter_fusion.1
  511.2 22.8 %all-reduce.14 = (f32[]{:T(128)}, f32[3,3]{1,0:T(4,128)S(1)}) all-reduce(f32[]{:T(128)} %fusion.234, f32[3,3]{1,0:T(4,128)S(1)} %convolution_bitcast_fusion.6), channel_id=1, replica_groups=mesh['dp'=4,'atom'=8] {'atom'}, use_global_device_ids=true, to_apply=%region_13.14 | all-reduce | flops 10 | bytes 80 | tf_op jit(solution)/shard_map/psum | solution.py:189
  537.6 22.4 %scatter_fusion.2 = f32[3,192]{0,1:T(8,128)S(1)} fusion(f32[3,192]{0,1:T(8,128)S(1)} %pad.89, s32[4096]{0:T(1024)S(1)} %copy-done.69, f32[4096,3]{1,0:T(8,128)S(1)} %bitcast.584), kind=kCustom, calls=%fused_computation.7 | custom fusion | flops 12288 | bytes 163840 | tf_op jit(solution)/shard_map/transpose(jvp(jit(_take)))/scatter-add | solution.py:34
  563.1 3.5 collective-permute-done.8
  570.4 4.7 collective-permute-start.11
  576.9 41.6 %all-reduce.12 = (f32[96,128]{1,0:T(8,128)}, f32[128]{0:T(128)}) all-reduce(f32[96,128]{1,0:T(8,128)S(1)} %convolution_multiply_fusion.9, f32[128]{0:T(128)S(1)} %fusion.233), channel_id=1, replica_groups=mesh['dp'=4,'atom'=8] {'dp','atom'}, use_global_device_ids=true, to_apply=%region_42.43 | all-reduce | flops 12416 | bytes 99328 | tf_op jit(solution)/shard_map/psum | solution.py:196
  618.5 81.5 %all-reduce.17.cloned.1.call-done = (f32[2,64,128]{2,1,0:T(8,128)}, f32[2,128,384]{2,1,0:T(8,128)}, f32[2,128,128]{2,1,0:T(8,128)}, f32[2,128,128]{2,1,0:T(8,128...) async-done(((f32[2,64,128]{2,1,0:T(8,128)}, f32[2,128,384]{2,1,0:T(8,128)}, f32[2,128,128]{2,1,0:T(8,128)}, f32[2,128,128]{2,1,0:T(8,128)}, f32[2,128,128]{2,1,0:T(8,128)}, ...) | async-done | bytes 917520 | tf_op jit(solution)/shard_map/psum | solution.py:196
  (1071 shorter events, 242.7 us)
Async XLA Ops:
  7.2 111.5 %copy-start = (f32[128,128]{1,0:T(8,128)S(1)}, f32[128,128]{1,0:T(8,128)}, u32[]{:S(2)}) copy-start(f32[128,128]{1,0:T(8,128)} %param.36) | copy-start | bytes 196612
  7.2 19.5 %copy-start.64 = (f32[2,128,128]{2,1,0:T(8,128)S(1)}, f32[2,128,128]{2,1,0:T(8,128)}, u32[]{:S(2)}) copy-start(f32[2,128,128]{2,1,0:T(8,128)} %param.34) | copy-start | bytes 393220
  7.2 19.5 %copy-start.63 = (f32[2,128,128]{2,1,0:T(8,128)S(1)}, f32[2,128,128]{2,1,0:T(8,128)}, u32[]{:S(2)}) copy-start(f32[2,128,128]{2,1,0:T(8,128)} %param.35) | copy-start | bytes 393220
  7.2 19.6 %copy-start.70 = (s32[3,32,128]{2,1,0:T(8,128)S(1)}, s32[3,32,128]{2,1,0:T(8,128)}, u32[]{:S(2)}) copy-start(s32[3,32,128]{2,1,0:T(8,128)} %param.27) | copy-start | bytes 147460
  7.2 692.7 %all-reduce.17.cloned.1.call-start = ((), (), s32[]{:S(2)}) async-start(), calls=%async_computation | async-start | bytes 1835008 | tf_op jit(solution)/shard_map/psum | solution.py:196
  8.3 18.5 %collective-permute-start = (f32[3,32]{1,0:T(4,128)S(1)}, f32[3,32]{1,0:T(4,128)S(1)}, u32[]{:S(2)}, u32[]{:S(2)}) collective-permute-start(f32[3,32]{1,0:T(4,128)S(1)} %get-tuple-element.1829), channel_id=1, source_target_pairs={{0,1},{1,2},{2,3},{3,4},{4,5},{5,6},{6,7},{7,0},{8,9},{9,10},{10,1... | collective-permute-start | bytes 1160 | tf_op jit(solution)/shard_map/ppermute | solution.py:25
  11.3 15.5 %collective-permute-start.1 = (f32[3,32]{1,0:T(4,128)S(1)}, f32[3,32]{1,0:T(4,128)S(1)}, u32[]{:S(2)}, u32[]{:S(2)}) collective-permute-start(f32[3,32]{1,0:T(4,128)S(1)} %get-tuple-element.1830), channel_id=1, source_target_pairs={{1,0},{2,1},{3,2},{4,3},{5,4},{6,5},{7,6},{0,7},{9,8},{10,9},{11,1... | collective-permute-start | bytes 1160 | tf_op jit(solution)/shard_map/ppermute | solution.py:26
  15.5 25.1 %collective-permute-start.2 = (f32[32,1,128]{2,0,1:T(8,128)S(1)}, f32[32,1,128]{2,0,1:T(8,128)S(1)}, u32[]{:S(2)}, u32[]{:S(2)}) collective-permute-start(f32[32,1,128]{2,0,1:T(8,128)S(1)} %get-tuple-element.1818), channel_id=1, source_target_pairs={{0,1},{1,2},{2,3},{3,4},{4,5},{5,6},{6,7},{7,0},{8,9},{9,10},{10,1... | collective-permute-start | bytes 49160 | tf_op jit(solution)/shard_map/ppermute | solution.py:25
  15.5 25.1 %collective-permute-start.3 = (f32[32,1,128]{2,0,1:T(8,128)S(1)}, f32[32,1,128]{2,0,1:T(8,128)S(1)}, u32[]{:S(2)}, u32[]{:S(2)}) collective-permute-start(f32[32,1,128]{2,0,1:T(8,128)S(1)} %get-tuple-element.1819), channel_id=1, source_target_pairs={{1,0},{2,1},{3,2},{4,3},{5,4},{6,5},{7,6},{0,7},{9,8},{10,9},{11,1... | collective-permute-start | bytes 49160 | tf_op jit(solution)/shard_map/ppermute | solution.py:26
  26.8 11.7 %copy-start.77 = (f32[1,3,3]{2,0,1:T(1,128)S(1)}, f32[1,3,3]{2,0,1:T(1,128)}, u32[]{:S(2)}) copy-start(f32[1,3,3]{2,0,1:T(1,128)} %param.28) | copy-start | bytes 112
  40.6 38.1 %copy-start.55 = (s32[32,128]{1,0:T(8,128)S(1)}, s32[32,128]{1,0:T(8,128)}, u32[]{:S(2)}) copy-start(s32[32,128]{1,0:T(8,128)} %param.25) | copy-start | bytes 49156
  72.8 9.0 %copy-start.12 = (f32[128,128]{1,0:T(8,128)}, f32[128,128]{1,0:T(8,128)S(1)}, u32[]{:S(2)}) copy-start(f32[128,128]{1,0:T(8,128)S(1)} %get-tuple-element.2577) | copy-start | bytes 196612
  72.8 9.0 %copy-start.24 = (f32[64,128]{1,0:T(8,128)}, f32[64,128]{1,0:T(8,128)S(1)}, u32[]{:S(2)}) copy-start(f32[64,128]{1,0:T(8,128)S(1)} %get-tuple-element.2582) | copy-start | bytes 98308
  74.0 7.0 collective-permute-start.4
  74.0 7.0 collective-permute-start.5
  81.8 37.9 %copy-start.83 = (f32[128]{0:T(128)S(1)}, f32[128]{0:T(128)}, u32[]{:S(2)}) copy-start(f32[128]{0:T(128)} %param.37) | copy-start | bytes 1540
  128.3 10.1 %copy-start.17 = (f32[32,32]{1,0:T(8,128)}, f32[32,32]{1,0:T(8,128)S(1)}, u32[]{:S(2)}) copy-start(f32[32,32]{1,0:T(8,128)S(1)} %get-tuple-element.2263) | copy-start | bytes 12292 | tf_op jit(solution)/shard_map/transpose(jvp())/while
  145.5 33.0 %copy-start.51 = (f32[32,32]{1,0:T(8,128)S(1)}, f32[32,32]{1,0:T(8,128)}, u32[]{:S(2)}) copy-start(f32[32,32]{1,0:T(8,128)} %copy-done.49) | copy-start | bytes 12292 | tf_op jit(solution)/shard_map/transpose(jvp())/while
  190.2 10.1 %copy-start.17 = (f32[32,32]{1,0:T(8,128)}, f32[32,32]{1,0:T(8,128)S(1)}, u32[]{:S(2)}) copy-start(f32[32,32]{1,0:T(8,128)S(1)} %get-tuple-element.2263) | copy-start | bytes 12292 | tf_op jit(solution)/shard_map/transpose(jvp())/while
  207.9 33.0 %copy-start.51 = (f32[32,32]{1,0:T(8,128)S(1)}, f32[32,32]{1,0:T(8,128)}, u32[]{:S(2)}) copy-start(f32[32,32]{1,0:T(8,128)} %copy-done.49) | copy-start | bytes 12292 | tf_op jit(solution)/shard_map/transpose(jvp())/while
  252.7 10.1 %copy-start.17 = (f32[32,32]{1,0:T(8,128)}, f32[32,32]{1,0:T(8,128)S(1)}, u32[]{:S(2)}) copy-start(f32[32,32]{1,0:T(8,128)S(1)} %get-tuple-element.2263) | copy-start | bytes 12292 | tf_op jit(solution)/shard_map/transpose(jvp())/while
  270.3 33.1 %copy-start.51 = (f32[32,32]{1,0:T(8,128)S(1)}, f32[32,32]{1,0:T(8,128)}, u32[]{:S(2)}) copy-start(f32[32,32]{1,0:T(8,128)} %copy-done.49) | copy-start | bytes 12292 | tf_op jit(solution)/shard_map/transpose(jvp())/while
  315.2 10.1 %copy-start.17 = (f32[32,32]{1,0:T(8,128)}, f32[32,32]{1,0:T(8,128)S(1)}, u32[]{:S(2)}) copy-start(f32[32,32]{1,0:T(8,128)S(1)} %get-tuple-element.2263) | copy-start | bytes 12292 | tf_op jit(solution)/shard_map/transpose(jvp())/while
  332.8 33.0 %copy-start.51 = (f32[32,32]{1,0:T(8,128)S(1)}, f32[32,32]{1,0:T(8,128)}, u32[]{:S(2)}) copy-start(f32[32,32]{1,0:T(8,128)} %copy-done.49) | copy-start | bytes 12292 | tf_op jit(solution)/shard_map/transpose(jvp())/while
  372.0 18.4 %copy-start.66 = (f32[128,128]{1,0:T(8,128)S(1)}, f32[128,128]{1,0:T(8,128)}, u32[]{:S(2)}) copy-start(f32[128,128]{1,0:T(8,128)} %copy-done.65) | copy-start | bytes 196612
  372.0 18.4 %copy-start.84 = (f32[128]{0:T(128)S(1)}, f32[128]{0:T(128)}, u32[]{:S(2)}) copy-start(f32[128]{0:T(128)} %param.37) | copy-start | bytes 1540
  372.6 21.1 %copy-start.13 = (f32[128,128]{1,0:T(8,128)S(1)}, f32[128,128]{1,0:T(8,128)}, u32[]{:S(2)}) copy-start(f32[128,128]{1,0:T(8,128)} %copy-done.12) | copy-start | bytes 196612
  372.6 21.1 %copy-start.25 = (f32[64,128]{1,0:T(8,128)S(1)}, f32[64,128]{1,0:T(8,128)}, u32[]{:S(2)}) copy-start(f32[64,128]{1,0:T(8,128)} %copy-done.24) | copy-start | bytes 98308
  372.6 21.1 %copy-start.31 = (f32[128,128]{1,0:T(8,128)S(1)}, f32[128,128]{1,0:T(8,128)}, u32[]{:S(2)}) copy-start(f32[128,128]{1,0:T(8,128)} %custom-call.7) | copy-start | bytes 196612
  373.7 11.9 %collective-permute-start.6 = (f32[32,4,128]{2,0,1:T(8,128)S(1)}, f32[32,4,128]{2,0,1:T(8,128)S(1)}, u32[]{:S(2)}, u32[]{:S(2)}) collective-permute-start(f32[32,4,128]{2,0,1:T(8,128)S(1)} %slice.364), channel_id=1, source_target_pairs={{7,0},{0,1},{1,2},{2,3},{3,4},{4,5},{5,6},{6,7},{15,8},{8,9},{9,10... | collective-permute-start | bytes 196616 | tf_op jit(solution)/shard_map/ppermute | solution.py:15
  385.6 6.7 collective-permute-start.7
  508.4 26.2 %copy-start.67 = (f32[128,128]{1,0:T(8,128)S(1)}, f32[128,128]{1,0:T(8,128)}, u32[]{:S(2)}) copy-start(f32[128,128]{1,0:T(8,128)} %copy-done.65) | copy-start | bytes 196612
  508.4 28.2 %copy-start.56 = (f32[4,32,1,128]{3,1,2,0:T(8,128)S(1)}, f32[4,32,1,128]{3,1,2,0:T(8,128)}, u32[]{:S(2)}) copy-start(f32[4,32,1,128]{3,1,2,0:T(8,128)} %get-tuple-element.1154) | copy-start | bytes 196612
  536.7 33.7 %collective-permute-start.10 = (f32[32,1,128]{2,0,1:T(8,128)S(1)}, f32[32,1,128]{2,0,1:T(8,128)S(1)}, u32[]{:S(2)}, u32[]{:S(2)}) collective-permute-start(f32[32,1,128]{2,0,1:T(8,128)S(1)} %slice.374), channel_id=1, source_target_pairs={{7,0},{0,1},{1,2},{2,3},{3,4},{4,5},{5,6},{6,7},{15,8},{8,9},{9,10... | collective-permute-start | bytes 49160 | tf_op jit(solution)/shard_map/ppermute | solution.py:15
  536.7 23.6 %copy-start.42 = (f32[128,128]{1,0:T(8,128)S(1)}, f32[128,128]{1,0:T(8,128)}, u32[]{:S(2)}) copy-start(f32[128,128]{1,0:T(8,128)} %get-tuple-element.1163) | copy-start | bytes 196612
  536.7 23.6 %copy-start.43 = (f32[128,128]{1,0:T(8,128)S(1)}, f32[128,128]{1,0:T(8,128)}, u32[]{:S(2)}) copy-start(f32[128,128]{1,0:T(8,128)} %get-tuple-element.1164) | copy-start | bytes 196612
  536.7 24.2 %copy-start.61 = (f32[128,384]{1,0:T(8,128)S(1)}, f32[128,384]{1,0:T(8,128)}, u32[]{:S(2)}) copy-start(f32[128,384]{1,0:T(8,128)} %get-tuple-element.1157) | copy-start | bytes 589828
  536.8 24.2 %copy-start.62 = (f32[128,384]{1,0:T(8,128)S(1)}, f32[128,384]{1,0:T(8,128)}, u32[]{:S(2)}) copy-start(f32[128,384]{1,0:T(8,128)} %get-tuple-element.1158) | copy-start | bytes 589828
  537.4 24.3 %copy-start.73 = (f32[64,128]{1,0:T(8,128)S(1)}, f32[64,128]{1,0:T(8,128)}, u32[]{:S(2)}) copy-start(f32[64,128]{1,0:T(8,128)} %get-tuple-element.1155) | copy-start | bytes 98308
  537.4 24.3 %copy-start.76 = (f32[64,128]{1,0:T(8,128)S(1)}, f32[64,128]{1,0:T(8,128)}, u32[]{:S(2)}) copy-start(f32[64,128]{1,0:T(8,128)} %get-tuple-element.1156) | copy-start | bytes 98308
  537.4 25.0 %copy-start.32 = (f32[128,128]{1,0:T(8,128)S(1)}, f32[128,128]{1,0:T(8,128)}, u32[]{:S(2)}) copy-start(f32[128,128]{1,0:T(8,128)} %get-tuple-element.1162) | copy-start | bytes 196612
  537.4 31.1 %copy-start.38 = (f32[128,128]{1,0:T(8,128)S(1)}, f32[128,128]{1,0:T(8,128)}, u32[]{:S(2)}) copy-start(f32[128,128]{1,0:T(8,128)} %get-tuple-element.1159) | copy-start | bytes 196612
  537.4 31.1 %copy-start.39 = (f32[128,128]{1,0:T(8,128)S(1)}, f32[128,128]{1,0:T(8,128)}, u32[]{:S(2)}) copy-start(f32[128,128]{1,0:T(8,128)} %get-tuple-element.1160) | copy-start | bytes 196612
  560.0 16.5 %copy-start.82 = (s32[128]{0:T(128)S(1)}, s32[128]{0:T(128)}, u32[]{:S(2)}) copy-start(s32[128]{0:T(128)} %param.24) | copy-start | bytes 1540
  560.1 6.5 collective-permute-start.8
  566.6 3.7 collective-permute-start.9
  570.4 6.2 collective-permute-start.11
  700.0 8.0 %copy-start.68 = (f32[128,128]{1,0:T(8,128)S(1)}, f32[128,128]{1,0:T(8,128)}, u32[]{:S(2)}) copy-start(f32[128,128]{1,0:T(8,128)} %get-tuple-element.2555) | copy-start | bytes 196612
  (220 other events, 676.5 us)
Sparse Core Ops, SparseCore 0:
  570.0 129.9 all-reduce.16
where the time goes:
time: 727 us; the launch traced here: 716 us
  other arithmetic  230 us (32%)
  matrix products  149 us (20%)
  local copies, waits for them, and re-layouts  125 us (17%)
  waiting for transfers between devices  88.2 us (12%)
  blocking collectives  64.4 us (9%)
  starting transfers between devices  27.5 us (4%)
  between operations  25.9 us (4%)
    scatter-add x8, other arithmetic, one_block(): gathered = jnp.take(wide_rows, rows, axis=0)  156 us
    psum x1, waiting for transfers between devices, local(): lax.psum((scaled[0], scaled[1], scaled[2], scaled[3], scaled[4], scaled[5...  81.5 us
    dot_general x32, matrix products, one_block(): jnp.einsum('kbc,cd->kbd', hidden, radial_out, precision=HIGH)  73.3 us
    gather x24, local copies, waits for them, and re-layouts, one_block(): gathered = jnp.take(wide_rows, rows, axis=0)  52 us
    psum x1, blocking collectives, local(): lax.psum((scaled[0], scaled[1], scaled[2], scaled[3], scaled[4], scaled[5...  41.6 us
    dot_general x32, matrix products, one_block(): jnp.einsum('kbn,nc->kbc', radial_basis, radial_in, precision=HIGH)  28.5 us
    psum x1, blocking collectives, local(): energy_total, virial_total = lax.psum((energy_part, virial), 'atom')  22.8 us
    scatter-add x1, other arithmetic, edge_geometry(): far_end = jnp.take(window_pos, neighbour_rows, axis=1)  22.4 us
  transfers between devices with their start and end apart: 13, of which 6 were waited for; matrix products, arithmetic and copies ran while one was open for 7% of the time, Pallas kernels for 0%

commit v1 on v0

v1 whole, which is shorter than its diff:
```python
import functools

import jax
import jax.numpy as jnp
from jax import lax
from jax.experimental import pallas as pl
from jax.experimental.pallas import tpu as pltpu
from jax.sharding import PartitionSpec as P

F32 = jnp.float32
BF16 = jnp.bfloat16
LANES = 128
HALF = 64
FWD_ROWS = 2
BWD_ROWS = 2
VMEM_LIMIT = 50 * 1024 * 1024
G_ROWS = 992


def split(x):
    high = x.astype(BF16)
    return high, (x - high.astype(F32)).astype(BF16)


def mm(a, b):
    return lax.dot_general(a, b, (((1,), (0,)), ((), ())), preferred_element_type=F32)


def mm_nt(a, b):
    return lax.dot_general(a, b, (((1,), (1,)), ((), ())), preferred_element_type=F32)


def mm3(a, b):
    ah, al = split(a)
    bh, bl = split(b)
    return mm(ah, bh) + (mm(ah, bl) + mm(al, bh))


def mm3_nt(a, b):
    ah, al = split(a)
    bh, bl = split(b)
    return mm_nt(ah, bh) + (mm_nt(ah, bl) + mm_nt(al, bh))


def sigmoid(x):
    return 1.0 / (1.0 + jnp.exp(-x))


def lane_ids(rows):
    return lax.broadcasted_iota(jnp.int32, (rows, LANES), 1)


def twice(x, half):
    low = lane_ids(x.shape[0]) < HALF
    other = pltpu.roll(x, HALF, 1)
    return jnp.where(low, x, other) if half == 0 else jnp.where(low, other, x)


def folded(first, second):
    low = lane_ids(first.shape[0]) < HALF
    return jnp.where(low, first + pltpu.roll(first, HALF, 1), second + pltpu.roll(second, HALF, 1))


def windows(own, beside, halo):
    lane = lane_ids(own.shape[0])
    return jnp.where(lane < LANES - halo, own, beside), jnp.where(lane >= halo, own, beside)


def packed(parts, halo, tail):
    lane = lane_ids(parts[0].shape[0])
    out = None
    for q, x in enumerate(parts):
        turn = (halo * (q + 1) if tail else halo * q) % LANES
        x = pltpu.roll(x, turn, 1) if turn else x
        out = x if out is None else jnp.where(lane < halo * q, out, x)
    return out


def unpacked(pack, q, halo, tail):
    turn = (LANES - halo * (q + 1) if tail else LANES - halo * q) % LANES
    return pltpu.roll(pack, turn, 1) if turn else pack


def is_even(par_ref, shape):
    return (jnp.zeros(shape, jnp.int32) + par_ref[0]) == 0


def prepare_weights(rin_ref, rout_ref, ri4, ro3, groups):
    rh, rl = split(rin_ref[0])
    rows = jnp.concatenate([rh, rh, rl, rl], axis=0).astype(F32)
    ri4[...] = rows.T.astype(BF16)
    wh, wl = split(rout_ref[0])
    for place, g in enumerate(groups):
        cols = slice(g * LANES, (g + 1) * LANES)
        th = wh[:, cols].astype(F32).T.astype(BF16)
        tl = wl[:, cols].astype(F32).T.astype(BF16)
        out = slice(place * LANES, (place + 1) * LANES)
        ro3[out, 0:LANES] = th
        ro3[out, LANES : 2 * LANES] = th
        ro3[out, 2 * LANES : 3 * LANES] = tl


def prepare_back(rin_ref, rout_ref, rib, rob, groups):
    rh, rl = split(rin_ref[0])
    count = rh.shape[0]
    rib[0:count, 0:LANES] = rh
    rib[0:count, LANES:] = rh
    rib[count:, 0:LANES] = rl
    rib[count:, LANES:] = rl
    wh, wl = split(rout_ref[0])
    width = len(groups) * LANES
    for place, g in enumerate(groups):
        cols = slice(g * LANES, (g + 1) * LANES)
        for copy in range(2):
            out = slice(copy * width + place * LANES, copy * width + (place + 1) * LANES)
            rob[0:LANES, out] = wh[:, cols]
            rob[LANES:, out] = wl[:, cols]


def store_tables(tab, parts, besides, halo):
    for q, (own, beside) in enumerate(zip(parts, besides)):
        for h, table in enumerate(windows(own, beside, halo)):
            hi, lo = split(table)
            tab[h, q * LANES : (q + 1) * LANES, 0:LANES] = hi
            tab[h, q * LANES : (q + 1) * LANES, LANES:] = lo


def radial(rows, ri4, ro3, basis_count):
    sharpness = 0.5 * ((basis_count - 1) / 8.0) ** 2
    place = lax.broadcasted_iota(jnp.int32, (basis_count, LANES), 0).astype(F32)
    centres = 8.0 * place / (basis_count - 1)
    offsets = [g[3:4] - centres for g in rows]
    offset = jnp.concatenate(offsets, axis=1)
    basis = jnp.exp(-sharpness * offset * offset)
    bh, bl = split(basis)
    pre = mm(ri4[...], jnp.concatenate([bh, bl, bh, bl], axis=0))
    gate = sigmoid(pre)
    mask = jnp.concatenate([g[4:5] for g in rows], axis=1)
    hidden = pre * gate * mask
    hh, hl = split(hidden)
    filters = mm(ro3[...], jnp.concatenate([hh, hl, hh], axis=0))
    return offset, basis, bh, bl, pre, gate, mask, hidden, hh, hl, filters, sharpness


def one_hot_of(rows):
    place = lax.broadcasted_iota(jnp.int32, (LANES, LANES), 0).astype(F32)
    return jnp.concatenate(
        [jnp.where(place == g[5:6], 1.0, 0.0).astype(BF16) for g in rows], axis=1
    )


def part(x, group, q):
    return x[group * LANES : (group + 1) * LANES, q * LANES : (q + 1) * LANES]


def forward_edges(geom, tab, ri4, ro3, acc, basis_count, vectors):
    total = geom.shape[0]
    per_half = total // 2 // FWD_ROWS
    acc[...] = jnp.zeros(acc.shape, F32)
    wide = 2 if vectors else 1

    def step(t, carry):
        h = t // per_half
        rows = [geom[t * FWD_ROWS + q] for q in range(FWD_ROWS)]
        filters = radial(rows, ri4, ro3, basis_count)[10]
        hot = one_hot_of(rows)
        found = mm(tab[h], jnp.concatenate([hot, hot], axis=0))
        sums = [None] * 4
        for q, g in enumerate(rows):
            s = part(found, 0, q)
            terms = [part(filters, 0, q) * s]
            push = part(filters, wide, q) * s
            for c in range(3):
                term = push * g[c : c + 1]
                if vectors:
                    term = term + part(filters, 1, q) * part(found, 1 + c, q)
                terms.append(term)
            sums = [x if y is None else y + x for x, y in zip(terms, sums)]
        for n in range(4):
            acc[h, n] += sums[n]
        return carry

    lax.fori_loop(0, 2 * per_half, step, 0)


def aggregates(acc, scale):
    return [folded(acc[0, n], acc[1, n]) * scale for n in range(4)]


def node_forward(agg, sm, vm, vg):
    mixed = mm3(vm.T, jnp.concatenate(agg[1:], axis=1))
    w = [mixed[:, c * LANES : (c + 1) * LANES] for c in range(3)]
    size = jnp.sqrt(w[0] * w[0] + w[1] * w[1] + w[2] * w[2] + 1.0)
    u = mm3(sm.T, agg[0]) + (size - 1.0)
    gate = sigmoid(mm3(vg.T, agg[0]))
    return w, size, u, gate


def node_backward(agg, w, size, u, gate, sm, vm, vg, ds, dv, scale):
    act = sigmoid(u)
    du = ds * (act * (1.0 + u * (1.0 - act)))
    ratio = du / size
    dw = [w[c] * ratio + dv[c] * gate for c in range(3)]
    dq = (dv[0] * w[0] + dv[1] * w[1] + dv[2] * w[2]) * gate * (1.0 - gate)
    dw_all = jnp.concatenate(dw, axis=1)
    da_s = (mm3(sm, du) + mm3(vg, dq)) * scale
    da_v = mm3(vm, dw_all) * scale
    da = [da_s] + [da_v[:, c * LANES : (c + 1) * LANES] for c in range(3)]
    g_sm = mm3_nt(agg[0], du)
    g_vg = mm3_nt(agg[0], dq)
    g_vm = mm3_nt(jnp.concatenate(agg[1:], axis=1), dw_all)
    return da, g_sm, g_vm, g_vg


def backward_edges(geom, dgeom, tab, ri4, ro3, rib, rob, gacc, dro, dri, dtab, basis_count, vectors, finish):
    total = geom.shape[0]
    per_half = total // 2 // BWD_ROWS
    dro[...] = jnp.zeros(dro.shape, F32)
    dri[...] = jnp.zeros(dri.shape, F32)
    dtab[...] = jnp.zeros(dtab.shape, F32)
    wide = 2 if vectors else 1

    def step(t, carry):
        h = t // per_half
        rows = [geom[t * BWD_ROWS + q] for q in range(BWD_ROWS)]
        offset, basis, bh, bl, pre, gate, mask, hidden, hh, hl, filters, sharpness = radial(
            rows, ri4, ro3, basis_count
        )
        hot = one_hot_of(rows)
        found = mm(tab[h], jnp.concatenate([hot, hot], axis=0))
        d_filters, d_found, d_dirs = [], [], []
        gs = gacc[h, 0]
        gv = [gacc[h, 1 + c] for c in range(3)]
        for q, g in enumerate(rows):
            s = part(found, 0, q)
            along = gv[0] * g[0:1] + gv[1] * g[1:2] + gv[2] * g[2:3]
            f_s, f_d = part(filters, 0, q), part(filters, wide, q)
            groups = [gs * s]
            sources = [f_s * gs + f_d * along]
            if vectors:
                f_v = part(filters, 1, q)
                v = [part(found, 1 + c, q) for c in range(3)]
                groups.append(gv[0] * v[0] + gv[1] * v[1] + gv[2] * v[2])
                sources += [f_v * gv[c] for c in range(3)]
            groups.append(s * along)
            d_filters.append(jnp.concatenate(groups, axis=0))
            push = f_d * s
            d_dirs.append([jnp.sum(push * gv[c], axis=0, keepdims=True) for c in range(3)])
            d_found.append(jnp.concatenate(sources, axis=0))
        d_filter = jnp.concatenate(d_filters, axis=1)
        fh, fl = split(d_filter)
        both = jnp.concatenate([hh, hl], axis=0)
        dro[...] += mm_nt(jnp.concatenate([fh, fl], axis=1), jnp.concatenate([both, both], axis=1))
        spread = mm(rob[...], jnp.concatenate([fh, fl], axis=0))
        d_hidden = (spread[:LANES] + spread[LANES:]) * mask
        d_pre = d_hidden * (gate * (1.0 + pre * (1.0 - gate)))
        ph, plo = split(d_pre)
        bb = jnp.concatenate([bh, bl], axis=0)
        dri[...] += mm_nt(jnp.concatenate([ph, plo], axis=1), jnp.concatenate([bb, bb], axis=1))
        back = mm(rib[...], jnp.concatenate([ph, plo], axis=0))
        d_basis = back[:basis_count] + back[basis_count:]
        d_dist = jnp.sum(d_basis * basis * offset, axis=0, keepdims=True) * (-2.0 * sharpness)
        extra = []
        for q, g in enumerate(rows):
            extra.append(finish(t * BWD_ROWS + q, h, g, d_dirs[q], d_dist[:, q * LANES : (q + 1) * LANES]))
        if extra[0] is not None:
            d_found = [jnp.concatenate([a, b], axis=0) for a, b in zip(d_found, extra)]
        sh, sl = split(jnp.concatenate(d_found, axis=1))
        dtab[h] += mm_nt(jnp.concatenate([sh, sl], axis=1), jnp.concatenate([hot, hot], axis=1))
        return carry

    lax.fori_loop(0, 2 * per_half, step, 0)


def radial_grads(dro, dri, out, row_in, row_out, basis_count, groups):
    both = dri[...]
    turned = both + pltpu.roll(both, HALF, 1)
    out[row_in : row_in + basis_count] = turned.T[0:basis_count]
    for place, g in enumerate(groups):
        rows = slice(place * LANES, (place + 1) * LANES)
        grad = dro[rows, 0:LANES] + dro[rows, LANES:]
        out[row_out + g * LANES : row_out + (g + 1) * LANES] = grad.T


def species_hot(row, count):
    place = lax.broadcasted_iota(jnp.int32, (count, LANES), 0).astype(F32)
    return jnp.where(place == row, 1.0, 0.0).astype(BF16)


def first_features(emb_ref, hot):
    high, rest = split(emb_ref[...])
    low = (emb_ref[...] - high.astype(F32) - rest.astype(F32)).astype(BF16)
    dims = (((0,), (0,)), ((), ()))
    terms = [
        lax.dot_general(x.astype(F32).T.astype(BF16), hot, (((1,), (0,)), ((), ())), preferred_element_type=F32)
        for x in (high, rest, low)
    ]
    return terms[0] + (terms[1] + terms[2])


def from_sides(par_ref, a_ref, b_ref):
    even = is_even(par_ref, a_ref.shape)
    a, b = a_ref[...], b_ref[...]
    return jnp.where(even, a, b), jnp.where(even, b, a)


def species_tables(own_ref, up, down, emb_ref, halo):
    lane = lane_ids(1)
    count = emb_ref.shape[0]
    beside = jnp.where(lane >= LANES - halo, down[3:4], up[3:4])
    hot_own, hot_beside = species_hot(own_ref[3:4], count), species_hot(beside, count)
    return hot_own, hot_beside


def first_kernel(
    halo, par_ref, cell_ref, own_ref, a_ref, b_ref, nb_ref, count_ref, shift_ref, emb_ref, rin_ref, rout_ref,
    sm_ref, vm_ref, vg_ref,
    geom_ref, feat_ref, agg_ref, send_a, send_b,
    tab, ri4, ro3, acc,
):
    slots = nb_ref.shape[0]
    basis_count = rin_ref.shape[1]
    pairs = slots // 2
    up, down = from_sides(par_ref, a_ref, b_ref)
    lane = lane_ids(pairs)
    low = lane < HALF

    def halves(ref, *lead):
        even = ref[(*lead, pl.ds(0, pairs, stride=2), slice(None))]
        odd = ref[(*lead, pl.ds(1, pairs, stride=2), slice(None))]
        return jnp.where(low, even, pltpu.roll(odd, HALF, 1)), jnp.where(low, pltpu.roll(even, HALF, 1), odd)

    nb = halves(nb_ref)
    shift = [halves(shift_ref, a) for a in range(3)]
    row_slot = 2 * lax.broadcasted_iota(jnp.int32, (pairs, LANES), 0) + jnp.where(low, 0, 1)
    own = own_ref[...]
    lane8 = lane_ids(own.shape[0])
    places = (jnp.where(lane8 < LANES - halo, own, down), jnp.where(lane8 >= halo, own, up))
    for h in range(2):
        index = (nb[h] - halo) & (LANES - 1)
        near = twice(own, h)
        count = twice(count_ref[...], h)
        mask = jnp.where(row_slot < count, 1.0, 0.0).astype(F32)
        steps = [shift[a][h].astype(F32) for a in range(3)]
        r = []
        for c in range(3):
            table = jnp.broadcast_to(places[h][c : c + 1], (pairs, LANES))
            far = jnp.take_along_axis(table, index, axis=1, mode="promise_in_bounds")
            image = steps[0] * cell_ref[0, 0, c] + steps[1] * cell_ref[0, 1, c] + steps[2] * cell_ref[0, 2, c]
            r.append(far - near[c : c + 1] + image)
        dist = jnp.sqrt(r[0] * r[0] + r[1] * r[1] + r[2] * r[2] + 1.0)
        values = [x / dist for x in r] + [dist, mask, index.astype(F32)]
        for n, x in enumerate(values):
            for m in range(pairs):
                geom_ref[h * pairs + m, n : n + 1, :] = x[m : m + 1]
    hot_own, hot_beside = species_tables(own_ref, up, down, emb_ref, halo)
    s, beside = first_features(emb_ref, hot_own), first_features(emb_ref, hot_beside)
    store_tables(tab, [s], [beside], halo)
    prepare_weights(rin_ref, rout_ref, ri4, ro3, (0, 2))
    forward_edges(geom_ref, tab, ri4, ro3, acc, basis_count, False)
    agg = aggregates(acc, slots**-0.5)
    w, size, u, gate = node_forward(agg, sm_ref[0], vm_ref[0], vg_ref[0])
    features = [s + u * sigmoid(u)] + [w[c] * gate for c in range(3)]
    for n in range(4):
        agg_ref[n] = agg[n]
        feat_ref[n] = features[n]
    tail, head = packed(features, halo, True), packed(features, halo, False)
    even = is_even(par_ref, tail.shape)
    send_a[...] = jnp.where(even, tail, head)
    send_b[...] = jnp.where(even, head, tail)


def second_kernel(
    halo, par_ref, geom_ref, feat_ref, a_ref, b_ref, rin_ref, rout_ref, sm_ref, vm_ref, vg_ref, mid_ref, out_ref,
    energy_ref, cot_ref, send_a, send_b, dgeom_ref, grad_ref,
    tab, ri4, ro3, rib, rob, acc, gacc, dro, dri, dtab,
):
    basis_count = rin_ref.shape[1]
    slots = geom_ref.shape[0]
    scale = slots**-0.5
    up, down = from_sides(par_ref, a_ref, b_ref)
    lane = lane_ids(LANES)
    features = [feat_ref[n] for n in range(4)]
    besides = [
        jnp.where(lane >= LANES - halo, unpacked(down, q, halo, True), unpacked(up, q, halo, False)) for q in range(4)
    ]
    store_tables(tab, features, besides, halo)
    groups = (0, 1, 2)
    prepare_weights(rin_ref, rout_ref, ri4, ro3, groups)
    prepare_back(rin_ref, rout_ref, rib, rob, groups)
    forward_edges(geom_ref, tab, ri4, ro3, acc, basis_count, True)

    @pl.when(par_ref[0] >= 0)
    def _():
        agg = aggregates(acc, scale)
        sm, vm, vg = sm_ref[0], vm_ref[0], vg_ref[0]
        w, size, u, gate = node_forward(agg, sm, vm, vg)
        s = feat_ref[0] + u * sigmoid(u)
        mid = mid_ref[...]
        hidden = mm3(mid.T, s)
        act = sigmoid(hidden)
        shown = hidden * act
        weights = jnp.broadcast_to(out_ref[...], (8, LANES))
        per_atom = mm3(weights, shown)
        energy_ref[...] = jnp.broadcast_to(jnp.sum(per_atom, axis=1, keepdims=True), (8, LANES))
        weight_column = jnp.broadcast_to(out_ref[...], (LANES, LANES)).T
        d_hidden = weight_column * (act * (1.0 + hidden * (1.0 - act)))
        ds = mm3(mid, d_hidden)
        zero = jnp.zeros((LANES, LANES), F32)
        dv = [zero, zero, zero]
        da, g_sm, g_vm, g_vg = node_backward(agg, w, size, u, gate, sm, vm, vg, ds, dv, scale)
        for n in range(4):
            for h in range(2):
                gacc[h, n] = twice(da[n], h)
        for n, x in enumerate([ds] + dv):
            cot_ref[n] = x
        row = basis_count + 3 * LANES
        for grad in (g_sm, g_vm, g_vg, mm3_nt(s, d_hidden)):
            grad_ref[row : row + LANES] = grad
            row += LANES
        grad_ref[row : row + 8] = mm3_nt(jnp.ones((8, LANES), F32), shown)
        row += 8
        grad_ref[row:] = jnp.zeros((grad_ref.shape[0] - row, LANES), F32)

    def finish(row, h, g, d_dir, d_dist):
        for c in range(3):
            dgeom_ref[row, c : c + 1, :] = d_dir[c]
        dgeom_ref[row, 3:4, :] = d_dist
        return None

    backward_edges(
        geom_ref, dgeom_ref, tab, ri4, ro3, rib, rob, gacc, dro, dri, dtab, basis_count, True, finish
    )
    radial_grads(dro, dri, grad_ref, 0, basis_count, basis_count, groups)
    firsts = [dtab[0, q * LANES : (q + 1) * LANES] for q in range(4)]
    seconds = [dtab[1, q * LANES : (q + 1) * LANES] for q in range(4)]
    for q in range(4):
        cot_ref[q] += (
            jnp.where(lane < LANES - halo, firsts[q], 0.0) + jnp.where(lane >= halo, seconds[q], 0.0)
        )
    to_prev, to_next = packed(firsts, halo, True), packed(seconds, halo, False)
    even = is_even(par_ref, to_prev.shape)
    send_a[...] = jnp.where(even, to_next, to_prev)
    send_b[...] = jnp.where(even, to_prev, to_next)


def third_kernel(
    halo, par_ref, geom_ref, dgeom_ref, agg_ref, cot_ref, a_ref, b_ref, own_ref, pa_ref, pb_ref, emb_ref, rin_ref,
    rout_ref, sm_ref, vm_ref, vg_ref,
    force_ref, send_a, send_b, grad_ref,
    tab, ri4, ro3, rib, rob, gacc, dro, dri, dtab, pull, virial,
):
    basis_count = rin_ref.shape[1]
    slots = geom_ref.shape[0]
    scale = slots**-0.5
    lane = lane_ids(LANES)
    up, down = from_sides(par_ref, a_ref, b_ref)
    cot = []
    for q in range(4):
        cot.append(
            cot_ref[q]
            + jnp.where(lane >= LANES - halo, unpacked(up, q, halo, True), 0.0)
            + jnp.where(lane < halo, unpacked(down, q, halo, False), 0.0)
        )
    place_up, place_down = from_sides(par_ref, pa_ref, pb_ref)
    hot_own, hot_beside = species_tables(own_ref, place_up, place_down, emb_ref, halo)
    s, beside = first_features(emb_ref, hot_own), first_features(emb_ref, hot_beside)
    store_tables(tab, [s], [beside], halo)
    groups = (0, 2)
    prepare_weights(rin_ref, rout_ref, ri4, ro3, groups)
    prepare_back(rin_ref, rout_ref, rib, rob, groups)
    count = emb_ref.shape[0]

    @pl.when(par_ref[0] >= 0)
    def _():
        agg = [agg_ref[n] for n in range(4)]
        sm, vm, vg = sm_ref[0], vm_ref[0], vg_ref[0]
        w, size, u, gate = node_forward(agg, sm, vm, vg)
        da, g_sm, g_vm, g_vg = node_backward(agg, w, size, u, gate, sm, vm, vg, cot[0], cot[1:], scale)
        for n in range(4):
            for h in range(2):
                gacc[h, n] = twice(da[n], h)
        row = count + basis_count + 3 * LANES
        for g in (g_sm, g_vm, g_vg):
            grad_ref[row : row + LANES] = g
            row += LANES

    pull[...] = jnp.zeros(pull.shape, F32)
    virial[...] = jnp.zeros(virial.shape, F32)

    def finish(row, h, g, d_dir, d_dist):
        more = dgeom_ref[row]
        dist = g[3:4]
        toward = [g[c : c + 1] for c in range(3)]
        turn = [d_dir[c] + more[c : c + 1] for c in range(3)]
        inner = turn[0] * toward[0] + turn[1] * toward[1] + turn[2] * toward[2]
        stretch = d_dist + more[3:4]
        inverse = 1.0 / dist
        dr = [(turn[c] - toward[c] * inner) * inverse + stretch * toward[c] for c in range(3)]
        r = [toward[c] * dist for c in range(3)]
        lines = jnp.concatenate(dr + [jnp.zeros((13, LANES), F32)], axis=0)
        pull[h] += lines
        products = [r[a] * dr[c] for a in range(3) for c in range(3)]
        virial[...] += jnp.concatenate(products + [jnp.zeros((7, LANES), F32)], axis=0)
        return lines

    backward_edges(
        geom_ref, None, tab, ri4, ro3, rib, rob, gacc, dro, dri, dtab, basis_count, False, finish
    )
    first, second = dtab[0, 0:LANES], dtab[1, 0:LANES]
    own_cot = cot[0] + jnp.where(lane < LANES - halo, first, 0.0) + jnp.where(lane >= halo, second, 0.0)
    side_cot = jnp.where(lane >= LANES - halo, first, 0.0) + jnp.where(lane < halo, second, 0.0)
    grad = 0.0
    for hot, value in ((hot_own, own_cot), (hot_beside, side_cot)):
        hi, lo = split(value)
        grad = grad + (mm_nt(hot, hi) + mm_nt(hot, lo))
    grad_ref[0:count] = grad
    row = count
    radial_grads(dro, dri, grad_ref, row, row + basis_count, basis_count, groups)
    grad_ref[row + basis_count + LANES : row + basis_count + 2 * LANES] = jnp.zeros((LANES, LANES), F32)
    row += basis_count + 6 * LANES
    grad_ref[row:] = jnp.zeros((grad_ref.shape[0] - row, LANES), F32)
    total = jnp.broadcast_to(jnp.sum(virial[...], axis=1, keepdims=True), virial.shape)
    grad_ref[pl.ds(pl.multiple_of(row + 16 * par_ref[1], 16), 16)] = total
    lane16 = lane_ids(16)
    first, second = dtab[0, LANES:], dtab[1, LANES:]
    force_ref[...] = (
        jnp.where(lane16 < LANES - halo, first, 0.0)
        + jnp.where(lane16 >= halo, second, 0.0)
        - folded(pull[0], pull[1])
    )
    even = is_even(par_ref, first.shape)
    send_a[...] = jnp.where(even, second, first)
    send_b[...] = jnp.where(even, first, second)


def sides(a, b, axis):
    size = lax.axis_size(axis)
    pairs_a = [(i, i ^ 1) for i in range(size)]
    pairs_b = [(i, (i + 1) % size if i % 2 else (i - 1) % size) for i in range(size)]
    return lax.ppermute(a, axis, pairs_a), lax.ppermute(b, axis, pairs_b)


def swap(x, axis, bit):
    return lax.ppermute(x, axis, [(i, i ^ bit) for i in range(lax.axis_size(axis))])


def layer_spec(x, layer):
    rest = x.shape[1:]
    return pl.BlockSpec((1,) + rest, lambda i: (layer,) + (0,) * len(rest))


def vmem():
    return pl.BlockSpec(memory_space=pltpu.VMEM)


def smem():
    return pl.BlockSpec(memory_space=pltpu.SMEM)


def f32(*shape):
    return jax.ShapeDtypeStruct(shape, F32)


def params():
    return pltpu.CompilerParams(vmem_limit_bytes=VMEM_LIMIT)


def local(
    frac, species, neighbours, counts, shifts, cell, energy_ref, embedding, radial_in, radial_out, scalar_mix,
    vector_mix, vector_gate, readout_mid, readout_out,
):
    atom_count = frac.shape[1]
    halo = atom_count // 4
    slots = neighbours.shape[0]
    basis_count = radial_in.shape[1]
    me = lax.axis_index("atom")
    group = lax.axis_index("dp")
    lattice = cell[0]
    pos = lattice[0][:, None] * frac[0] + lattice[1][:, None] * frac[1] + lattice[2][:, None] * frac[2]
    own = jnp.concatenate([pos, species.astype(F32)[None], jnp.zeros((4, atom_count), F32)], axis=0)
    side_a, side_b = sides(own, own, "atom")
    par = jnp.stack([me % 2, group]).astype(jnp.int32)
    layer = (radial_in, radial_out, scalar_mix, vector_mix, vector_gate)
    block = f32(LANES, LANES)
    geom, feat, agg, feat_a, feat_b = pl.pallas_call(
        functools.partial(first_kernel, halo),
        grid=(1,),
        out_shape=(f32(slots, 8, LANES), f32(4, LANES, LANES), f32(4, LANES, LANES), block, block),
        in_specs=[smem(), smem()] + [vmem()] * 7 + [layer_spec(x, 0) for x in layer],
        out_specs=[vmem()] * 5,
        scratch_shapes=[
            pltpu.VMEM((2, LANES, 2 * LANES), BF16),
            pltpu.VMEM((LANES, 4 * basis_count), BF16),
            pltpu.VMEM((2 * LANES, 3 * LANES), BF16),
            pltpu.VMEM((2, 4, LANES, LANES), F32),
        ],
        compiler_params=params(),
        name="layer_one",
    )(par, cell, own, side_a, side_b, neighbours, counts[None], shifts, embedding, *layer)
    feat_a, feat_b = sides(feat_a, feat_b, "atom")
    energy_part, cot, cot_a, cot_b, dgeom, grads_two = pl.pallas_call(
        functools.partial(second_kernel, halo),
        grid=(1,),
        out_shape=(f32(8, LANES), f32(4, LANES, LANES), block, block, f32(slots, 8, LANES), f32(G_ROWS, LANES)),
        in_specs=[smem()] + [vmem()] * 4 + [layer_spec(x, 1) for x in layer] + [vmem()] * 2,
        out_specs=[vmem()] * 6,
        scratch_shapes=[
            pltpu.VMEM((2, 4 * LANES, 2 * LANES), BF16),
            pltpu.VMEM((LANES, 4 * basis_count), BF16),
            pltpu.VMEM((3 * LANES, 3 * LANES), BF16),
            pltpu.VMEM((2 * basis_count, 2 * LANES), BF16),
            pltpu.VMEM((2 * LANES, 6 * LANES), BF16),
            pltpu.VMEM((2, 4, LANES, LANES), F32),
            pltpu.VMEM((2, 4, LANES, LANES), F32),
            pltpu.VMEM((3 * LANES, 2 * LANES), F32),
            pltpu.VMEM((LANES, 2 * basis_count), F32),
            pltpu.VMEM((2, 4 * LANES, LANES), F32),
        ],
        compiler_params=params(),
        name="layer_two",
    )(par, geom, feat, feat_a, feat_b, *layer, readout_mid, readout_out[None])
    cot_a, cot_b = sides(cot_a, cot_b, "atom")
    force, force_a, force_b, grads_one = pl.pallas_call(
        functools.partial(third_kernel, halo),
        grid=(1,),
        out_shape=(f32(16, LANES), f32(16, LANES), f32(16, LANES), f32(G_ROWS, LANES)),
        in_specs=[smem()] + [vmem()] * 10 + [layer_spec(x, 0) for x in layer],
        out_specs=[vmem()] * 4,
        scratch_shapes=[
            pltpu.VMEM((2, LANES, 2 * LANES), BF16),
            pltpu.VMEM((LANES, 4 * basis_count), BF16),
            pltpu.VMEM((2 * LANES, 3 * LANES), BF16),
            pltpu.VMEM((2 * basis_count, 2 * LANES), BF16),
            pltpu.VMEM((2 * LANES, 4 * LANES), BF16),
            pltpu.VMEM((2, 4, LANES, LANES), F32),
            pltpu.VMEM((2 * LANES, 2 * LANES), F32),
            pltpu.VMEM((LANES, 2 * basis_count), F32),
            pltpu.VMEM((2, LANES + 16, LANES), F32),
            pltpu.VMEM((2, 16, LANES), F32),
            pltpu.VMEM((16, LANES), F32),
        ],
        compiler_params=params(),
        name="layer_one_back",
    )(par, geom, dgeom, agg, cot, cot_a, cot_b, own, side_a, side_b, embedding, *layer)
    bits = [1 << n for n in range((lax.axis_size("atom") - 1).bit_length())]
    energy = energy_part
    for bit in bits:
        energy = energy + swap(energy, "atom", bit)
    energy_total = energy[0, 0]
    cell_atoms = atom_count * lax.axis_size("atom")
    loss_scale = 2.0 * (energy_total / cell_atoms - energy_ref[0]) / cell_atoms
    force_a, force_b = sides(force_a, force_b, "atom")
    even = me % 2 == 0
    from_next, from_prev = jnp.where(even, force_a, force_b), jnp.where(even, force_b, force_a)
    lane = lax.broadcasted_iota(jnp.int32, (1, atom_count), 1)
    forces = -(
        force
        + jnp.where(lane >= atom_count - halo, from_next, 0.0)
        + jnp.where(lane < halo, from_prev, 0.0)
    )[:3]
    virial_row = embedding.shape[0] + basis_count + 6 * LANES
    is_virial = lax.broadcasted_iota(jnp.int32, (G_ROWS, 1), 0) >= virial_row
    one = grads_one * jnp.where(is_virial, 1.0, loss_scale)
    two = grads_two * loss_scale
    core = group % 2 == 1
    x = jnp.where(core, one, two) + swap(jnp.where(core, two, one), "dp", 1)
    high = group // 2 == 1
    low_part, high_part = x[: G_ROWS // 2], x[G_ROWS // 2 :]
    x = jnp.where(high, high_part, low_part) + swap(jnp.where(high, low_part, high_part), "dp", 2)
    for bit in bits:
        x = x + swap(x, "atom", bit)
    other = swap(x, "dp", 2)
    x = jnp.where(high, jnp.concatenate([other, x]), jnp.concatenate([x, other]))
    other = swap(x, "dp", 1)
    two, one = jnp.where(core, other, x), jnp.where(core, x, other)
    count = embedding.shape[0]
    virial = lax.dynamic_slice_in_dim(one, virial_row + 16 * group, 9, 0)[:, 0].reshape(3, 3)
    det = (
        lattice[0, 0] * (lattice[1, 1] * lattice[2, 2] - lattice[1, 2] * lattice[2, 1])
        - lattice[0, 1] * (lattice[1, 0] * lattice[2, 2] - lattice[1, 2] * lattice[2, 0])
        + lattice[0, 2] * (lattice[1, 0] * lattice[2, 1] - lattice[1, 1] * lattice[2, 0])
    )

    def cut(x, row, groups):
        return jnp.concatenate([x[row + g * LANES : row + (g + 1) * LANES] for g in range(groups)], axis=1)

    row_one, row_two = count + basis_count, basis_count
    mixes = [
        jnp.stack(
            [
                one[row_one + (3 + n) * LANES : row_one + (4 + n) * LANES],
                two[row_two + (3 + n) * LANES : row_two + (4 + n) * LANES],
            ]
        )
        for n in range(3)
    ]
    row = row_two + 6 * LANES
    return (
        energy_total.reshape(1),
        forces,
        (virial / det)[None],
        one[:count],
        jnp.stack([one[count:row_one], two[:row_two]]),
        jnp.stack([cut(one, row_one, 3), cut(two, row_two, 3)]),
        *mixes,
        two[row : row + LANES],
        two[row + LANES],
    )


def solution(mesh):
    both = ("dp", "atom")
    return jax.shard_map(
        local,
        mesh=mesh,
        in_specs=(
            P(None, both), P(both), P(None, both), P(both), P(None, None, both), P("dp", None, None), P("dp"),
        ) + (P(),) * 8,
        out_specs=(P("dp"), P(None, both), P("dp", None, None)) + (P(),) * 8,
        check_vma=False,
    )
```

time: 727 us -> 164 us (0.23); the launches traced: 716 us -> 164 us
  other arithmetic: 230 us -> 5.12 us
  matrix products: 149 us -> 0 us
  local copies, waits for them, and re-layouts: 125 us -> 12.5 us
  blocking collectives: 64.4 us -> 0 us
  Pallas kernels: 0 us -> 56.7 us
  waiting for transfers between devices: 88.2 us -> 57.4 us
  between operations: 25.9 us -> 11.9 us
  starting transfers between devices: 27.5 us -> 19.8 us
    scatter-add x9 -> x0, other arithmetic: 179 us -> none  [the longest x8 156 us: one_block(): gathered = jnp.take(wide_rows, rows, axis=0)]
    dot_general x170 -> x0, matrix products: 149 us -> none  [the longest x32 73.3 us: one_block(): jnp.einsum('kbc,cd->kbd', hidden, radial_out, precision=HIGH)]
    psum x1 -> x0, waiting for transfers between devices: 81.5 us -> none  [local(): lax.psum((scaled[0], scaled[1], scaled[2], scaled[3], scaled[4], scaled[5...]
    psum x2 -> x0, blocking collectives: 64.4 us -> none  [the longest x1 41.6 us: local(): lax.psum((scaled[0], scaled[1], scaled[2], scaled[3], scaled[4], scaled[5...]
    gather x26 -> x0, local copies, waits for them, and re-layouts: 63.4 us -> none  [the longest x24 52 us: one_block(): gathered = jnp.take(wide_rows, rows, axis=0)]
    pallas_call x0 -> x3, Pallas kernels: none -> 56.7 us  [the longest x1 29.9 us: local(): pl.pallas_call(functools.partial(second_kernel, halo), grid=(1,), out_sha...]
    ppermute x12 -> x18, waiting for transfers between devices: 6.71 us -> 57.4 us  [the longest x10 46.5 us: swap(): lax.ppermute(x, axis, [(i, i ^ bit) for i in range(lax.axis_size(axis))])]
    reduce_sum x69 -> x0, other arithmetic: 24.2 us -> none  [the longest x8 8.79 us: one_block(): (filter_direction * neighbour_scalar)[:, :, None, :]]
  transfers between devices with their start and end apart: 13 -> 18, of which waited for: 6 -> 13; matrix products, arithmetic and copies ran while one was open for 7% -> 1% of each run, Pallas kernels for 0% -> 0%
where the time goes in v1:
time: 164 us
  waiting for transfers between devices  57.4 us (35%)
  Pallas kernels  56.7 us (35%)
  starting transfers between devices  19.8 us (12%)
  local copies, waits for them, and re-layouts  12.5 us (8%)
  between operations  11.9 us (7%)
  other arithmetic  5.12 us (3%)
    ppermute x10, waiting for transfers between devices, swap(): lax.ppermute(x, axis, [(i, i ^ bit) for i in range(lax.axis_size(axis))])  46.5 us
    pallas_call x1, Pallas kernels, local(): pl.pallas_call(functools.partial(second_kernel, halo), grid=(1,), out_sha...  29.9 us
    pallas_call x1, Pallas kernels, local(): pl.pallas_call(functools.partial(third_kernel, halo), grid=(1,), out_shap...  17.6 us
    ppermute x8, starting transfers between devices, sides(): return (lax.ppermute(a, axis, pairs_a), lax.ppermute(b, axis, pairs_b))  15.9 us
    ppermute x8, waiting for transfers between devices, sides(): return (lax.ppermute(a, axis, pairs_a), lax.ppermute(b, axis, pairs_b))  10.9 us
    pallas_call x1, Pallas kernels, local(): pl.pallas_call(functools.partial(first_kernel, halo), grid=(1,), out_shap...  9.16 us
    unnamed x35, local copies, waits for them, and re-layouts  7.29 us
    ppermute x10, starting transfers between devices, swap(): lax.ppermute(x, axis, [(i, i ^ bit) for i in range(lax.axis_size(axis))])  3.91 us
  transfers between devices with their start and end apart: 18, of which 13 were waited for; matrix products, arithmetic and copies ran while one was open for 1% of the time, Pallas kernels for 0%

profile of v1, /device:TPU:0, one launch (start us, length us, event | category | flops | bytes accessed | tf_op | source)
XLA Modules:
  0.0 163.5 jit_solution(18221336315986776721)
XLA Ops:
  0.7 0.7 convert_bitcast_fusion
  1.3 0.8 slice_bitcast_fusion.13
  2.1 0.7 slice_bitcast_fusion.14
  3.1 6.0 %collective-permute-start.1 = (f32[8,128]{1,0:T(8,128)S(1)}, f32[8,128]{1,0:T(8,128)S(1)}, u32[]{:S(2)}, u32[]{:S(2)}) collective-permute-start(f32[8,128]{1,0:T(8,128)S(1)} %maximum_maximum_fusion.own_ref), channel_id=1, source_target_pairs={{0,7},{1,2},{2,1},{3,4},{4,3},{5,6},{6,5},{7,0},{8,15},{9,10},{10,... | collective-permute-start | bytes 12296 | tf_op jit(solution)/shard_map/ppermute | solution.py:541
  9.1 0.6 copy-done.16
  9.8 0.9 collective-permute-done.1.b_ref.pb_ref
  10.6 2.0 %collective-permute-done.a_ref.pa_ref = f32[8,128]{1,0:T(8,128)S(1)} collective-permute-done((f32[8,128]{1,0:T(8,128)S(1)}, f32[8,128]{1,0:T(8,128)S(1)}, u32[]{:S(2)}, u32[]{:S(2)}) %collective-permute-start) | collective-permute-done | bytes 4128 | tf_op jit(solution)/shard_map/ppermute | solution.py:541
  12.7 1.0 copy-done
  13.7 0.9 copy-done.2
  14.6 0.9 copy-done.4
  15.5 0.9 copy-done.6
  16.4 0.8 copy-done.9
  17.2 0.8 copy-done.12
  18.0 0.7 copy-done.13
  18.7 9.2 %layer_one.1 = (f32[32,8,128]{2,1,0:T(8,128)S(1)}, f32[4,128,128]{2,1,0:T(8,128)S(1)}, f32[4,128,128]{2,1,0:T(8,128)S(1)}, f32[128,128]{1,0:T(8,128)S(1)}, f32[128,128]{1,0:T(8,128)S(1)}) custom-call(s32[2]{0:T(128)S(1)} %pad_add_fusion.par_ref, f32[1,3,3]{2,1,0:T(4,128)S(1)} %copy.33.cell_ref, f32[8,128]{1,0:T(8,128)S(1)} %maximum_maximum_fusion.own_ref, ...), custom_call_target="tpu_custom_call" | custom-call | tf_op jit(solution)/shard_map/layer_one/pallas_call | solution.py:586
  28.0 2.8 %collective-permute-start.3 = (f32[128,128]{1,0:T(8,128)S(1)}, f32[128,128]{1,0:T(8,128)S(1)}, u32[]{:S(2)}, u32[]{:S(2)}) collective-permute-start(f32[128,128]{1,0:T(8,128)S(1)} %get-tuple-element.29), channel_id=1, source_target_pairs={{0,7},{1,2},{2,1},{3,4},{4,3},{5,6},{6,5},{7,0},{8,15},{9,10},{10,... | collective-permute-start | bytes 196616 | tf_op jit(solution)/shard_map/ppermute | solution.py:541
  30.7 2.2 %collective-permute-done.2.a_ref = f32[128,128]{1,0:T(8,128)S(1)} collective-permute-done((f32[128,128]{1,0:T(8,128)S(1)}, f32[128,128]{1,0:T(8,128)S(1)}, u32[]{:S(2)}, u32[]{:S(2)}) %collective-permute-start.2) | collective-permute-done | bytes 65568 | tf_op jit(solution)/shard_map/ppermute | solution.py:541
  32.9 2.1 %collective-permute-done.3.b_ref = f32[128,128]{1,0:T(8,128)S(1)} collective-permute-done((f32[128,128]{1,0:T(8,128)S(1)}, f32[128,128]{1,0:T(8,128)S(1)}, u32[]{:S(2)}, u32[]{:S(2)}) %collective-permute-start.3) | collective-permute-done | bytes 65568 | tf_op jit(solution)/shard_map/ppermute | solution.py:541
  35.0 0.6 copy-done.14
  35.7 29.9 %layer_two.1 = (f32[8,128]{1,0:T(8,128)S(1)}, f32[4,128,128]{2,1,0:T(8,128)S(1)}, f32[128,128]{1,0:T(8,128)S(1)}, f32[128,128]{1,0:T(8,128)S(1)}, f32[32,8,128]{2,1,0:T(8,128)S(1)}, /*index=5*/f32[992,128]{1,0:T(8,128)S(1)}) custom-call(s32[2]{0:T(128)S(1)} %pad_add_fusion.par_ref, f32[32,8,128]{2,1,0:T(8,128)S(1)} %get-tuple-element.26.geom_ref, ...), custom_call_target="tpu_custom_call" | custom-call | tf_op jit(solution)/shard_map/layer_two/pallas_call | solution.py:602
  65.8 3.5 %collective-permute-done.4 = f32[8,128]{1,0:T(8,128)S(1)} collective-permute-done((f32[8,128]{1,0:T(8,128)S(1)}, f32[8,128]{1,0:T(8,128)S(1)}, u32[]{:S(2)}, u32[]{:S(2)}) %collective-permute-start.4) | collective-permute-done | bytes 4128 | tf_op jit(solution)/shard_map/ppermute | solution.py:545
  69.3 3.6 %collective-permute-done.5 = f32[8,128]{1,0:T(8,128)S(1)} collective-permute-done((f32[8,128]{1,0:T(8,128)S(1)}, f32[8,128]{1,0:T(8,128)S(1)}, u32[]{:S(2)}, u32[]{:S(2)}) %collective-permute-start.5) | collective-permute-done | bytes 4128 | tf_op jit(solution)/shard_map/ppermute | solution.py:545
  73.5 1.9 %collective-permute-start.7 = (f32[128,128]{1,0:T(8,128)S(1)}, f32[128,128]{1,0:T(8,128)S(1)}, u32[]{:S(2)}, u32[]{:S(2)}) collective-permute-start(f32[128,128]{1,0:T(8,128)S(1)} %get-tuple-element.34), channel_id=1, source_target_pairs={{0,1},{1,0},{2,3},{3,2},{4,5},{5,4},{6,7},{7,6},{8,9},{9,8},{10,11... | collective-permute-start | bytes 196616 | tf_op jit(solution)/shard_map/ppermute | solution.py:541
  75.4 2.0 %collective-permute-start.8 = (f32[128,128]{1,0:T(8,128)S(1)}, f32[128,128]{1,0:T(8,128)S(1)}, u32[]{:S(2)}, u32[]{:S(2)}) collective-permute-start(f32[128,128]{1,0:T(8,128)S(1)} %get-tuple-element.35), channel_id=1, source_target_pairs={{0,7},{1,2},{2,1},{3,4},{4,3},{5,6},{6,5},{7,0},{8,15},{9,10},{10,... | collective-permute-start | bytes 196616 | tf_op jit(solution)/shard_map/ppermute | solution.py:541
  77.4 0.5 slice.126
  78.6 3.7 %collective-permute-done.8.b_ref = f32[128,128]{1,0:T(8,128)S(1)} collective-permute-done((f32[128,128]{1,0:T(8,128)S(1)}, f32[128,128]{1,0:T(8,128)S(1)}, u32[]{:S(2)}, u32[]{:S(2)}) %collective-permute-start.8) | collective-permute-done | bytes 65568 | tf_op jit(solution)/shard_map/ppermute | solution.py:541
  82.4 17.6 %layer_one_back.1 = (f32[16,128]{1,0:T(8,128)S(1)}, f32[16,128]{1,0:T(8,128)S(1)}, f32[16,128]{1,0:T(8,128)S(1)}, f32[992,128]{1,0:T(8,128)S(1)}) custom-call(s32[2]{0:T(128)S(1)} %pad_add_fusion.par_ref, f32[32,8,128]{2,1,0:T(8,128)S(1)} %get-tuple-element.26.geom_ref, f32[32,8,128]{2,1,0:T(8,128)S(1)} %get-tuple-element.31.dgeom_ref, ...), custom_call_target="tpu_custom_call" | custom-call | tf_op jit(solution)/shard_map/layer_one_back/pallas_call | solution.py:624
  100.3 1.9 %collective-permute-done.11 = f32[992,128]{1,0:T(8,128)S(1)} collective-permute-done((f32[992,128]{1,0:T(8,128)S(1)}, f32[992,128]{1,0:T(8,128)S(1)}, u32[]{:S(2)}, u32[]{:S(2)}) %collective-permute-start.11) | collective-permute-done | bytes 507936 | tf_op jit(solution)/shard_map/ppermute | solution.py:545
  102.4 1.6 collective-permute-start.12
  103.9 6.7 %collective-permute-done.12 = f32[496,128]{1,0:T(8,128)S(1)} collective-permute-done((f32[496,128]{1,0:T(8,128)S(1)}, f32[496,128]{1,0:T(8,128)S(1)}, u32[]{:S(2)}, u32[]{:S(2)}) %collective-permute-start.12) | collective-permute-done | bytes 253984 | tf_op jit(solution)/shard_map/ppermute | solution.py:545
  110.7 7.3 %collective-permute-done.13 = f32[496,128]{1,0:T(8,128)S(1)} collective-permute-done((f32[496,128]{1,0:T(8,128)S(1)}, f32[496,128]{1,0:T(8,128)S(1)}, u32[]{:S(2)}, u32[]{:S(2)}) %collective-permute-start.13) | collective-permute-done | bytes 253984 | tf_op jit(solution)/shard_map/ppermute | solution.py:545
  118.1 0.3 collective-permute-start.14
  118.4 6.2 %collective-permute-done.14 = f32[496,128]{1,0:T(8,128)S(1)} collective-permute-done((f32[496,128]{1,0:T(8,128)S(1)}, f32[496,128]{1,0:T(8,128)S(1)}, u32[]{:S(2)}, u32[]{:S(2)}) %collective-permute-start.14) | collective-permute-done | bytes 253984 | tf_op jit(solution)/shard_map/ppermute | solution.py:545
  124.7 11.6 %collective-permute-done.15 = f32[496,128]{1,0:T(8,128)S(1)} collective-permute-done((f32[496,128]{1,0:T(8,128)S(1)}, f32[496,128]{1,0:T(8,128)S(1)}, u32[]{:S(2)}, u32[]{:S(2)}) %collective-permute-start.15) | collective-permute-done | bytes 253984 | tf_op jit(solution)/shard_map/ppermute | solution.py:545
  136.4 1.6 collective-permute-start.16
  137.9 5.8 %collective-permute-done.16 = f32[496,128]{1,0:T(8,128)S(1)} collective-permute-done((f32[496,128]{1,0:T(8,128)S(1)}, f32[496,128]{1,0:T(8,128)S(1)}, u32[]{:S(2)}, u32[]{:S(2)}) %collective-permute-start.16) | collective-permute-done | bytes 253984 | tf_op jit(solution)/shard_map/ppermute | solution.py:545
  143.8 0.7 fusion.5
  144.5 1.3 collective-permute-start.9
  145.7 1.9 %collective-permute-start.10 = (f32[16,128]{1,0:T(8,128)S(1)}, f32[16,128]{1,0:T(8,128)S(1)}, u32[]{:S(2)}, u32[]{:S(2)}) collective-permute-start(f32[16,128]{1,0:T(8,128)S(1)} %get-tuple-element.38), channel_id=1, source_target_pairs={{0,7},{1,2},{2,1},{3,4},{4,3},{5,6},{6,5},{7,0},{8,15},{9,10},{10,... | collective-permute-start | bytes 24584 | tf_op jit(solution)/shard_map/ppermute | solution.py:541
  157.4 0.6 fusion.3
  158.1 0.5 slice_bitcast_fusion.8
  158.6 0.6 slice.162
  159.2 0.7 fusion.4
  160.0 0.7 div.41
  160.7 0.7 pad_maximum_fusion.3
  161.3 0.6 pad_maximum_fusion.4
  162.0 0.8 pad_maximum_fusion
  162.8 0.7 pad_maximum_fusion.1
  (63 shorter events, 1.8 us)
Async XLA Ops:
  0.6 12.0 %copy-start.8 = (f32[2,64,128]{2,1,0:T(8,128)S(1)}, f32[2,64,128]{2,1,0:T(8,128)}, u32[]{:S(2)}) copy-start(f32[2,64,128]{2,1,0:T(8,128)} %rin_ref.5) | copy-start | bytes 196612
  3.1 7.6 %collective-permute-start.1 = (f32[8,128]{1,0:T(8,128)S(1)}, f32[8,128]{1,0:T(8,128)S(1)}, u32[]{:S(2)}, u32[]{:S(2)}) collective-permute-start(f32[8,128]{1,0:T(8,128)S(1)} %maximum_maximum_fusion.own_ref), channel_id=1, source_target_pairs={{0,7},{1,2},{2,1},{3,4},{4,3},{5,6},{6,5},{7,0},{8,15},{9,10},{10,... | collective-permute-start | bytes 12296 | tf_op jit(solution)/shard_map/ppermute | solution.py:541
  9.1 3.6 %collective-permute-start = (f32[8,128]{1,0:T(8,128)S(1)}, f32[8,128]{1,0:T(8,128)S(1)}, u32[]{:S(2)}, u32[]{:S(2)}) collective-permute-start(f32[8,128]{1,0:T(8,128)S(1)} %maximum_maximum_fusion.own_ref), channel_id=1, source_target_pairs={{0,1},{1,0},{2,3},{3,2},{4,5},{5,4},{6,7},{7,6},{8,9},{9,8},{10,11... | collective-permute-start | bytes 12296 | tf_op jit(solution)/shard_map/ppermute | solution.py:541
  9.1 0.7 copy-start.16
  9.7 2.9 %copy-start.15 = (s32[128]{0:T(128)S(1)}, s32[128]{0:T(128)}, u32[]{:S(2)}) copy-start(s32[128]{0:T(128)} %param.18) | copy-start | bytes 1540
  12.7 1.0 copy-start
  13.7 0.9 copy-start.2
  14.6 0.9 copy-start.4
  15.5 0.9 copy-start.6
  16.4 0.8 copy-start.9
  17.2 0.8 copy-start.12
  18.0 0.7 copy-start.13
  18.7 16.3 %copy-start.1 = (f32[2,128,384]{2,1,0:T(8,128)S(1)}, f32[2,128,384]{2,1,0:T(8,128)}, u32[]{:S(2)}) copy-start(f32[2,128,384]{2,1,0:T(8,128)} %rout_ref.5) | copy-start | bytes 1179652
  18.7 16.3 %copy-start.3 = (f32[2,128,128]{2,1,0:T(8,128)S(1)}, f32[2,128,128]{2,1,0:T(8,128)}, u32[]{:S(2)}) copy-start(f32[2,128,128]{2,1,0:T(8,128)} %sm_ref.5) | copy-start | bytes 393220
  18.7 16.3 %copy-start.5 = (f32[2,128,128]{2,1,0:T(8,128)S(1)}, f32[2,128,128]{2,1,0:T(8,128)}, u32[]{:S(2)}) copy-start(f32[2,128,128]{2,1,0:T(8,128)} %vm_ref.5) | copy-start | bytes 393220
  18.7 16.3 %copy-start.7 = (f32[2,128,128]{2,1,0:T(8,128)S(1)}, f32[2,128,128]{2,1,0:T(8,128)}, u32[]{:S(2)}) copy-start(f32[2,128,128]{2,1,0:T(8,128)} %vg_ref.5) | copy-start | bytes 393220
  18.7 16.3 %copy-start.11 = (f32[128,128]{1,0:T(8,128)S(1)}, f32[128,128]{1,0:T(8,128)}, u32[]{:S(2)}) copy-start(f32[128,128]{1,0:T(8,128)} %mid_ref.1) | copy-start | bytes 196612
  27.9 5.0 %collective-permute-start.2 = (f32[128,128]{1,0:T(8,128)S(1)}, f32[128,128]{1,0:T(8,128)S(1)}, u32[]{:S(2)}, u32[]{:S(2)}) collective-permute-start(f32[128,128]{1,0:T(8,128)S(1)} %get-tuple-element.28), channel_id=1, source_target_pairs={{0,1},{1,0},{2,3},{3,2},{4,5},{5,4},{6,7},{7,6},{8,9},{9,8},{10,11... | collective-permute-start | bytes 196616 | tf_op jit(solution)/shard_map/ppermute | solution.py:541
  28.0 7.0 %collective-permute-start.3 = (f32[128,128]{1,0:T(8,128)S(1)}, f32[128,128]{1,0:T(8,128)S(1)}, u32[]{:S(2)}, u32[]{:S(2)}) collective-permute-start(f32[128,128]{1,0:T(8,128)S(1)} %get-tuple-element.29), channel_id=1, source_target_pairs={{0,7},{1,2},{2,1},{3,4},{4,3},{5,6},{6,5},{7,0},{8,15},{9,10},{10,... | collective-permute-start | bytes 196616 | tf_op jit(solution)/shard_map/ppermute | solution.py:541
  35.0 0.7 copy-start.14
  65.6 16.8 %copy-start.10 = (f32[96,128]{1,0:T(8,128)S(1)}, f32[96,128]{1,0:T(8,128)}, u32[]{:S(2)}) copy-start(f32[96,128]{1,0:T(8,128)} %emb_ref.3) | copy-start | bytes 147460
  65.6 3.7 %collective-permute-start.4 = (f32[8,128]{1,0:T(8,128)S(1)}, f32[8,128]{1,0:T(8,128)S(1)}, u32[]{:S(2)}, u32[]{:S(2)}) collective-permute-start(f32[8,128]{1,0:T(8,128)S(1)} %get-tuple-element.30), channel_id=1, source_target_pairs={{0,1},{1,0},{2,3},{3,2},{4,5},{5,4},{6,7},{7,6},{8,9},{9,8},{10,11... | collective-permute-start | bytes 12296 | tf_op jit(solution)/shard_map/ppermute | solution.py:545
  69.3 3.6 %collective-permute-start.5 = (f32[8,128]{1,0:T(8,128)S(1)}, f32[8,128]{1,0:T(8,128)S(1)}, u32[]{:S(2)}, u32[]{:S(2)}) collective-permute-start(f32[8,128]{1,0:T(8,128)S(1)} %add.59), channel_id=1, source_target_pairs={{0,2},{1,3},{2,0},{3,1},{4,6},{5,7},{6,4},{7,5},{8,10},{9,11},{10,... | collective-permute-start | bytes 12296 | tf_op jit(solution)/shard_map/ppermute | solution.py:545
  72.9 4.5 %collective-permute-start.6 = (f32[8,128]{1,0:T(8,128)S(1)}, f32[8,128]{1,0:T(8,128)S(1)}, u32[]{:S(2)}, u32[]{:S(2)}) collective-permute-start(f32[8,128]{1,0:T(8,128)S(1)} %add.60), channel_id=1, source_target_pairs={{0,4},{1,5},{2,6},{3,7},{4,0},{5,1},{6,2},{7,3},{8,12},{9,13},{10,... | collective-permute-start | bytes 12296 | tf_op jit(solution)/shard_map/ppermute | solution.py:545
  73.5 5.1 %collective-permute-start.7 = (f32[128,128]{1,0:T(8,128)S(1)}, f32[128,128]{1,0:T(8,128)S(1)}, u32[]{:S(2)}, u32[]{:S(2)}) collective-permute-start(f32[128,128]{1,0:T(8,128)S(1)} %get-tuple-element.34), channel_id=1, source_target_pairs={{0,1},{1,0},{2,3},{3,2},{4,5},{5,4},{6,7},{7,6},{8,9},{9,8},{10,11... | collective-permute-start | bytes 196616 | tf_op jit(solution)/shard_map/ppermute | solution.py:541
  75.4 7.0 %collective-permute-start.8 = (f32[128,128]{1,0:T(8,128)S(1)}, f32[128,128]{1,0:T(8,128)S(1)}, u32[]{:S(2)}, u32[]{:S(2)}) collective-permute-start(f32[128,128]{1,0:T(8,128)S(1)} %get-tuple-element.35), channel_id=1, source_target_pairs={{0,7},{1,2},{2,1},{3,4},{4,3},{5,6},{6,5},{7,0},{8,15},{9,10},{10,... | collective-permute-start | bytes 196616 | tf_op jit(solution)/shard_map/ppermute | solution.py:541
  100.2 2.0 %collective-permute-start.11 = (f32[992,128]{1,0:T(8,128)S(1)}, f32[992,128]{1,0:T(8,128)S(1)}, u32[]{:S(2)}, u32[]{:S(2)}) collective-permute-start(f32[992,128]{1,0:T(8,128)S(1)} %multiply_select_fusion), channel_id=1, source_target_pairs={{0,8},{8,0},{16,24},{24,16},{1,9},{9,1},{17,25},{25,17},{2,10},{10... | collective-permute-start | bytes 1523720 | tf_op jit(solution)/shard_map/ppermute | solution.py:545
  102.4 8.2 %collective-permute-start.12 = (f32[496,128]{1,0:T(8,128)S(1)}, f32[496,128]{1,0:T(8,128)S(1)}, u32[]{:S(2)}, u32[]{:S(2)}) collective-permute-start(f32[496,128]{1,0:T(8,128)S(1)} %slice_select_fusion), channel_id=1, source_target_pairs={{0,16},{8,24},{16,0},{24,8},{1,17},{9,25},{17,1},{25,9},{2,18},{10... | collective-permute-start | bytes 761864 | tf_op jit(solution)/shard_map/ppermute | solution.py:545
  110.7 7.4 %collective-permute-start.13 = (f32[496,128]{1,0:T(8,128)S(1)}, f32[496,128]{1,0:T(8,128)S(1)}, u32[]{:S(2)}, u32[]{:S(2)}) collective-permute-start(f32[496,128]{1,0:T(8,128)S(1)} %select_add_fusion.1), channel_id=1, source_target_pairs={{0,1},{1,0},{2,3},{3,2},{4,5},{5,4},{6,7},{7,6},{8,9},{9,8},{10,11... | collective-permute-start | bytes 761864 | tf_op jit(solution)/shard_map/ppermute | solution.py:545
  118.1 6.5 %collective-permute-start.14 = (f32[496,128]{1,0:T(8,128)S(1)}, f32[496,128]{1,0:T(8,128)S(1)}, u32[]{:S(2)}, u32[]{:S(2)}) collective-permute-start(f32[496,128]{1,0:T(8,128)S(1)} %add.67), channel_id=1, source_target_pairs={{0,2},{1,3},{2,0},{3,1},{4,6},{5,7},{6,4},{7,5},{8,10},{9,11},{10,... | collective-permute-start | bytes 761864 | tf_op jit(solution)/shard_map/ppermute | solution.py:545
  124.6 11.7 %collective-permute-start.15 = (f32[496,128]{1,0:T(8,128)S(1)}, f32[496,128]{1,0:T(8,128)S(1)}, u32[]{:S(2)}, u32[]{:S(2)}) collective-permute-start(f32[496,128]{1,0:T(8,128)S(1)} %add.68), channel_id=1, source_target_pairs={{0,4},{1,5},{2,6},{3,7},{4,0},{5,1},{6,2},{7,3},{8,12},{9,13},{10,... | collective-permute-start | bytes 761864 | tf_op jit(solution)/shard_map/ppermute | solution.py:545
  136.4 7.3 %collective-permute-start.16 = (f32[496,128]{1,0:T(8,128)S(1)}, f32[496,128]{1,0:T(8,128)S(1)}, u32[]{:S(2)}, u32[]{:S(2)}) collective-permute-start(f32[496,128]{1,0:T(8,128)S(1)} %add.69), channel_id=1, source_target_pairs={{0,16},{8,24},{16,0},{24,8},{1,17},{9,25},{17,1},{25,9},{2,18},{10... | collective-permute-start | bytes 761864 | tf_op jit(solution)/shard_map/ppermute | solution.py:545
  143.7 14.3 %collective-permute-start.17 = (f32[992,128]{1,0:T(8,128)S(1)}, f32[992,128]{1,0:T(8,128)S(1)}, u32[]{:S(2)}, u32[]{:S(2)}) collective-permute-start(f32[992,128]{1,0:T(8,128)S(1)} %maximum_select_fusion), channel_id=1, source_target_pairs={{0,8},{8,0},{16,24},{24,16},{1,9},{9,1},{17,25},{25,17},{2,10},{10... | collective-permute-start | bytes 1523720 | tf_op jit(solution)/shard_map/ppermute | solution.py:545
  144.5 12.9 %collective-permute-start.9 = (f32[16,128]{1,0:T(8,128)S(1)}, f32[16,128]{1,0:T(8,128)S(1)}, u32[]{:S(2)}, u32[]{:S(2)}) collective-permute-start(f32[16,128]{1,0:T(8,128)S(1)} %get-tuple-element.37), channel_id=1, source_target_pairs={{0,1},{1,0},{2,3},{3,2},{4,5},{5,4},{6,7},{7,6},{8,9},{9,8},{10,11... | collective-permute-start | bytes 24584 | tf_op jit(solution)/shard_map/ppermute | solution.py:541
  145.7 11.7 %collective-permute-start.10 = (f32[16,128]{1,0:T(8,128)S(1)}, f32[16,128]{1,0:T(8,128)S(1)}, u32[]{:S(2)}, u32[]{:S(2)}) collective-permute-start(f32[16,128]{1,0:T(8,128)S(1)} %get-tuple-element.38), channel_id=1, source_target_pairs={{0,7},{1,2},{2,1},{3,4},{4,3},{5,6},{6,5},{7,0},{8,15},{9,10},{10,... | collective-permute-start | bytes 24584 | tf_op jit(solution)/shard_map/ppermute | solution.py:541

commit v2 on v1

--- a/solution.py
+++ b/solution.py
@@ -11,10 +11,11 @@
 BF16 = jnp.bfloat16
 LANES = 128
 HALF = 64
-FWD_ROWS = 2
-BWD_ROWS = 2
+FWD_ROWS = 16
+BWD_ROWS = 16
 VMEM_LIMIT = 50 * 1024 * 1024
-G_ROWS = 992
+G_ROWS = 928
+MID_ROWS = 88
 
 
 def split(x):
@@ -43,7 +44,7 @@
 
 
 def sigmoid(x):
-    return 1.0 / (1.0 + jnp.exp(-x))
+    return 0.5 * jnp.tanh(0.5 * x) + 0.5
 
 
 def lane_ids(rows):
@@ -276,10 +277,10 @@
     both = dri[...]
     turned = both + pltpu.roll(both, HALF, 1)
     out[row_in : row_in + basis_count] = turned.T[0:basis_count]
-    for place, g in enumerate(groups):
+    for place in range(groups):
         rows = slice(place * LANES, (place + 1) * LANES)
         grad = dro[rows, 0:LANES] + dro[rows, LANES:]
-        out[row_out + g * LANES : row_out + (g + 1) * LANES] = grad.T
+        out[row_out + place * LANES : row_out + (place + 1) * LANES] = grad.T
 
 
 def species_hot(row, count):
@@ -310,6 +311,15 @@
     beside = jnp.where(lane >= LANES - halo, down[3:4], up[3:4])
     hot_own, hot_beside = species_hot(own_ref[3:4], count), species_hot(beside, count)
     return hot_own, hot_beside
+
+
+def place_kernel(cell_ref, frac_ref, species_ref, own_ref):
+    own_ref[...] = jnp.zeros(own_ref.shape, F32)
+    for c in range(3):
+        own_ref[c : c + 1] = (
+            frac_ref[0:1] * cell_ref[0, 0, c] + frac_ref[1:2] * cell_ref[0, 1, c] + frac_ref[2:3] * cell_ref[0, 2, c]
+        )
+    own_ref[3:4] = species_ref[...].astype(F32)
 
 
 def first_kernel(
@@ -372,7 +382,7 @@
 
 def second_kernel(
     halo, par_ref, geom_ref, feat_ref, a_ref, b_ref, rin_ref, rout_ref, sm_ref, vm_ref, vg_ref, mid_ref, out_ref,
-    energy_ref, cot_ref, send_a, send_b, dgeom_ref, grad_ref,
+    cot_ref, send_a, send_b, dgeom_ref, grad_ref, mid_tail,
     tab, ri4, ro3, rib, rob, acc, gacc, dro, dri, dtab,
 ):
     basis_count = rin_ref.shape[1]
@@ -402,7 +412,7 @@
         shown = hidden * act
         weights = jnp.broadcast_to(out_ref[...], (8, LANES))
         per_atom = mm3(weights, shown)
-        energy_ref[...] = jnp.broadcast_to(jnp.sum(per_atom, axis=1, keepdims=True), (8, LANES))
+        send_a[LANES:] = jnp.broadcast_to(jnp.sum(per_atom, axis=1, keepdims=True), (8, LANES))
         weight_column = jnp.broadcast_to(out_ref[...], (LANES, LANES)).T
         d_hidden = weight_column * (act * (1.0 + hidden * (1.0 - act)))
         ds = mm3(mid, d_hidden)
@@ -415,12 +425,13 @@
         for n, x in enumerate([ds] + dv):
             cot_ref[n] = x
         row = basis_count + 3 * LANES
-        for grad in (g_sm, g_vm, g_vg, mm3_nt(s, d_hidden)):
+        for grad in (g_sm, g_vm, g_vg):
             grad_ref[row : row + LANES] = grad
             row += LANES
         grad_ref[row : row + 8] = mm3_nt(jnp.ones((8, LANES), F32), shown)
-        row += 8
-        grad_ref[row:] = jnp.zeros((grad_ref.shape[0] - row, LANES), F32)
+        g_mid = mm3_nt(s, d_hidden)
+        grad_ref[row + 8 :] = g_mid[:MID_ROWS]
+        mid_tail[...] = g_mid[MID_ROWS:]
 
     def finish(row, h, g, d_dir, d_dist):
         for c in range(3):
@@ -431,7 +442,7 @@
     backward_edges(
         geom_ref, dgeom_ref, tab, ri4, ro3, rib, rob, gacc, dro, dri, dtab, basis_count, True, finish
     )
-    radial_grads(dro, dri, grad_ref, 0, basis_count, basis_count, groups)
+    radial_grads(dro, dri, grad_ref, 0, basis_count, basis_count, len(groups))
     firsts = [dtab[0, q * LANES : (q + 1) * LANES] for q in range(4)]
     seconds = [dtab[1, q * LANES : (q + 1) * LANES] for q in range(4)]
     for q in range(4):
@@ -440,13 +451,13 @@
         )
     to_prev, to_next = packed(firsts, halo, True), packed(seconds, halo, False)
     even = is_even(par_ref, to_prev.shape)
-    send_a[...] = jnp.where(even, to_next, to_prev)
+    send_a[:LANES] = jnp.where(even, to_next, to_prev)
     send_b[...] = jnp.where(even, to_prev, to_next)
 
 
 def third_kernel(
-    halo, par_ref, geom_ref, dgeom_ref, agg_ref, cot_ref, a_ref, b_ref, own_ref, pa_ref, pb_ref, emb_ref, rin_ref,
-    rout_ref, sm_ref, vm_ref, vg_ref,
+    halo, par_ref, geom_ref, dgeom_ref, agg_ref, cot_ref, a_ref, b_ref, own_ref, pa_ref, pb_ref, mid_tail, emb_ref,
+    rin_ref, rout_ref, sm_ref, vm_ref, vg_ref,
     force_ref, send_a, send_b, grad_ref,
     tab, ri4, ro3, rib, rob, gacc, dro, dri, dtab, pull, virial,
 ):
@@ -454,7 +465,7 @@
     slots = geom_ref.shape[0]
     scale = slots**-0.5
     lane = lane_ids(LANES)
-    up, down = from_sides(par_ref, a_ref, b_ref)
+    up, down = from_sides(par_ref, a_ref.at[:LANES], b_ref)
     cot = []
     for q in range(4):
         cot.append(
@@ -480,7 +491,7 @@
         for n in range(4):
             for h in range(2):
                 gacc[h, n] = twice(da[n], h)
-        row = count + basis_count + 3 * LANES
+        row = count + basis_count + 2 * LANES
         for g in (g_sm, g_vm, g_vg):
             grad_ref[row : row + LANES] = g
             row += LANES
@@ -516,10 +527,10 @@
         grad = grad + (mm_nt(hot, hi) + mm_nt(hot, lo))
     grad_ref[0:count] = grad
     row = count
-    radial_grads(dro, dri, grad_ref, row, row + basis_count, basis_count, groups)
-    grad_ref[row + basis_count + LANES : row + basis_count + 2 * LANES] = jnp.zeros((LANES, LANES), F32)
-    row += basis_count + 6 * LANES
+    radial_grads(dro, dri, grad_ref, row, row + basis_count, basis_count, len(groups))
+    row += basis_count + 5 * LANES
     grad_ref[row:] = jnp.zeros((grad_ref.shape[0] - row, LANES), F32)
+    grad_ref[row + 64 : row + 64 + mid_tail.shape[0]] = mid_tail[...]
     total = jnp.broadcast_to(jnp.sum(virial[...], axis=1, keepdims=True), virial.shape)
     grad_ref[pl.ds(pl.multiple_of(row + 16 * par_ref[1], 16), 16)] = total
     lane16 = lane_ids(16)
@@ -534,6 +545,63 @@
     send_b[...] = jnp.where(even, first, second)
 
 
+def final_kernel(
+    halo, par_ref, cell_ref, sum_energy, force_ref, a_ref, b_ref, mine, other,
+    energy_ref, forces_ref, stress_ref, emb_ref, rin_ref, rout_ref, sm_ref, vm_ref, vg_ref, mid_ref, out_ref,
+):
+    energy_ref[0, 0] = jnp.max(sum_energy[0:1])
+    lane = lane_ids(16)
+    up, down = from_sides(par_ref, a_ref, b_ref)
+    force = force_ref[...] + jnp.where(lane >= LANES - halo, up, 0.0) + jnp.where(lane < halo, down, 0.0)
+    forces_ref[...] = -force[0:3]
+    count, basis_count = emb_ref.shape[0], rin_ref.shape[1]
+    m = [[cell_ref[0, a, c] for c in range(3)] for a in range(3)]
+    det = (
+        m[0][0] * (m[1][1] * m[2][2] - m[1][2] * m[2][1])
+        - m[0][1] * (m[1][0] * m[2][2] - m[1][2] * m[2][0])
+        + m[0][2] * (m[1][0] * m[2][1] - m[1][1] * m[2][0])
+    )
+
+    def write(one, two):
+        emb_ref[...] = one[0:count]
+        row = count
+        rin_ref[0] = one[row : row + basis_count]
+        rin_ref[1] = two[0:basis_count]
+        row += basis_count
+        rout_ref[0, :, 0:LANES] = one[row : row + LANES]
+        rout_ref[0, :, LANES : 2 * LANES] = jnp.zeros((LANES, LANES), F32)
+        rout_ref[0, :, 2 * LANES :] = one[row + LANES : row + 2 * LANES]
+        row += 2 * LANES
+        line = basis_count
+        for g in range(3):
+            rout_ref[1, :, g * LANES : (g + 1) * LANES] = two[line : line + LANES]
+            line += LANES
+        for ref in (sm_ref, vm_ref, vg_ref):
+            ref[0] = one[row : row + LANES]
+            ref[1] = two[line : line + LANES]
+            row += LANES
+            line += LANES
+        out_ref[...] = two[line : line + 1]
+        mid_ref[0:MID_ROWS] = two[line + 8 : line + 8 + MID_ROWS]
+        mid_ref[MID_ROWS:] = one[row + 64 : row + 64 + LANES - MID_ROWS]
+        virial = one[pl.ds(pl.multiple_of(row + 16 * par_ref[1], 16), 16)]
+        place = lane_ids(1)
+        lines = [
+            jnp.where(place == 0, virial[3 * a : 3 * a + 1], jnp.where(place == 1, virial[3 * a + 1 : 3 * a + 2], virial[3 * a + 2 : 3 * a + 3]))
+            for a in range(3)
+        ]
+        stress = jnp.concatenate(lines, axis=0) / (jnp.zeros((3, LANES), F32) + det)
+        stress_ref[0] = stress[:, 0:3]
+
+    @pl.when(par_ref[1] % 2 == 0)
+    def _():
+        write(other, mine)
+
+    @pl.when(par_ref[1] % 2 == 1)
+    def _():
+        write(mine, other)
+
+
 def sides(a, b, axis):
     size = lax.axis_size(axis)
     pairs_a = [(i, i ^ 1) for i in range(size)]
@@ -558,12 +626,36 @@
     return pl.BlockSpec(memory_space=pltpu.SMEM)
 
 
+def whole(x):
+    return pl.BlockSpec(x.shape, lambda i: (0,) * len(x.shape))
+
+
 def f32(*shape):
     return jax.ShapeDtypeStruct(shape, F32)
 
 
-def params():
-    return pltpu.CompilerParams(vmem_limit_bytes=VMEM_LIMIT)
+def call(kernel, name, outs, in_specs, out_specs, scratch, flops, *args):
+    return pl.pallas_call(
+        kernel,
+        grid=(1,),
+        out_shape=outs,
+        in_specs=in_specs,
+        out_specs=out_specs,
+        scratch_shapes=scratch,
+        compiler_params=pltpu.CompilerParams(vmem_limit_bytes=VMEM_LIMIT),
+        cost_estimate=pl.CostEstimate(flops=flops, bytes_accessed=flops // 500, transcendentals=0),
+        name=name,
+    )(*args)
+
+
+def exchange(x, moves):
+    groups, slabs = lax.axis_size("dp"), lax.axis_size("atom")
+    route = []
+    for g in range(groups):
+        for p in range(slabs):
+            to_g, to_p = moves(g, p)
+            route.append((g * slabs + p, to_g * slabs + to_p))
+    return lax.ppermute(x, ("dp", "atom"), route)
 
 
 def local(
@@ -576,36 +668,42 @@
     basis_count = radial_in.shape[1]
     me = lax.axis_index("atom")
     group = lax.axis_index("dp")
-    lattice = cell[0]
-    pos = lattice[0][:, None] * frac[0] + lattice[1][:, None] * frac[1] + lattice[2][:, None] * frac[2]
-    own = jnp.concatenate([pos, species.astype(F32)[None], jnp.zeros((4, atom_count), F32)], axis=0)
+    species_row, counts_row, out_row = species[None], counts[None], readout_out[None]
+    own = call(
+        place_kernel, "place", f32(8, LANES), [smem(), whole(frac), whole(species_row)], vmem(), [], 10**6,
+        cell, frac, species_row,
+    )
     side_a, side_b = sides(own, own, "atom")
     par = jnp.stack([me % 2, group]).astype(jnp.int32)
     layer = (radial_in, radial_out, scalar_mix, vector_mix, vector_gate)
     block = f32(LANES, LANES)
-    geom, feat, agg, feat_a, feat_b = pl.pallas_call(
+    geom, feat, agg, feat_a, feat_b = call(
         functools.partial(first_kernel, halo),
-        grid=(1,),
-        out_shape=(f32(slots, 8, LANES), f32(4, LANES, LANES), f32(4, LANES, LANES), block, block),
-        in_specs=[smem(), smem()] + [vmem()] * 7 + [layer_spec(x, 0) for x in layer],
-        out_specs=[vmem()] * 5,
-        scratch_shapes=[
+        "layer_one",
+        (f32(slots, 8, LANES), f32(4, LANES, LANES), f32(4, LANES, LANES), block, block),
+        [smem(), smem()] + [vmem()] * 3 + [whole(x) for x in (neighbours, counts_row, shifts, embedding)]
+        + [layer_spec(x, 0) for x in layer],
+        [vmem()] * 5,
+        [
             pltpu.VMEM((2, LANES, 2 * LANES), BF16),
             pltpu.VMEM((LANES, 4 * basis_count), BF16),
             pltpu.VMEM((2 * LANES, 3 * LANES), BF16),
             pltpu.VMEM((2, 4, LANES, LANES), F32),
         ],
-        compiler_params=params(),
-        name="layer_one",
-    )(par, cell, own, side_a, side_b, neighbours, counts[None], shifts, embedding, *layer)
+        3 * 10**9,
+        par, cell, own, side_a, side_b, neighbours, counts_row, shifts, embedding, *layer,
+    )
     feat_a, feat_b = sides(feat_a, feat_b, "atom")
-    energy_part, cot, cot_a, cot_b, dgeom, grads_two = pl.pallas_call(
+    cot, cot_a, cot_b, dgeom, grads_two, mid_tail = call(
         functools.partial(second_kernel, halo),
-        grid=(1,),
-        out_shape=(f32(8, LANES), f32(4, LANES, LANES), block, block, f32(slots, 8, LANES), f32(G_ROWS, LANES)),
-        in_specs=[smem()] + [vmem()] * 4 + [layer_spec(x, 1) for x in layer] + [vmem()] * 2,
-        out_specs=[vmem()] * 6,
-        scratch_shapes=[
+        "layer_two",
+        (
+            f32(4, LANES, LANES), f32(LANES + 8, LANES), block, f32(slots, 8, LANES), f32(G_ROWS, LANES),
+            f32(LANES - MID_ROWS, LANES),
+        ),
+        [smem()] + [vmem()] * 4 + [layer_spec(x, 1) for x in layer] + [whole(readout_mid), whole(out_row)],
+        [vmem()] * 6,
+        [
             pltpu.VMEM((2, 4 * LANES, 2 * LANES), BF16),
             pltpu.VMEM((LANES, 4 * basis_count), BF16),
             pltpu.VMEM((3 * LANES, 3 * LANES), BF16),
@@ -617,17 +715,22 @@
             pltpu.VMEM((LANES, 2 * basis_count), F32),
             pltpu.VMEM((2, 4 * LANES, LANES), F32),
         ],
-        compiler_params=params(),
-        name="layer_two",
-    )(par, geom, feat, feat_a, feat_b, *layer, readout_mid, readout_out[None])
+        10**10,
+        par, geom, feat, feat_a, feat_b, *layer, readout_mid, out_row,
+    )
+    energy = cot_a[LANES:]
     cot_a, cot_b = sides(cot_a, cot_b, "atom")
-    force, force_a, force_b, grads_one = pl.pallas_call(
+    energy = energy + cot_a[LANES:]
+    bits = [1 << n for n in range(1, (lax.axis_size("atom") - 1).bit_length())]
+    for bit in bits[:1]:
+        energy = energy + swap(energy, "atom", bit)
+    force, force_a, force_b, grads_one = call(
         functools.partial(third_kernel, halo),
-        grid=(1,),
-        out_shape=(f32(16, LANES), f32(16, LANES), f32(16, LANES), f32(G_ROWS, LANES)),
-        in_specs=[smem()] + [vmem()] * 10 + [layer_spec(x, 0) for x in layer],
-        out_specs=[vmem()] * 4,
-        scratch_shapes=[
+        "layer_one_back",
+        (f32(16, LANES), f32(16, LANES), f32(16, LANES), f32(G_ROWS, LANES)),
+        [smem()] + [vmem()] * 11 + [layer_spec(x, 0) for x in layer],
+        [vmem()] * 4,
+        [
             pltpu.VMEM((2, LANES, 2 * LANES), BF16),
             pltpu.VMEM((LANES, 4 * basis_count), BF16),
             pltpu.VMEM((2 * LANES, 3 * LANES), BF16),
@@ -640,73 +743,54 @@
             pltpu.VMEM((2, 16, LANES), F32),
             pltpu.VMEM((16, LANES), F32),
         ],
-        compiler_params=params(),
-        name="layer_one_back",
-    )(par, geom, dgeom, agg, cot, cot_a, cot_b, own, side_a, side_b, embedding, *layer)
-    bits = [1 << n for n in range((lax.axis_size("atom") - 1).bit_length())]
-    energy = energy_part
-    for bit in bits:
+        6 * 10**9,
+        par, geom, dgeom, agg, cot, cot_a, cot_b, own, side_a, side_b, mid_tail, embedding, *layer,
+    )
+    for bit in bits[1:]:
         energy = energy + swap(energy, "atom", bit)
-    energy_total = energy[0, 0]
+    force_a, force_b = sides(force_a, force_b, "atom")
     cell_atoms = atom_count * lax.axis_size("atom")
-    loss_scale = 2.0 * (energy_total / cell_atoms - energy_ref[0]) / cell_atoms
-    force_a, force_b = sides(force_a, force_b, "atom")
-    even = me % 2 == 0
-    from_next, from_prev = jnp.where(even, force_a, force_b), jnp.where(even, force_b, force_a)
-    lane = lax.broadcasted_iota(jnp.int32, (1, atom_count), 1)
-    forces = -(
-        force
-        + jnp.where(lane >= atom_count - halo, from_next, 0.0)
-        + jnp.where(lane < halo, from_prev, 0.0)
-    )[:3]
-    virial_row = embedding.shape[0] + basis_count + 6 * LANES
-    is_virial = lax.broadcasted_iota(jnp.int32, (G_ROWS, 1), 0) >= virial_row
-    one = grads_one * jnp.where(is_virial, 1.0, loss_scale)
+    loss_scale = 2.0 * (energy[0, 0] / cell_atoms - energy_ref[0]) / cell_atoms
+    virial_row = embedding.shape[0] + basis_count + 5 * LANES
+    line = lax.broadcasted_iota(jnp.int32, (G_ROWS, 1), 0)
+    one = grads_one * jnp.where((line >= virial_row) & (line < virial_row + 64), 1.0, loss_scale)
     two = grads_two * loss_scale
     core = group % 2 == 1
     x = jnp.where(core, one, two) + swap(jnp.where(core, two, one), "dp", 1)
-    high = group // 2 == 1
-    low_part, high_part = x[: G_ROWS // 2], x[G_ROWS // 2 :]
-    x = jnp.where(high, high_part, low_part) + swap(jnp.where(high, low_part, high_part), "dp", 2)
-    for bit in bits:
-        x = x + swap(x, "atom", bit)
-    other = swap(x, "dp", 2)
-    x = jnp.where(high, jnp.concatenate([other, x]), jnp.concatenate([x, other]))
+    x, force_a, force_b = lax.optimization_barrier((x, force_a, force_b))
+    far = [b for b in bits[1:]]
+    across, along = group // 2 == 1, (me // 2) % 2 == 1
+    upper = (jnp.where(core, along, across), jnp.where(core, across, along))
+
+    def x_or_z(g, p, turned):
+        return (g, p ^ 2) if (g % 2 == 1) != turned else (g ^ 2, p)
+
+    for n in range(2):
+        half = x.shape[0] // 2
+        low_part, high_part = x[:half], x[half:]
+        sent = jnp.where(upper[n], low_part, high_part)
+        x = jnp.where(upper[n], high_part, low_part) + exchange(sent, lambda g, p: x_or_z(g, p, n == 1))
+    order = [1] + far
+    for n in range(len(order)):
+        first, second = order[n], order[(n + 1) % len(order)]
+        x = x + exchange(x, lambda g, p: (g, p ^ (second if g % 2 else first)))
+    for n in (1, 0):
+        received = exchange(x, lambda g, p: x_or_z(g, p, n == 1))
+        x = jnp.where(upper[n], jnp.concatenate([received, x]), jnp.concatenate([x, received]))
     other = swap(x, "dp", 1)
-    two, one = jnp.where(core, other, x), jnp.where(core, x, other)
-    count = embedding.shape[0]
-    virial = lax.dynamic_slice_in_dim(one, virial_row + 16 * group, 9, 0)[:, 0].reshape(3, 3)
-    det = (
-        lattice[0, 0] * (lattice[1, 1] * lattice[2, 2] - lattice[1, 2] * lattice[2, 1])
-        - lattice[0, 1] * (lattice[1, 0] * lattice[2, 2] - lattice[1, 2] * lattice[2, 0])
-        + lattice[0, 2] * (lattice[1, 0] * lattice[2, 1] - lattice[1, 1] * lattice[2, 0])
-    )
-
-    def cut(x, row, groups):
-        return jnp.concatenate([x[row + g * LANES : row + (g + 1) * LANES] for g in range(groups)], axis=1)
-
-    row_one, row_two = count + basis_count, basis_count
-    mixes = [
-        jnp.stack(
-            [
-                one[row_one + (3 + n) * LANES : row_one + (4 + n) * LANES],
-                two[row_two + (3 + n) * LANES : row_two + (4 + n) * LANES],
-            ]
-        )
-        for n in range(3)
-    ]
-    row = row_two + 6 * LANES
-    return (
-        energy_total.reshape(1),
-        forces,
-        (virial / det)[None],
-        one[:count],
-        jnp.stack([one[count:row_one], two[:row_two]]),
-        jnp.stack([cut(one, row_one, 3), cut(two, row_two, 3)]),
-        *mixes,
-        two[row : row + LANES],
-        two[row + LANES],
-    )
+    weights = (embedding,) + layer + (readout_mid, out_row)
+    outs = (f32(1, 1), f32(3, atom_count), f32(1, 3, 3)) + tuple(f32(*x.shape) for x in weights)
+    result = call(
+        functools.partial(final_kernel, halo),
+        "final",
+        outs,
+        [smem(), smem()] + [vmem()] * 6,
+        [smem()] + [whole(x) for x in outs[1:]],
+        [],
+        10**8,
+        par, cell, energy, force, force_a, force_b, x, other,
+    )
+    return (result[0].reshape(1),) + tuple(result[1:-1]) + (result[-1].reshape(LANES),)
 
 
 def solution(mesh):

time: 164 us -> 114 us (0.70)
  Pallas kernels: 56.7 us -> 33.2 us
  waiting for transfers between devices: 57.4 us -> 46.6 us
  between operations: 11.9 us -> 2.21 us
  other arithmetic: 5.12 us -> 0.69 us
  local copies, waits for them, and re-layouts: 12.5 us -> 9.15 us
  starting transfers between devices: 19.8 us -> 22.1 us
    ppermute x10 -> x4, waiting for transfers between devices: 46.5 us -> 4.78 us  [swap(): lax.ppermute(x, axis, [(i, i ^ bit) for i in range(lax.axis_size(axis))])]
    ppermute x0 -> x6, waiting for transfers between devices: none -> 30.2 us  [exchange(): return lax.ppermute(x, ('dp', 'atom'), route)]
    pallas_call x3 -> x5, Pallas kernels: 56.7 us -> 33.2 us  [call(): pl.pallas_call(kernel, grid=(1,), out_shape=outs, in_specs=in_specs, out_...]
    ppermute x0 -> x6, starting transfers between devices: none -> 3.89 us  [exchange(): return lax.ppermute(x, ('dp', 'atom'), route)]
    ppermute x10 -> x4, starting transfers between devices: 3.91 us -> 0.93 us  [swap(): lax.ppermute(x, axis, [(i, i ^ bit) for i in range(lax.axis_size(axis))])]
    another operation x5 -> x0, other arithmetic: 2.81 us -> none  [the longest x2 1.38 us: local(): jnp.stack([one[row_one + (3 + n) * LANES:row_one + (4 + n) * LANES], two[...]
    slice x4 -> x1, local copies, waits for them, and re-layouts: 2.46 us -> 0.52 us  [local(): loss_scale = 2.0 * (energy[0, 0] / cell_atoms - energy_ref[0]) / cell_atoms]
    unnamed x35 -> x40, local copies, waits for them, and re-layouts: 7.29 us -> 8.63 us
  transfers between devices with their start and end apart: 18 -> 18, of which waited for: 13 -> 14; matrix products, arithmetic and copies ran while one was open for 1% -> 0% of each run, Pallas kernels for 0% -> 8%
where the time goes in v2:
time: 114 us
  waiting for transfers between devices  46.6 us (41%)
  Pallas kernels  33.2 us (29%)
  starting transfers between devices  22.1 us (19%)
  local copies, waits for them, and re-layouts  9.15 us (8%)
  between operations  2.21 us (2%)
    pallas_call x5, Pallas kernels, call(): pl.pallas_call(kernel, grid=(1,), out_shape=outs, in_specs=in_specs, out_...  33.2 us
    ppermute x6, waiting for transfers between devices, exchange(): return lax.ppermute(x, ('dp', 'atom'), route)  30.2 us
    ppermute x8, starting transfers between devices, sides(): return (lax.ppermute(a, axis, pairs_a), lax.ppermute(b, axis, pairs_b))  17.2 us
    ppermute x8, waiting for transfers between devices, sides(): return (lax.ppermute(a, axis, pairs_a), lax.ppermute(b, axis, pairs_b))  11.6 us
    unnamed x40, local copies, waits for them, and re-layouts  8.63 us
    ppermute x4, waiting for transfers between devices, swap(): lax.ppermute(x, axis, [(i, i ^ bit) for i in range(lax.axis_size(axis))])  4.78 us
    ppermute x6, starting transfers between devices, exchange(): return lax.ppermute(x, ('dp', 'atom'), route)  3.89 us
  transfers between devices with their start and end apart: 18, of which 14 were waited for; matrix products, arithmetic and copies ran while one was open for 0% of the time, Pallas kernels for 8%

profile of v2, /device:TPU:0, one launch (start us, length us, event | category | flops | bytes accessed | tf_op | source)
XLA Modules:
  0.0 113.9 jit_solution(17530443361986845938)
XLA Ops:
  0.7 0.7 copy.28.cell_ref
  1.3 0.6 copy-done.1
  2.0 0.6 place.1.own_ref
  2.6 3.0 %collective-permute-start = (f32[8,128]{1,0:T(8,128)S(1)}, f32[8,128]{1,0:T(8,128)S(1)}, u32[]{:S(2)}, u32[]{:S(2)}) collective-permute-start(f32[8,128]{1,0:T(8,128)S(1)} %place.1.own_ref), channel_id=1, source_target_pairs={{0,1},{1,0},{2,3},{3,2},{4,5},{5,4},{6,7},{7,6},{8,9},{9,8},{10,11... | collective-permute-start | bytes 12296 | tf_op jit(solution)/shard_map/ppermute | solution.py:609
  5.6 3.5 %collective-permute-start.1 = (f32[8,128]{1,0:T(8,128)S(1)}, f32[8,128]{1,0:T(8,128)S(1)}, u32[]{:S(2)}, u32[]{:S(2)}) collective-permute-start(f32[8,128]{1,0:T(8,128)S(1)} %place.1.own_ref), channel_id=1, source_target_pairs={{0,7},{1,2},{2,1},{3,4},{4,3},{5,6},{6,5},{7,0},{8,15},{9,10},{10,... | collective-permute-start | bytes 12296 | tf_op jit(solution)/shard_map/ppermute | solution.py:609
  9.2 0.1 pad_add_fusion.par_ref
  9.2 2.7 %collective-permute-done.1.b_ref.pb_ref = f32[8,128]{1,0:T(8,128)S(1)} collective-permute-done((f32[8,128]{1,0:T(8,128)S(1)}, f32[8,128]{1,0:T(8,128)S(1)}, u32[]{:S(2)}, u32[]{:S(2)}) %collective-permute-start.1) | collective-permute-done | bytes 4128 | tf_op jit(solution)/shard_map/ppermute | solution.py:609
  11.9 1.0 copy-done.2
  12.9 0.9 copy-done.4
  13.8 0.9 copy-done.6
  14.7 0.9 copy-done.8
  15.6 0.8 copy-done.11
  16.5 0.8 copy-done.14
  17.3 0.7 copy-done.16
  18.0 4.3 %layer_one.1 = (f32[32,8,128]{2,1,0:T(8,128)S(1)}, f32[4,128,128]{2,1,0:T(8,128)S(1)}, f32[4,128,128]{2,1,0:T(8,128)S(1)}, f32[128,128]{1,0:T(8,128)S(1)}, f32[128,128]{1,0:T(8,128)S(1)}) custom-call(s32[2]{0:T(128)S(1)} %pad_add_fusion.par_ref, f32[1,3,3]{2,1,0:T(4,128)S(1)} %copy.28.cell_ref, f32[8,128]{1,0:T(8,128)S(1)} %place.1.own_ref, ...), custom_call_target="tpu_custom_call" | custom-call | flops 3000000000 | bytes 6000000 | tf_op jit(solution)/shard_map/layer_one/pallas_call | solution.py:638
  22.4 3.6 %collective-permute-start.3 = (f32[128,128]{1,0:T(8,128)S(1)}, f32[128,128]{1,0:T(8,128)S(1)}, u32[]{:S(2)}, u32[]{:S(2)}) collective-permute-start(f32[128,128]{1,0:T(8,128)S(1)} %get-tuple-element.43), channel_id=1, source_target_pairs={{0,7},{1,2},{2,1},{3,4},{4,3},{5,6},{6,5},{7,0},{8,15},{9,10},{10,... | collective-permute-start | bytes 196616 | tf_op jit(solution)/shard_map/ppermute | solution.py:609
  26.0 1.3 %collective-permute-done.2.a_ref = f32[128,128]{1,0:T(8,128)S(1)} collective-permute-done((f32[128,128]{1,0:T(8,128)S(1)}, f32[128,128]{1,0:T(8,128)S(1)}, u32[]{:S(2)}, u32[]{:S(2)}) %collective-permute-start.2) | collective-permute-done | bytes 65568 | tf_op jit(solution)/shard_map/ppermute | solution.py:609
  27.3 2.1 %collective-permute-done.3.b_ref = f32[128,128]{1,0:T(8,128)S(1)} collective-permute-done((f32[128,128]{1,0:T(8,128)S(1)}, f32[128,128]{1,0:T(8,128)S(1)}, u32[]{:S(2)}, u32[]{:S(2)}) %collective-permute-start.3) | collective-permute-done | bytes 65568 | tf_op jit(solution)/shard_map/ppermute | solution.py:609
  29.4 0.6 copy-done.18
  30.1 17.6 %layer_two.1 = (f32[4,128,128]{2,1,0:T(8,128)S(1)}, f32[136,128]{1,0:T(8,128)S(1)}, f32[128,128]{1,0:T(8,128)S(1)}, f32[32,8,128]{2,1,0:T(8,128)S(1)}, f32[928,128]{1,0:T(8,128)S(1)}, /*index=5*/f32[40,128]{1,0:T(8,128)S(1)}) custom-call(s32[2]{0:T(128)S(1)} %pad_add_fusion.par_ref, f32[32,8,128]{2,1,0:T(8,128)S(1)} %get-tuple-element.40.geom_ref, ...), custom_call_target="tpu_custom_call" | custom-call | flops 10000000000 | bytes 20000000 | tf_op jit(solution)/shard_map/layer_two/pallas_call | solution.py:638
  47.7 0.2 collective-permute-start.4
  48.0 3.5 %collective-permute-start.7 = (f32[128,128]{1,0:T(8,128)S(1)}, f32[128,128]{1,0:T(8,128)S(1)}, u32[]{:S(2)}, u32[]{:S(2)}) collective-permute-start(f32[128,128]{1,0:T(8,128)S(1)} %get-tuple-element.48), channel_id=1, source_target_pairs={{0,7},{1,2},{2,1},{3,4},{4,3},{5,6},{6,5},{7,0},{8,15},{9,10},{10,... | collective-permute-start | bytes 196616 | tf_op jit(solution)/shard_map/ppermute | solution.py:609
  51.5 0.6 collective-permute-done.4.a_ref
  52.8 2.9 %collective-permute-done.5 = f32[8,128]{1,0:T(8,128)S(1)} collective-permute-done((f32[8,128]{1,0:T(8,128)S(1)}, f32[8,128]{1,0:T(8,128)S(1)}, u32[]{:S(2)}, u32[]{:S(2)}) %collective-permute-start.5) | collective-permute-done | bytes 4128 | tf_op jit(solution)/shard_map/ppermute | solution.py:613
  55.7 0.8 collective-permute-start.6
  56.5 9.0 %layer_one_back.1 = (f32[16,128]{1,0:T(8,128)S(1)}, f32[16,128]{1,0:T(8,128)S(1)}, f32[16,128]{1,0:T(8,128)S(1)}, f32[928,128]{1,0:T(8,128)S(1)}) custom-call(s32[2]{0:T(128)S(1)} %pad_add_fusion.par_ref, f32[32,8,128]{2,1,0:T(8,128)S(1)} %get-tuple-element.40.geom_ref, f32[32,8,128]{2,1,0:T(8,128)S(1)} %get-tuple-element.45.dgeom_ref, ...), custom_call_target="tpu_custom_call" | custom-call | flops 6000000000 | bytes 12000000 | tf_op jit(solution)/shard_map/layer_one_back/pallas_call | solution.py:638
  65.6 0.5 slice.23
  66.8 0.2 multiply_select_fusion
  67.0 0.1 collective-permute-start.8
  67.1 2.0 %collective-permute-start.9 = (f32[16,128]{1,0:T(8,128)S(1)}, f32[16,128]{1,0:T(8,128)S(1)}, u32[]{:S(2)}, u32[]{:S(2)}) collective-permute-start(f32[16,128]{1,0:T(8,128)S(1)} %get-tuple-element.53), channel_id=1, source_target_pairs={{0,1},{1,0},{2,3},{3,2},{4,5},{5,4},{6,7},{7,6},{8,9},{9,8},{10,11... | collective-permute-start | bytes 24584 | tf_op jit(solution)/shard_map/ppermute | solution.py:609
  69.0 1.3 %collective-permute-start.10 = (f32[16,128]{1,0:T(8,128)S(1)}, f32[16,128]{1,0:T(8,128)S(1)}, u32[]{:S(2)}, u32[]{:S(2)}) collective-permute-start(f32[16,128]{1,0:T(8,128)S(1)} %get-tuple-element.54), channel_id=1, source_target_pairs={{0,7},{1,2},{2,1},{3,4},{4,3},{5,6},{6,5},{7,0},{8,15},{9,10},{10,... | collective-permute-start | bytes 24584 | tf_op jit(solution)/shard_map/ppermute | solution.py:609
  70.3 0.2 select_add_fusion
  70.5 0.3 collective-permute-done.9.a_ref
  70.8 4.6 %collective-permute-done.10.b_ref = f32[16,128]{1,0:T(8,128)S(1)} collective-permute-done((f32[16,128]{1,0:T(8,128)S(1)}, f32[16,128]{1,0:T(8,128)S(1)}, u32[]{:S(2)}, u32[]{:S(2)}) %collective-permute-start.10) | collective-permute-done | bytes 8224 | tf_op jit(solution)/shard_map/ppermute | solution.py:609
  75.4 1.6 %collective-permute-start.11 = (f32[464,128]{1,0:T(8,128)S(1)}, f32[464,128]{1,0:T(8,128)S(1)}, u32[]{:S(2)}, u32[]{:S(2)}) collective-permute-start(f32[464,128]{1,0:T(8,128)S(1)} %slice_select_fusion), channel_id=1, source_target_pairs={{0,16},{1,17},{2,18},{3,19},{4,20},{5,21},{6,22},{7,23},{8,10},{9,... | collective-permute-start | bytes 712712 | tf_op jit(solution)/shard_map/ppermute | solution.py:658
  77.0 4.6 %collective-permute-done.11 = f32[464,128]{1,0:T(8,128)S(1)} collective-permute-done((f32[464,128]{1,0:T(8,128)S(1)}, f32[464,128]{1,0:T(8,128)S(1)}, u32[]{:S(2)}, u32[]{:S(2)}) %collective-permute-start.11) | collective-permute-done | bytes 237600 | tf_op jit(solution)/shard_map/ppermute | solution.py:658
  81.7 0.3 collective-permute-start.12
  82.0 4.6 %collective-permute-done.12 = f32[232,128]{1,0:T(8,128)S(1)} collective-permute-done((f32[232,128]{1,0:T(8,128)S(1)}, f32[232,128]{1,0:T(8,128)S(1)}, u32[]{:S(2)}, u32[]{:S(2)}) %collective-permute-start.12) | collective-permute-done | bytes 118816 | tf_op jit(solution)/shard_map/ppermute | solution.py:658
  86.7 4.8 %collective-permute-done.13 = f32[232,128]{1,0:T(8,128)S(1)} collective-permute-done((f32[232,128]{1,0:T(8,128)S(1)}, f32[232,128]{1,0:T(8,128)S(1)}, u32[]{:S(2)}, u32[]{:S(2)}) %collective-permute-start.13) | collective-permute-done | bytes 118816 | tf_op jit(solution)/shard_map/ppermute | solution.py:658
  91.5 0.1 collective-permute-start.14
  91.6 7.0 %collective-permute-done.14 = f32[232,128]{1,0:T(8,128)S(1)} collective-permute-done((f32[232,128]{1,0:T(8,128)S(1)}, f32[232,128]{1,0:T(8,128)S(1)}, u32[]{:S(2)}, u32[]{:S(2)}) %collective-permute-start.14) | collective-permute-done | bytes 118816 | tf_op jit(solution)/shard_map/ppermute | solution.py:658
  98.6 0.3 collective-permute-start.15
  99.0 4.6 %collective-permute-done.15 = f32[232,128]{1,0:T(8,128)S(1)} collective-permute-done((f32[232,128]{1,0:T(8,128)S(1)}, f32[232,128]{1,0:T(8,128)S(1)}, u32[]{:S(2)}, u32[]{:S(2)}) %collective-permute-start.15) | collective-permute-done | bytes 118816 | tf_op jit(solution)/shard_map/ppermute | solution.py:658
  103.5 1.6 %collective-permute-start.16 = (f32[464,128]{1,0:T(8,128)S(1)}, f32[464,128]{1,0:T(8,128)S(1)}, u32[]{:S(2)}, u32[]{:S(2)}) collective-permute-start(f32[464,128]{1,0:T(8,128)S(1)} %maximum_select_fusion.1), channel_id=1, source_target_pairs={{0,16},{1,17},{2,18},{3,19},{4,20},{5,21},{6,22},{7,23},{8,10},{9,... | collective-permute-start | bytes 712712 | tf_op jit(solution)/shard_map/ppermute | solution.py:658
  105.1 4.6 %collective-permute-done.16 = f32[464,128]{1,0:T(8,128)S(1)} collective-permute-done((f32[464,128]{1,0:T(8,128)S(1)}, f32[464,128]{1,0:T(8,128)S(1)}, u32[]{:S(2)}, u32[]{:S(2)}) %collective-permute-start.16) | collective-permute-done | bytes 237600 | tf_op jit(solution)/shard_map/ppermute | solution.py:658
  109.8 1.8 %collective-permute-done.17.other = f32[928,128]{1,0:T(8,128)S(1)} collective-permute-done((f32[928,128]{1,0:T(8,128)S(1)}, f32[928,128]{1,0:T(8,128)S(1)}, u32[]{:S(2)}, u32[]{:S(2)}) %collective-permute-start.17) | collective-permute-done | bytes 475168 | tf_op jit(solution)/shard_map/ppermute | solution.py:613
  111.7 1.7 %final.1 = (f32[1,1]{1,0:T(1,128)}, f32[3,128]{1,0:T(4,128)}, f32[1,3,3]{2,1,0:T(4,128)S(1)}, f32[96,128]{1,0:T(8,128)}, f32[2,64,128]{2,1,0:T(8,128)}, /*index=...) custom-call(s32[2]{0:T(128)S(1)} %pad_add_fusion.par_ref, ...), custom_call_target="tpu_custom_call" | custom-call | flops 100000000 | bytes 200000 | tf_op jit(solution)/shard_map/final/pallas_call | solution.py:638
  113.3 0.6 copy.29
  (49 shorter events, 0.5 us)
Async XLA Ops:
  0.6 0.7 copy-start
  1.3 0.7 copy-start.1
  1.3 10.6 %copy-start.13 = (s32[3,32,128]{2,1,0:T(8,128)S(1)}, s32[3,32,128]{2,1,0:T(8,128)}, u32[]{:S(2)}) copy-start(s32[3,32,128]{2,1,0:T(8,128)} %shift_ref.1) | copy-start | bytes 147460
  2.6 6.7 %collective-permute-start = (f32[8,128]{1,0:T(8,128)S(1)}, f32[8,128]{1,0:T(8,128)S(1)}, u32[]{:S(2)}, u32[]{:S(2)}) collective-permute-start(f32[8,128]{1,0:T(8,128)S(1)} %place.1.own_ref), channel_id=1, source_target_pairs={{0,1},{1,0},{2,3},{3,2},{4,5},{5,4},{6,7},{7,6},{8,9},{9,8},{10,11... | collective-permute-start | bytes 12296 | tf_op jit(solution)/shard_map/ppermute | solution.py:609
  5.6 6.3 %collective-permute-start.1 = (f32[8,128]{1,0:T(8,128)S(1)}, f32[8,128]{1,0:T(8,128)S(1)}, u32[]{:S(2)}, u32[]{:S(2)}) collective-permute-start(f32[8,128]{1,0:T(8,128)S(1)} %place.1.own_ref), channel_id=1, source_target_pairs={{0,7},{1,2},{2,1},{3,4},{4,3},{5,6},{6,5},{7,0},{8,15},{9,10},{10,... | collective-permute-start | bytes 12296 | tf_op jit(solution)/shard_map/ppermute | solution.py:609
  9.2 2.7 %copy-start.17 = (s32[128]{0:T(128)S(1)}, s32[128]{0:T(128)}, u32[]{:S(2)}) copy-start(s32[128]{0:T(128)} %param.18) | copy-start | bytes 1540
  11.9 1.0 copy-start.2
  12.9 0.9 copy-start.4
  13.8 0.9 copy-start.6
  14.7 0.9 copy-start.8
  15.6 0.8 copy-start.11
  16.5 0.8 copy-start.14
  17.3 0.7 copy-start.16
  18.0 11.4 %copy-start.3 = (f32[2,128,384]{2,1,0:T(8,128)S(1)}, f32[2,128,384]{2,1,0:T(8,128)}, u32[]{:S(2)}) copy-start(f32[2,128,384]{2,1,0:T(8,128)} %rout_ref.5) | copy-start | bytes 1179652
  18.0 11.4 %copy-start.5 = (f32[2,128,128]{2,1,0:T(8,128)S(1)}, f32[2,128,128]{2,1,0:T(8,128)}, u32[]{:S(2)}) copy-start(f32[2,128,128]{2,1,0:T(8,128)} %sm_ref.5) | copy-start | bytes 393220
  18.0 11.4 %copy-start.7 = (f32[2,128,128]{2,1,0:T(8,128)S(1)}, f32[2,128,128]{2,1,0:T(8,128)}, u32[]{:S(2)}) copy-start(f32[2,128,128]{2,1,0:T(8,128)} %vm_ref.5) | copy-start | bytes 393220
  18.0 11.4 %copy-start.9 = (f32[2,128,128]{2,1,0:T(8,128)S(1)}, f32[2,128,128]{2,1,0:T(8,128)}, u32[]{:S(2)}) copy-start(f32[2,128,128]{2,1,0:T(8,128)} %vg_ref.5) | copy-start | bytes 393220
  18.0 11.4 %copy-start.10 = (f32[128,128]{1,0:T(8,128)S(1)}, f32[128,128]{1,0:T(8,128)}, u32[]{:S(2)}) copy-start(f32[128,128]{1,0:T(8,128)} %mid_ref.1) | copy-start | bytes 196612
  22.3 5.0 %collective-permute-start.2 = (f32[128,128]{1,0:T(8,128)S(1)}, f32[128,128]{1,0:T(8,128)S(1)}, u32[]{:S(2)}, u32[]{:S(2)}) collective-permute-start(f32[128,128]{1,0:T(8,128)S(1)} %get-tuple-element.42), channel_id=1, source_target_pairs={{0,1},{1,0},{2,3},{3,2},{4,5},{5,4},{6,7},{7,6},{8,9},{9,8},{10,11... | collective-permute-start | bytes 196616 | tf_op jit(solution)/shard_map/ppermute | solution.py:609
  22.4 7.0 %collective-permute-start.3 = (f32[128,128]{1,0:T(8,128)S(1)}, f32[128,128]{1,0:T(8,128)S(1)}, u32[]{:S(2)}, u32[]{:S(2)}) collective-permute-start(f32[128,128]{1,0:T(8,128)S(1)} %get-tuple-element.43), channel_id=1, source_target_pairs={{0,7},{1,2},{2,1},{3,4},{4,3},{5,6},{6,5},{7,0},{8,15},{9,10},{10,... | collective-permute-start | bytes 196616 | tf_op jit(solution)/shard_map/ppermute | solution.py:609
  29.4 0.7 copy-start.18
  30.1 26.4 %copy-start.12 = (f32[2,64,128]{2,1,0:T(8,128)S(1)}, f32[2,64,128]{2,1,0:T(8,128)}, u32[]{:S(2)}) copy-start(f32[2,64,128]{2,1,0:T(8,128)} %rin_ref.5) | copy-start | bytes 196612
  47.7 8.8 %copy-start.15 = (f32[96,128]{1,0:T(8,128)S(1)}, f32[96,128]{1,0:T(8,128)}, u32[]{:S(2)}) copy-start(f32[96,128]{1,0:T(8,128)} %emb_ref.3) | copy-start | bytes 147460
  47.7 4.4 %collective-permute-start.4 = (f32[136,128]{1,0:T(8,128)S(1)}, f32[136,128]{1,0:T(8,128)S(1)}, u32[]{:S(2)}, u32[]{:S(2)}) collective-permute-start(f32[136,128]{1,0:T(8,128)S(1)} %get-tuple-element.44), channel_id=1, source_target_pairs={{0,1},{1,0},{2,3},{3,2},{4,5},{5,4},{6,7},{7,6},{8,9},{9,8},{10,11... | collective-permute-start | bytes 208904 | tf_op jit(solution)/shard_map/ppermute | solution.py:609
  48.0 8.6 %collective-permute-start.7 = (f32[128,128]{1,0:T(8,128)S(1)}, f32[128,128]{1,0:T(8,128)S(1)}, u32[]{:S(2)}, u32[]{:S(2)}) collective-permute-start(f32[128,128]{1,0:T(8,128)S(1)} %get-tuple-element.48), channel_id=1, source_target_pairs={{0,7},{1,2},{2,1},{3,4},{4,3},{5,6},{6,5},{7,0},{8,15},{9,10},{10,... | collective-permute-start | bytes 196616 | tf_op jit(solution)/shard_map/ppermute | solution.py:609
  52.1 3.6 %collective-permute-start.5 = (f32[8,128]{1,0:T(8,128)S(1)}, f32[8,128]{1,0:T(8,128)S(1)}, u32[]{:S(2)}, u32[]{:S(2)}) collective-permute-start(f32[8,128]{1,0:T(8,128)S(1)} %slice_add_fusion), channel_id=1, source_target_pairs={{0,2},{1,3},{2,0},{3,1},{4,6},{5,7},{6,4},{7,5},{8,10},{9,11},{10,... | collective-permute-start | bytes 12296 | tf_op jit(solution)/shard_map/ppermute | solution.py:613
  55.7 9.8 %collective-permute-start.6 = (f32[8,128]{1,0:T(8,128)S(1)}, f32[8,128]{1,0:T(8,128)S(1)}, u32[]{:S(2)}, u32[]{:S(2)}) collective-permute-start(f32[8,128]{1,0:T(8,128)S(1)} %add.38), channel_id=1, source_target_pairs={{0,4},{1,5},{2,6},{3,7},{4,0},{5,1},{6,2},{7,3},{8,12},{9,13},{10,... | collective-permute-start | bytes 12296 | tf_op jit(solution)/shard_map/ppermute | solution.py:613
  67.0 3.3 %collective-permute-start.8 = (f32[928,128]{1,0:T(8,128)S(1)}, f32[928,128]{1,0:T(8,128)S(1)}, u32[]{:S(2)}, u32[]{:S(2)}) collective-permute-start(f32[928,128]{1,0:T(8,128)S(1)} %multiply_select_fusion), channel_id=1, source_target_pairs={{0,8},{8,0},{16,24},{24,16},{1,9},{9,1},{17,25},{25,17},{2,10},{10... | collective-permute-start | bytes 1425416 | tf_op jit(solution)/shard_map/ppermute | solution.py:613
  67.1 3.7 %collective-permute-start.9 = (f32[16,128]{1,0:T(8,128)S(1)}, f32[16,128]{1,0:T(8,128)S(1)}, u32[]{:S(2)}, u32[]{:S(2)}) collective-permute-start(f32[16,128]{1,0:T(8,128)S(1)} %get-tuple-element.53), channel_id=1, source_target_pairs={{0,1},{1,0},{2,3},{3,2},{4,5},{5,4},{6,7},{7,6},{8,9},{9,8},{10,11... | collective-permute-start | bytes 24584 | tf_op jit(solution)/shard_map/ppermute | solution.py:609
  69.0 6.3 %collective-permute-start.10 = (f32[16,128]{1,0:T(8,128)S(1)}, f32[16,128]{1,0:T(8,128)S(1)}, u32[]{:S(2)}, u32[]{:S(2)}) collective-permute-start(f32[16,128]{1,0:T(8,128)S(1)} %get-tuple-element.54), channel_id=1, source_target_pairs={{0,7},{1,2},{2,1},{3,4},{4,3},{5,6},{6,5},{7,0},{8,15},{9,10},{10,... | collective-permute-start | bytes 24584 | tf_op jit(solution)/shard_map/ppermute | solution.py:609
  75.4 6.2 %collective-permute-start.11 = (f32[464,128]{1,0:T(8,128)S(1)}, f32[464,128]{1,0:T(8,128)S(1)}, u32[]{:S(2)}, u32[]{:S(2)}) collective-permute-start(f32[464,128]{1,0:T(8,128)S(1)} %slice_select_fusion), channel_id=1, source_target_pairs={{0,16},{1,17},{2,18},{3,19},{4,20},{5,21},{6,22},{7,23},{8,10},{9,... | collective-permute-start | bytes 712712 | tf_op jit(solution)/shard_map/ppermute | solution.py:658
  81.7 4.9 %collective-permute-start.12 = (f32[232,128]{1,0:T(8,128)S(1)}, f32[232,128]{1,0:T(8,128)S(1)}, u32[]{:S(2)}, u32[]{:S(2)}) collective-permute-start(f32[232,128]{1,0:T(8,128)S(1)} %slice_select_fusion.1), channel_id=1, source_target_pairs={{0,2},{1,3},{2,0},{3,1},{4,6},{5,7},{6,4},{7,5},{8,24},{9,25},{10,... | collective-permute-start | bytes 356360 | tf_op jit(solution)/shard_map/ppermute | solution.py:658
  86.6 4.9 %collective-permute-start.13 = (f32[232,128]{1,0:T(8,128)S(1)}, f32[232,128]{1,0:T(8,128)S(1)}, u32[]{:S(2)}, u32[]{:S(2)}) collective-permute-start(f32[232,128]{1,0:T(8,128)S(1)} %select_add_fusion.2), channel_id=1, source_target_pairs={{0,1},{1,0},{2,3},{3,2},{4,5},{5,4},{6,7},{7,6},{8,12},{9,13},{10,... | collective-permute-start | bytes 356360 | tf_op jit(solution)/shard_map/ppermute | solution.py:658
  91.5 7.1 %collective-permute-start.14 = (f32[232,128]{1,0:T(8,128)S(1)}, f32[232,128]{1,0:T(8,128)S(1)}, u32[]{:S(2)}, u32[]{:S(2)}) collective-permute-start(f32[232,128]{1,0:T(8,128)S(1)} %add.45), channel_id=1, source_target_pairs={{0,4},{1,5},{2,6},{3,7},{4,0},{5,1},{6,2},{7,3},{8,9},{9,8},{10,11... | collective-permute-start | bytes 356360 | tf_op jit(solution)/shard_map/ppermute | solution.py:658
  98.6 4.9 %collective-permute-start.15 = (f32[232,128]{1,0:T(8,128)S(1)}, f32[232,128]{1,0:T(8,128)S(1)}, u32[]{:S(2)}, u32[]{:S(2)}) collective-permute-start(f32[232,128]{1,0:T(8,128)S(1)} %add.46), channel_id=1, source_target_pairs={{0,2},{1,3},{2,0},{3,1},{4,6},{5,7},{6,4},{7,5},{8,24},{9,25},{10,... | collective-permute-start | bytes 356360 | tf_op jit(solution)/shard_map/ppermute | solution.py:658
  103.5 6.2 %collective-permute-start.16 = (f32[464,128]{1,0:T(8,128)S(1)}, f32[464,128]{1,0:T(8,128)S(1)}, u32[]{:S(2)}, u32[]{:S(2)}) collective-permute-start(f32[464,128]{1,0:T(8,128)S(1)} %maximum_select_fusion.1), channel_id=1, source_target_pairs={{0,16},{1,17},{2,18},{3,19},{4,20},{5,21},{6,22},{7,23},{8,10},{9,... | collective-permute-start | bytes 712712 | tf_op jit(solution)/shard_map/ppermute | solution.py:658
  109.7 1.9 %collective-permute-start.17 = (f32[928,128]{1,0:T(8,128)S(1)}, f32[928,128]{1,0:T(8,128)S(1)}, u32[]{:S(2)}, u32[]{:S(2)}) collective-permute-start(f32[928,128]{1,0:T(8,128)S(1)} %maximum_select_fusion.mine), channel_id=1, source_target_pairs={{0,8},{8,0},{16,24},{24,16},{1,9},{9,1},{17,25},{25,17},{2,10},{10... | collective-permute-start | bytes 1425416 | tf_op jit(solution)/shard_map/ppermute | solution.py:613

commit v3 on v2

--- a/solution.py
+++ b/solution.py
@@ -11,9 +11,8 @@
 BF16 = jnp.bfloat16
 LANES = 128
 HALF = 64
-FWD_ROWS = 16
-BWD_ROWS = 16
-VMEM_LIMIT = 50 * 1024 * 1024
+ROWS = 16
+VMEM_LIMIT = 20 * 1024 * 1024
 G_ROWS = 928
 MID_ROWS = 88
 
@@ -126,21 +125,34 @@
             tab[h, q * LANES : (q + 1) * LANES, LANES:] = lo
 
 
-def radial(rows, ri4, ro3, basis_count):
-    sharpness = 0.5 * ((basis_count - 1) / 8.0) ** 2
+def centre_offsets(rows, basis_count):
     place = lax.broadcasted_iota(jnp.int32, (basis_count, LANES), 0).astype(F32)
     centres = 8.0 * place / (basis_count - 1)
-    offsets = [g[3:4] - centres for g in rows]
-    offset = jnp.concatenate(offsets, axis=1)
-    basis = jnp.exp(-sharpness * offset * offset)
-    bh, bl = split(basis)
+    return jnp.concatenate([g[3:4] - centres for g in rows], axis=1)
+
+
+def sharpness(basis_count):
+    return 0.5 * ((basis_count - 1) / 8.0) ** 2
+
+
+def edge_rows(geom, t):
+    return [geom[t * ROWS + q] for q in range(ROWS)]
+
+
+def radial(rows, t, ri4, ro3, kept, basis_count):
+    filters_ref, hidden_ref, basis_ref, slope_ref = kept
+    offset = centre_offsets(rows, basis_count)
+    bh, bl = split(jnp.exp(-sharpness(basis_count) * offset * offset))
+    basis_ref[t] = jnp.concatenate([bh, bl], axis=0)
     pre = mm(ri4[...], jnp.concatenate([bh, bl, bh, bl], axis=0))
     gate = sigmoid(pre)
     mask = jnp.concatenate([g[4:5] for g in rows], axis=1)
-    hidden = pre * gate * mask
-    hh, hl = split(hidden)
+    slope_ref[t] = mask * (gate * (1.0 + pre * (1.0 - gate)))
+    hh, hl = split(pre * gate * mask)
+    hidden_ref[t] = jnp.concatenate([hh, hl], axis=0)
     filters = mm(ro3[...], jnp.concatenate([hh, hl, hh], axis=0))
-    return offset, basis, bh, bl, pre, gate, mask, hidden, hh, hl, filters, sharpness
+    filters_ref[t] = filters
+    return filters
 
 
 def one_hot_of(rows):
@@ -154,18 +166,26 @@
     return x[group * LANES : (group + 1) * LANES, q * LANES : (q + 1) * LANES]
 
 
-def forward_edges(geom, tab, ri4, ro3, acc, basis_count, vectors):
-    total = geom.shape[0]
-    per_half = total // 2 // FWD_ROWS
+def radial_edges(geom, ri4, ro3, kept, basis_count):
+    def step(t, carry):
+        radial(edge_rows(geom, t), t, ri4, ro3, kept, basis_count)
+        return carry
+
+    lax.fori_loop(0, geom.shape[0] // ROWS, step, 0)
+
+
+def forward_edges(geom, tab, acc, found_ref, filters_of, vectors):
+    per_half = geom.shape[0] // 2 // ROWS
     acc[...] = jnp.zeros(acc.shape, F32)
     wide = 2 if vectors else 1
 
     def step(t, carry):
         h = t // per_half
-        rows = [geom[t * FWD_ROWS + q] for q in range(FWD_ROWS)]
-        filters = radial(rows, ri4, ro3, basis_count)[10]
+        rows = edge_rows(geom, t)
+        filters = filters_of(rows, t)
         hot = one_hot_of(rows)
         found = mm(tab[h], jnp.concatenate([hot, hot], axis=0))
+        found_ref[t] = found
         sums = [None] * 4
         for q, g in enumerate(rows):
             s = part(found, 0, q)
@@ -213,64 +233,57 @@
     return da, g_sm, g_vm, g_vg
 
 
-def backward_edges(geom, dgeom, tab, ri4, ro3, rib, rob, gacc, dro, dri, dtab, basis_count, vectors, finish):
-    total = geom.shape[0]
-    per_half = total // 2 // BWD_ROWS
-    dro[...] = jnp.zeros(dro.shape, F32)
-    dri[...] = jnp.zeros(dri.shape, F32)
-    dtab[...] = jnp.zeros(dtab.shape, F32)
+def source_terms(rows, filters, found, gs, gv, vectors):
     wide = 2 if vectors else 1
-
-    def step(t, carry):
-        h = t // per_half
-        rows = [geom[t * BWD_ROWS + q] for q in range(BWD_ROWS)]
-        offset, basis, bh, bl, pre, gate, mask, hidden, hh, hl, filters, sharpness = radial(
-            rows, ri4, ro3, basis_count
-        )
-        hot = one_hot_of(rows)
-        found = mm(tab[h], jnp.concatenate([hot, hot], axis=0))
-        d_filters, d_found, d_dirs = [], [], []
-        gs = gacc[h, 0]
-        gv = [gacc[h, 1 + c] for c in range(3)]
-        for q, g in enumerate(rows):
-            s = part(found, 0, q)
-            along = gv[0] * g[0:1] + gv[1] * g[1:2] + gv[2] * g[2:3]
-            f_s, f_d = part(filters, 0, q), part(filters, wide, q)
-            groups = [gs * s]
-            sources = [f_s * gs + f_d * along]
-            if vectors:
-                f_v = part(filters, 1, q)
-                v = [part(found, 1 + c, q) for c in range(3)]
-                groups.append(gv[0] * v[0] + gv[1] * v[1] + gv[2] * v[2])
-                sources += [f_v * gv[c] for c in range(3)]
-            groups.append(s * along)
-            d_filters.append(jnp.concatenate(groups, axis=0))
-            push = f_d * s
-            d_dirs.append([jnp.sum(push * gv[c], axis=0, keepdims=True) for c in range(3)])
-            d_found.append(jnp.concatenate(sources, axis=0))
-        d_filter = jnp.concatenate(d_filters, axis=1)
-        fh, fl = split(d_filter)
-        both = jnp.concatenate([hh, hl], axis=0)
-        dro[...] += mm_nt(jnp.concatenate([fh, fl], axis=1), jnp.concatenate([both, both], axis=1))
-        spread = mm(rob[...], jnp.concatenate([fh, fl], axis=0))
-        d_hidden = (spread[:LANES] + spread[LANES:]) * mask
-        d_pre = d_hidden * (gate * (1.0 + pre * (1.0 - gate)))
-        ph, plo = split(d_pre)
-        bb = jnp.concatenate([bh, bl], axis=0)
-        dri[...] += mm_nt(jnp.concatenate([ph, plo], axis=1), jnp.concatenate([bb, bb], axis=1))
-        back = mm(rib[...], jnp.concatenate([ph, plo], axis=0))
-        d_basis = back[:basis_count] + back[basis_count:]
-        d_dist = jnp.sum(d_basis * basis * offset, axis=0, keepdims=True) * (-2.0 * sharpness)
-        extra = []
-        for q, g in enumerate(rows):
-            extra.append(finish(t * BWD_ROWS + q, h, g, d_dirs[q], d_dist[:, q * LANES : (q + 1) * LANES]))
-        if extra[0] is not None:
-            d_found = [jnp.concatenate([a, b], axis=0) for a, b in zip(d_found, extra)]
-        sh, sl = split(jnp.concatenate(d_found, axis=1))
-        dtab[h] += mm_nt(jnp.concatenate([sh, sl], axis=1), jnp.concatenate([hot, hot], axis=1))
-        return carry
-
-    lax.fori_loop(0, 2 * per_half, step, 0)
+    columns = []
+    for q, g in enumerate(rows):
+        along = gv[0] * g[0:1] + gv[1] * g[1:2] + gv[2] * g[2:3]
+        sources = [part(filters, 0, q) * gs + part(filters, wide, q) * along]
+        if vectors:
+            f_v = part(filters, 1, q)
+            sources += [f_v * gv[c] for c in range(3)]
+        columns.append(jnp.concatenate(sources, axis=0))
+    return columns
+
+
+def scatter(columns, hot):
+    sh, sl = split(jnp.concatenate(columns, axis=1))
+    return mm_nt(jnp.concatenate([sh, sl], axis=1), jnp.concatenate([hot, hot], axis=1))
+
+
+def step_derivatives(gacc, h):
+    return gacc[h, 0], [gacc[h, 1 + c] for c in range(3)]
+
+
+def filter_terms(rows, t, kept, found, gs, gv, rib, rob, dro, dri, basis_count, vectors):
+    filters_ref, hidden_ref, basis_ref, slope_ref = kept
+    wide = 2 if vectors else 1
+    d_filters, d_dirs = [], []
+    for q, g in enumerate(rows):
+        s = part(found, 0, q)
+        along = gv[0] * g[0:1] + gv[1] * g[1:2] + gv[2] * g[2:3]
+        groups = [gs * s]
+        if vectors:
+            v = [part(found, 1 + c, q) for c in range(3)]
+            groups.append(gv[0] * v[0] + gv[1] * v[1] + gv[2] * v[2])
+        groups.append(s * along)
+        d_filters.append(jnp.concatenate(groups, axis=0))
+        push = part(filters_ref.at[t], wide, q) * s
+        d_dirs.append([jnp.sum(push * gv[c], axis=0, keepdims=True) for c in range(3)])
+    fh, fl = split(jnp.concatenate(d_filters, axis=1))
+    both = hidden_ref[t]
+    dro[...] += mm_nt(jnp.concatenate([fh, fl], axis=1), jnp.concatenate([both, both], axis=1))
+    spread = mm(rob[...], jnp.concatenate([fh, fl], axis=0))
+    d_pre = (spread[:LANES] + spread[LANES:]) * slope_ref[t]
+    ph, plo = split(d_pre)
+    bb = basis_ref[t]
+    dri[...] += mm_nt(jnp.concatenate([ph, plo], axis=1), jnp.concatenate([bb, bb], axis=1))
+    back = mm(rib[...], jnp.concatenate([ph, plo], axis=0))
+    d_basis = back[:basis_count] + back[basis_count:]
+    basis = bb[:basis_count].astype(F32) + bb[basis_count:].astype(F32)
+    offset = centre_offsets(rows, basis_count)
+    d_dist = jnp.sum(d_basis * basis * offset, axis=0, keepdims=True) * (-2.0 * sharpness(basis_count))
+    return d_dirs, [d_dist[:, q * LANES : (q + 1) * LANES] for q in range(len(rows))]
 
 
 def radial_grads(dro, dri, out, row_in, row_out, basis_count, groups):
@@ -325,7 +338,7 @@
 def first_kernel(
     halo, par_ref, cell_ref, own_ref, a_ref, b_ref, nb_ref, count_ref, shift_ref, emb_ref, rin_ref, rout_ref,
     sm_ref, vm_ref, vg_ref,
-    geom_ref, feat_ref, agg_ref, send_a, send_b,
+    geom_ref, feat_ref, agg_ref, send_a, send_b, filters_ref, hidden_ref, basis_ref, slope_ref, found_ref,
     tab, ri4, ro3, acc,
 ):
     slots = nb_ref.shape[0]
@@ -367,7 +380,10 @@
     s, beside = first_features(emb_ref, hot_own), first_features(emb_ref, hot_beside)
     store_tables(tab, [s], [beside], halo)
     prepare_weights(rin_ref, rout_ref, ri4, ro3, (0, 2))
-    forward_edges(geom_ref, tab, ri4, ro3, acc, basis_count, False)
+    kept = (filters_ref, hidden_ref, basis_ref, slope_ref)
+    forward_edges(
+        geom_ref, tab, acc, found_ref, lambda rows, t: radial(rows, t, ri4, ro3, kept, basis_count), False
+    )
     agg = aggregates(acc, slots**-0.5)
     w, size, u, gate = node_forward(agg, sm_ref[0], vm_ref[0], vg_ref[0])
     features = [s + u * sigmoid(u)] + [w[c] * gate for c in range(3)]
@@ -380,12 +396,16 @@
     send_b[...] = jnp.where(even, head, tail)
 
 
+def radial_kernel(geom_ref, rin_ref, rout_ref, filters_ref, hidden_ref, basis_ref, slope_ref, ri4, ro3):
+    prepare_weights(rin_ref, rout_ref, ri4, ro3, (0, 1, 2))
+    radial_edges(geom_ref, ri4, ro3, (filters_ref, hidden_ref, basis_ref, slope_ref), rin_ref.shape[1])
+
+
 def second_kernel(
-    halo, par_ref, geom_ref, feat_ref, a_ref, b_ref, rin_ref, rout_ref, sm_ref, vm_ref, vg_ref, mid_ref, out_ref,
-    cot_ref, send_a, send_b, dgeom_ref, grad_ref, mid_tail,
-    tab, ri4, ro3, rib, rob, acc, gacc, dro, dri, dtab,
+    halo, par_ref, geom_ref, feat_ref, a_ref, b_ref, filters_ref, sm_ref, vm_ref, vg_ref, mid_ref, out_ref,
+    cot_ref, send_a, send_b, grad_ref, mid_tail, gacc, found_ref,
+    tab, acc, dtab,
 ):
-    basis_count = rin_ref.shape[1]
     slots = geom_ref.shape[0]
     scale = slots**-0.5
     up, down = from_sides(par_ref, a_ref, b_ref)
@@ -395,10 +415,7 @@
         jnp.where(lane >= LANES - halo, unpacked(down, q, halo, True), unpacked(up, q, halo, False)) for q in range(4)
     ]
     store_tables(tab, features, besides, halo)
-    groups = (0, 1, 2)
-    prepare_weights(rin_ref, rout_ref, ri4, ro3, groups)
-    prepare_back(rin_ref, rout_ref, rib, rob, groups)
-    forward_edges(geom_ref, tab, ri4, ro3, acc, basis_count, True)
+    forward_edges(geom_ref, tab, acc, found_ref, lambda rows, t: filters_ref.at[t], True)
 
     @pl.when(par_ref[0] >= 0)
     def _():
@@ -424,7 +441,7 @@
                 gacc[h, n] = twice(da[n], h)
         for n, x in enumerate([ds] + dv):
             cot_ref[n] = x
-        row = basis_count + 3 * LANES
+        row = 0
         for grad in (g_sm, g_vm, g_vg):
             grad_ref[row : row + LANES] = grad
             row += LANES
@@ -433,16 +450,18 @@
         grad_ref[row + 8 :] = g_mid[:MID_ROWS]
         mid_tail[...] = g_mid[MID_ROWS:]
 
-    def finish(row, h, g, d_dir, d_dist):
-        for c in range(3):
-            dgeom_ref[row, c : c + 1, :] = d_dir[c]
-        dgeom_ref[row, 3:4, :] = d_dist
-        return None
-
-    backward_edges(
-        geom_ref, dgeom_ref, tab, ri4, ro3, rib, rob, gacc, dro, dri, dtab, basis_count, True, finish
-    )
-    radial_grads(dro, dri, grad_ref, 0, basis_count, basis_count, len(groups))
+    per_half = slots // 2 // ROWS
+    dtab[...] = jnp.zeros(dtab.shape, F32)
+
+    def step(t, carry):
+        h = t // per_half
+        rows = edge_rows(geom_ref, t)
+        gs, gv = step_derivatives(gacc, h)
+        columns = source_terms(rows, filters_ref.at[t], found_ref.at[t], gs, gv, True)
+        dtab[h] += scatter(columns, one_hot_of(rows))
+        return carry
+
+    lax.fori_loop(0, 2 * per_half, step, 0)
     firsts = [dtab[0, q * LANES : (q + 1) * LANES] for q in range(4)]
     seconds = [dtab[1, q * LANES : (q + 1) * LANES] for q in range(4)]
     for q in range(4):
@@ -455,11 +474,41 @@
     send_b[...] = jnp.where(even, to_prev, to_next)
 
 
+def radial_back_kernel(
+    geom_ref, filters_ref, hidden_ref, basis_ref, slope_ref, found_ref, gacc, mixed_ref, rin_ref, rout_ref,
+    dgeom_ref, grad_ref,
+    rib, rob, dro, dri,
+):
+    basis_count = rin_ref.shape[1]
+    groups = (0, 1, 2)
+    prepare_back(rin_ref, rout_ref, rib, rob, groups)
+    kept = (filters_ref, hidden_ref, basis_ref, slope_ref)
+    per_half = geom_ref.shape[0] // 2 // ROWS
+    dro[...] = jnp.zeros(dro.shape, F32)
+    dri[...] = jnp.zeros(dri.shape, F32)
+
+    def step(t, carry):
+        rows = edge_rows(geom_ref, t)
+        gs, gv = step_derivatives(gacc, t // per_half)
+        d_dirs, d_dists = filter_terms(
+            rows, t, kept, found_ref.at[t], gs, gv, rib, rob, dro, dri, basis_count, True
+        )
+        for q in range(ROWS):
+            for c in range(3):
+                dgeom_ref[t * ROWS + q, c : c + 1, :] = d_dirs[q][c]
+            dgeom_ref[t * ROWS + q, 3:4, :] = d_dists[q]
+        return carry
+
+    lax.fori_loop(0, 2 * per_half, step, 0)
+    radial_grads(dro, dri, grad_ref, 0, basis_count, basis_count, len(groups))
+    grad_ref[basis_count + 3 * LANES :] = mixed_ref[...]
+
+
 def third_kernel(
-    halo, par_ref, geom_ref, dgeom_ref, agg_ref, cot_ref, a_ref, b_ref, own_ref, pa_ref, pb_ref, mid_tail, emb_ref,
-    rin_ref, rout_ref, sm_ref, vm_ref, vg_ref,
-    force_ref, send_a, send_b, grad_ref,
-    tab, ri4, ro3, rib, rob, gacc, dro, dri, dtab, pull, virial,
+    halo, par_ref, geom_ref, dgeom_ref, agg_ref, cot_ref, a_ref, b_ref, own_ref, pa_ref, pb_ref, mid_tail,
+    filters_ref, hidden_ref, basis_ref, slope_ref, found_ref, emb_ref, rin_ref, rout_ref, sm_ref, vm_ref, vg_ref,
+    force_ref, send_ref, grad_ref,
+    rib, rob, gacc, dro, dri, dtab, pull, virial,
 ):
     basis_count = rin_ref.shape[1]
     slots = geom_ref.shape[0]
@@ -475,10 +524,7 @@
         )
     place_up, place_down = from_sides(par_ref, pa_ref, pb_ref)
     hot_own, hot_beside = species_tables(own_ref, place_up, place_down, emb_ref, halo)
-    s, beside = first_features(emb_ref, hot_own), first_features(emb_ref, hot_beside)
-    store_tables(tab, [s], [beside], halo)
     groups = (0, 2)
-    prepare_weights(rin_ref, rout_ref, ri4, ro3, groups)
     prepare_back(rin_ref, rout_ref, rib, rob, groups)
     count = emb_ref.shape[0]
 
@@ -499,7 +545,7 @@
     pull[...] = jnp.zeros(pull.shape, F32)
     virial[...] = jnp.zeros(virial.shape, F32)
 
-    def finish(row, h, g, d_dir, d_dist):
+    def finish(row, g, d_dir, d_dist):
         more = dgeom_ref[row]
         dist = g[3:4]
         toward = [g[c : c + 1] for c in range(3)]
@@ -510,14 +556,30 @@
         dr = [(turn[c] - toward[c] * inner) * inverse + stretch * toward[c] for c in range(3)]
         r = [toward[c] * dist for c in range(3)]
         lines = jnp.concatenate(dr + [jnp.zeros((13, LANES), F32)], axis=0)
-        pull[h] += lines
         products = [r[a] * dr[c] for a in range(3) for c in range(3)]
-        virial[...] += jnp.concatenate(products + [jnp.zeros((7, LANES), F32)], axis=0)
-        return lines
-
-    backward_edges(
-        geom_ref, None, tab, ri4, ro3, rib, rob, gacc, dro, dri, dtab, basis_count, False, finish
-    )
+        return lines, jnp.concatenate(products + [jnp.zeros((7, LANES), F32)], axis=0)
+
+    kept = (filters_ref, hidden_ref, basis_ref, slope_ref)
+    per_half = slots // 2 // ROWS
+    dro[...] = jnp.zeros(dro.shape, F32)
+    dri[...] = jnp.zeros(dri.shape, F32)
+    dtab[...] = jnp.zeros(dtab.shape, F32)
+
+    def step(t, carry):
+        h = t // per_half
+        rows = edge_rows(geom_ref, t)
+        gs, gv = step_derivatives(gacc, h)
+        found = found_ref.at[t]
+        d_dirs, d_dists = filter_terms(rows, t, kept, found, gs, gv, rib, rob, dro, dri, basis_count, False)
+        columns = source_terms(rows, filters_ref.at[t], found, gs, gv, False)
+        pairs = [finish(t * ROWS + q, g, d_dirs[q], d_dists[q]) for q, g in enumerate(rows)]
+        pull[h] += sum(x for x, _ in pairs[1:]) + pairs[0][0]
+        virial[...] += sum(x for _, x in pairs[1:]) + pairs[0][1]
+        columns = [jnp.concatenate([x, y], axis=0) for x, (y, _) in zip(columns, pairs)]
+        dtab[h] += scatter(columns, one_hot_of(rows))
+        return carry
+
+    lax.fori_loop(0, 2 * per_half, step, 0)
     first, second = dtab[0, 0:LANES], dtab[1, 0:LANES]
     own_cot = cot[0] + jnp.where(lane < LANES - halo, first, 0.0) + jnp.where(lane >= halo, second, 0.0)
     side_cot = jnp.where(lane >= LANES - halo, first, 0.0) + jnp.where(lane < halo, second, 0.0)
@@ -541,18 +603,24 @@
         - folded(pull[0], pull[1])
     )
     even = is_even(par_ref, first.shape)
-    send_a[...] = jnp.where(even, second, first)
-    send_b[...] = jnp.where(even, first, second)
+    send_ref[0:8] = jnp.where(even, second, first)[0:8]
+    send_ref[8:16] = jnp.where(even, first, second)[0:8]
 
 
 def final_kernel(
-    halo, par_ref, cell_ref, sum_energy, force_ref, a_ref, b_ref, mine, other,
+    halo, par_ref, cell_ref, sum_energy, force_ref, a_ref, b_ref, mine_turned, other_turned,
     energy_ref, forces_ref, stress_ref, emb_ref, rin_ref, rout_ref, sm_ref, vm_ref, vg_ref, mid_ref, out_ref,
+    mine, other,
 ):
     energy_ref[0, 0] = jnp.max(sum_energy[0:1])
-    lane = lane_ids(16)
-    up, down = from_sides(par_ref, a_ref, b_ref)
-    force = force_ref[...] + jnp.where(lane >= LANES - halo, up, 0.0) + jnp.where(lane < halo, down, 0.0)
+    rows = mine.shape[0] // 4
+    for c in range(4):
+        turned = pl.ds(pl.multiple_of((par_ref[2] ^ c) * rows, 8), rows)
+        mine[c * rows : (c + 1) * rows] = mine_turned[turned]
+        other[c * rows : (c + 1) * rows] = other_turned[turned]
+    lane = lane_ids(8)
+    up, down = from_sides(par_ref, a_ref, b_ref.at[pl.ds(pl.multiple_of(8 * par_ref[3], 8), 8)])
+    force = force_ref[0:8] + jnp.where(lane >= LANES - halo, up, 0.0) + jnp.where(lane < halo, down, 0.0)
     forces_ref[...] = -force[0:3]
     count, basis_count = emb_ref.shape[0], rin_ref.shape[1]
     m = [[cell_ref[0, a, c] for c in range(3)] for a in range(3)]
@@ -670,20 +738,33 @@
     group = lax.axis_index("dp")
     species_row, counts_row, out_row = species[None], counts[None], readout_out[None]
     own = call(
-        place_kernel, "place", f32(8, LANES), [smem(), whole(frac), whole(species_row)], vmem(), [], 10**6,
+        place_kernel, "place", f32(8, LANES), [smem(), whole(frac), whole(species_row)], vmem(), [], 10**10,
         cell, frac, species_row,
     )
     side_a, side_b = sides(own, own, "atom")
-    par = jnp.stack([me % 2, group]).astype(jnp.int32)
+    plane = group // 2 * 2 + me % 2
+    slabs = lax.axis_size("atom")
+    levels = (slabs - 1).bit_length() - 1
+    bits = [2 << n for n in range(levels)]
+    opposite = jnp.where(me % 2 == 1, (me + 1) % slabs, (me + slabs - 1) % slabs)
+    turned = (me ^ opposite ^ 1) >> 1
+    turned = jnp.where(group % 2 == 1, (turned >> 1) | ((turned & 1) << (levels - 1)), turned)
+    par = jnp.stack([me % 2, group, plane, turned]).astype(jnp.int32)
     layer = (radial_in, radial_out, scalar_mix, vector_mix, vector_gate)
     block = f32(LANES, LANES)
-    geom, feat, agg, feat_a, feat_b = call(
+    edges, steps = ROWS * LANES, slots // ROWS
+
+    def kept(groups):
+        halves = tuple(jax.ShapeDtypeStruct((steps, n, edges), BF16) for n in (2 * LANES, 2 * basis_count))
+        return (f32(steps, groups * LANES, edges),) + halves + (f32(steps, LANES, edges),)
+
+    geom, feat, agg, feat_a, feat_b, *kept_one = call(
         functools.partial(first_kernel, halo),
         "layer_one",
-        (f32(slots, 8, LANES), f32(4, LANES, LANES), f32(4, LANES, LANES), block, block),
-        [smem(), smem()] + [vmem()] * 3 + [whole(x) for x in (neighbours, counts_row, shifts, embedding)]
-        + [layer_spec(x, 0) for x in layer],
-        [vmem()] * 5,
+        (f32(slots, 8, LANES), f32(4, LANES, LANES), f32(4, LANES, LANES), block, block) + kept(2)
+        + (f32(steps, LANES, edges),),
+        [smem(), smem()] + [vmem()] * 7 + [layer_spec(x, 0) for x in layer],
+        [vmem()] * 10,
         [
             pltpu.VMEM((2, LANES, 2 * LANES), BF16),
             pltpu.VMEM((LANES, 4 * basis_count), BF16),
@@ -694,46 +775,63 @@
         par, cell, own, side_a, side_b, neighbours, counts_row, shifts, embedding, *layer,
     )
     feat_a, feat_b = sides(feat_a, feat_b, "atom")
-    cot, cot_a, cot_b, dgeom, grads_two, mid_tail = call(
+    kept_two = call(
+        radial_kernel,
+        "radial_two",
+        kept(3),
+        [vmem(), layer_spec(radial_in, 1), layer_spec(radial_out, 1)],
+        [vmem()] * 4,
+        [pltpu.VMEM((LANES, 4 * basis_count), BF16), pltpu.VMEM((3 * LANES, 3 * LANES), BF16)],
+        3 * 10**9,
+        geom, radial_in, radial_out,
+    )
+    tail_rows = LANES - MID_ROWS
+    mixed_rows = 3 * LANES + 8 + MID_ROWS
+    cot, cot_a, cot_b, mixed, mid_tail, gacc, found_two = call(
         functools.partial(second_kernel, halo),
         "layer_two",
         (
-            f32(4, LANES, LANES), f32(LANES + 8, LANES), block, f32(slots, 8, LANES), f32(G_ROWS, LANES),
-            f32(LANES - MID_ROWS, LANES),
+            f32(4, LANES, LANES), f32(LANES + 8, LANES), block, f32(mixed_rows, LANES), f32(tail_rows, LANES),
+            f32(2, 4, LANES, LANES), f32(steps, 4 * LANES, edges),
         ),
-        [smem()] + [vmem()] * 4 + [layer_spec(x, 1) for x in layer] + [whole(readout_mid), whole(out_row)],
-        [vmem()] * 6,
+        [smem()] + [vmem()] * 5 + [layer_spec(x, 1) for x in layer[2:]] + [whole(readout_mid), whole(out_row)],
+        [vmem()] * 7,
         [
             pltpu.VMEM((2, 4 * LANES, 2 * LANES), BF16),
-            pltpu.VMEM((LANES, 4 * basis_count), BF16),
-            pltpu.VMEM((3 * LANES, 3 * LANES), BF16),
+            pltpu.VMEM((2, 4, LANES, LANES), F32),
+            pltpu.VMEM((2, 4 * LANES, LANES), F32),
+        ],
+        5 * 10**9,
+        par, geom, feat, feat_a, feat_b, kept_two[0], *layer[2:], readout_mid, out_row,
+    )
+    energy = cot_a[LANES:]
+    cot_a, cot_b = sides(cot_a, cot_b, "atom")
+    dgeom, grads_two = call(
+        radial_back_kernel,
+        "radial_two_back",
+        (f32(slots, 8, LANES), f32(G_ROWS, LANES)),
+        [vmem()] * 8 + [layer_spec(radial_in, 1), layer_spec(radial_out, 1)],
+        [vmem()] * 2,
+        [
             pltpu.VMEM((2 * basis_count, 2 * LANES), BF16),
             pltpu.VMEM((2 * LANES, 6 * LANES), BF16),
-            pltpu.VMEM((2, 4, LANES, LANES), F32),
-            pltpu.VMEM((2, 4, LANES, LANES), F32),
             pltpu.VMEM((3 * LANES, 2 * LANES), F32),
             pltpu.VMEM((LANES, 2 * basis_count), F32),
-            pltpu.VMEM((2, 4 * LANES, LANES), F32),
         ],
-        10**10,
-        par, geom, feat, feat_a, feat_b, *layer, readout_mid, out_row,
-    )
-    energy = cot_a[LANES:]
-    cot_a, cot_b = sides(cot_a, cot_b, "atom")
+        5 * 10**9,
+        geom, *kept_two, found_two, gacc, mixed, radial_in, radial_out,
+    )
     energy = energy + cot_a[LANES:]
-    bits = [1 << n for n in range(1, (lax.axis_size("atom") - 1).bit_length())]
-    for bit in bits[:1]:
-        energy = energy + swap(energy, "atom", bit)
-    force, force_a, force_b, grads_one = call(
+    others = [swap(energy, "atom", k) for k in range(2, min(slabs, 8), 2)]
+    for other in others:
+        energy = energy + other
+    force, force_sent, grads_one = call(
         functools.partial(third_kernel, halo),
         "layer_one_back",
-        (f32(16, LANES), f32(16, LANES), f32(16, LANES), f32(G_ROWS, LANES)),
-        [smem()] + [vmem()] * 11 + [layer_spec(x, 0) for x in layer],
-        [vmem()] * 4,
+        (f32(16, LANES), f32(16, LANES), f32(G_ROWS, LANES)),
+        [smem()] + [vmem()] * 16 + [layer_spec(x, 0) for x in layer],
+        [vmem()] * 3,
         [
-            pltpu.VMEM((2, LANES, 2 * LANES), BF16),
-            pltpu.VMEM((LANES, 4 * basis_count), BF16),
-            pltpu.VMEM((2 * LANES, 3 * LANES), BF16),
             pltpu.VMEM((2 * basis_count, 2 * LANES), BF16),
             pltpu.VMEM((2 * LANES, 4 * LANES), BF16),
             pltpu.VMEM((2, 4, LANES, LANES), F32),
@@ -744,39 +842,37 @@
             pltpu.VMEM((16, LANES), F32),
         ],
         6 * 10**9,
-        par, geom, dgeom, agg, cot, cot_a, cot_b, own, side_a, side_b, mid_tail, embedding, *layer,
-    )
-    for bit in bits[1:]:
+        par, geom, dgeom, agg, cot, cot_a, cot_b, own, side_a, side_b, mid_tail, *kept_one, embedding,
+        *layer,
+    )
+    for bit in bits[2:]:
         energy = energy + swap(energy, "atom", bit)
-    force_a, force_b = sides(force_a, force_b, "atom")
-    cell_atoms = atom_count * lax.axis_size("atom")
-    loss_scale = 2.0 * (energy[0, 0] / cell_atoms - energy_ref[0]) / cell_atoms
+    cell_atoms = atom_count * slabs
+    loss_scale = 2.0 * (energy[0:1] / cell_atoms - energy_ref[0]) / cell_atoms
     virial_row = embedding.shape[0] + basis_count + 5 * LANES
     line = lax.broadcasted_iota(jnp.int32, (G_ROWS, 1), 0)
     one = grads_one * jnp.where((line >= virial_row) & (line < virial_row + 64), 1.0, loss_scale)
     two = grads_two * loss_scale
     core = group % 2 == 1
     x = jnp.where(core, one, two) + swap(jnp.where(core, two, one), "dp", 1)
-    x, force_a, force_b = lax.optimization_barrier((x, force_a, force_b))
-    far = [b for b in bits[1:]]
-    across, along = group // 2 == 1, (me // 2) % 2 == 1
-    upper = (jnp.where(core, along, across), jnp.where(core, across, along))
-
-    def x_or_z(g, p, turned):
-        return (g, p ^ 2) if (g % 2 == 1) != turned else (g ^ 2, p)
-
-    for n in range(2):
-        half = x.shape[0] // 2
-        low_part, high_part = x[:half], x[half:]
-        sent = jnp.where(upper[n], low_part, high_part)
-        x = jnp.where(upper[n], high_part, low_part) + exchange(sent, lambda g, p: x_or_z(g, p, n == 1))
-    order = [1] + far
-    for n in range(len(order)):
-        first, second = order[n], order[(n + 1) % len(order)]
-        x = x + exchange(x, lambda g, p: (g, p ^ (second if g % 2 else first)))
-    for n in (1, 0):
-        received = exchange(x, lambda g, p: x_or_z(g, p, n == 1))
-        x = jnp.where(upper[n], jnp.concatenate([received, x]), jnp.concatenate([x, received]))
+    quarter = G_ROWS // 4
+
+    def piece(k):
+        return lax.dynamic_slice_in_dim(x, (plane ^ k) * quarter, quarter, 0)
+
+    def plane_move(k):
+        return lambda g, p: (g ^ (2 * (k >> 1)), p ^ (k & 1))
+
+    joined = exchange(jnp.concatenate([piece(1), force_sent]), plane_move(1))
+    second, third = exchange(piece(2), plane_move(2)), exchange(piece(3), plane_move(3))
+    force_a, force_b = joined[quarter : quarter + 8], joined[quarter + 8 :]
+    y = piece(0) + joined[:quarter] + second + third
+    for n in range(levels):
+        one_bit, two_bit = bits[n], bits[(n + 1) % levels]
+        joined = exchange(jnp.concatenate([y, force_b]), lambda g, p: (g, p ^ (two_bit if g % 2 else one_bit)))
+        y = y + joined[:quarter]
+        force_b = jnp.concatenate([force_b, joined[quarter:]])
+    x = jnp.concatenate([y] + [exchange(y, plane_move(k)) for k in (1, 2, 3)])
     other = swap(x, "dp", 1)
     weights = (embedding,) + layer + (readout_mid, out_row)
     outs = (f32(1, 1), f32(3, atom_count), f32(1, 3, 3)) + tuple(f32(*x.shape) for x in weights)
@@ -786,7 +882,7 @@
         outs,
         [smem(), smem()] + [vmem()] * 6,
         [smem()] + [whole(x) for x in outs[1:]],
-        [],
+        [pltpu.VMEM((G_ROWS, LANES), F32)] * 2,
         10**8,
         par, cell, energy, force, force_a, force_b, x, other,
     )

time: 114 us -> 88.7 us (0.78)
  waiting for transfers between devices: 46.6 us -> 27.5 us
  local copies, waits for them, and re-layouts: 9.15 us -> 2.68 us
  starting transfers between devices: 22.1 us -> 25.8 us
  Pallas kernels: 33.2 us -> 30.1 us
    ppermute x8 -> x6, waiting for transfers between devices: 11.6 us -> 2.31 us  [sides(): return (lax.ppermute(a, axis, pairs_a), lax.ppermute(b, axis, pairs_b))]
    ppermute x6 -> x8, waiting for transfers between devices: 30.2 us -> 21.6 us  [exchange(): return lax.ppermute(x, ('dp', 'atom'), route)]
    unnamed x40 -> x28, local copies, waits for them, and re-layouts: 8.63 us -> 2.64 us
    ppermute x4 -> x5, starting transfers between devices: 0.93 us -> 4.59 us  [swap(): lax.ppermute(x, axis, [(i, i ^ bit) for i in range(lax.axis_size(axis))])]
    ppermute x6 -> x8, starting transfers between devices: 3.89 us -> 7.23 us  [exchange(): return lax.ppermute(x, ('dp', 'atom'), route)]
    ppermute x8 -> x6, starting transfers between devices: 17.2 us -> 14 us  [sides(): return (lax.ppermute(a, axis, pairs_a), lax.ppermute(b, axis, pairs_b))]
    pallas_call x5 -> x7, Pallas kernels: 33.2 us -> 30.1 us  [call(): pl.pallas_call(kernel, grid=(1,), out_shape=outs, in_specs=in_specs, out_...]
    ppermute x4 -> x5, waiting for transfers between devices: 4.78 us -> 3.62 us  [swap(): lax.ppermute(x, axis, [(i, i ^ bit) for i in range(lax.axis_size(axis))])]
  transfers between devices with their start and end apart: 18 -> 19, of which waited for: 14 -> 11; matrix products, arithmetic and copies ran while one was open for 0% -> 0% of each run, Pallas kernels for 8% -> 18%
where the time goes in v3:
time: 88.7 us; the launch traced here: 88.5 us
  Pallas kernels  30.1 us (34%)
  waiting for transfers between devices  27.5 us (31%)
  starting transfers between devices  25.8 us (29%)
  local copies, waits for them, and re-layouts  2.68 us (3%)
  between operations  1.66 us (2%)
    pallas_call x7, Pallas kernels, call(): pl.pallas_call(kernel, grid=(1,), out_shape=outs, in_specs=in_specs, out_...  30.1 us
    ppermute x8, waiting for transfers between devices, exchange(): return lax.ppermute(x, ('dp', 'atom'), route)  21.6 us
    ppermute x6, starting transfers between devices, sides(): return (lax.ppermute(a, axis, pairs_a), lax.ppermute(b, axis, pairs_b))  14 us
    ppermute x8, starting transfers between devices, exchange(): return lax.ppermute(x, ('dp', 'atom'), route)  7.23 us
    ppermute x5, starting transfers between devices, swap(): lax.ppermute(x, axis, [(i, i ^ bit) for i in range(lax.axis_size(axis))])  4.59 us
    ppermute x5, waiting for transfers between devices, swap(): lax.ppermute(x, axis, [(i, i ^ bit) for i in range(lax.axis_size(axis))])  3.62 us
    unnamed x28, local copies, waits for them, and re-layouts  2.64 us
    ppermute x6, waiting for transfers between devices, sides(): return (lax.ppermute(a, axis, pairs_a), lax.ppermute(b, axis, pairs_b))  2.31 us
  transfers between devices with their start and end apart: 19, of which 11 were waited for; matrix products, arithmetic and copies ran while one was open for 0% of the time, Pallas kernels for 18%

profile of v3, /device:TPU:0, one launch (start us, length us, event | category | flops | bytes accessed | tf_op | source)
XLA Modules:
  0.0 88.5 jit_solution(9110604012078241580)
XLA Ops:
  0.6 0.7 copy.28.cell_ref
  1.3 0.7 copy-done.9
  2.0 0.7 copy-done.10
  2.7 0.0 copy-start.4
  2.7 0.0 copy-start.6
  2.7 0.0 copy-start.7
  2.7 0.0 copy-start.8
  2.7 0.6 place.1.own_ref
  3.3 3.0 %collective-permute-start = (f32[8,128]{1,0:T(8,128)S(1)}, f32[8,128]{1,0:T(8,128)S(1)}, u32[]{:S(2)}, u32[]{:S(2)}) collective-permute-start(f32[8,128]{1,0:T(8,128)S(1)} %place.1.own_ref), channel_id=1, source_target_pairs={{0,1},{1,0},{2,3},{3,2},{4,5},{5,4},{6,7},{7,6},{8,9},{9,8},{10,11... | collective-permute-start | bytes 12296 | tf_op jit(solution)/shard_map/ppermute | solution.py:677
  6.4 3.5 %collective-permute-start.1 = (f32[8,128]{1,0:T(8,128)S(1)}, f32[8,128]{1,0:T(8,128)S(1)}, u32[]{:S(2)}, u32[]{:S(2)}) collective-permute-start(f32[8,128]{1,0:T(8,128)S(1)} %place.1.own_ref), channel_id=1, source_target_pairs={{0,7},{1,2},{2,1},{3,4},{4,3},{5,6},{6,5},{7,0},{8,15},{9,10},{10,... | collective-permute-start | bytes 12296 | tf_op jit(solution)/shard_map/ppermute | solution.py:677
  9.9 0.1 pad_add_fusion.par_ref
  10.6 2.0 %collective-permute-done.1.b_ref.pb_ref = f32[8,128]{1,0:T(8,128)S(1)} collective-permute-done((f32[8,128]{1,0:T(8,128)S(1)}, f32[8,128]{1,0:T(8,128)S(1)}, u32[]{:S(2)}, u32[]{:S(2)}) %collective-permute-start.1) | collective-permute-done | bytes 4128 | tf_op jit(solution)/shard_map/ppermute | solution.py:677
  12.7 4.7 %layer_one.1 = (f32[32,8,128]{2,1,0:T(8,128)S(1)}, f32[4,128,128]{2,1,0:T(8,128)S(1)}, f32[4,128,128]{2,1,0:T(8,128)S(1)}, f32[128,128]{1,0:T(8,128)S(1)}, f32[1...) custom-call(s32[4]{0:T(128)S(1)} %pad_add_fusion.par_ref, ...), custom_call_target="tpu_custom_call" | custom-call | flops 3000000000 | bytes 6000000 | tf_op jit(solution)/shard_map/layer_one/pallas_call | solution.py:706
  17.5 0.1 collective-permute-start.2
  17.6 3.6 %collective-permute-start.3 = (f32[128,128]{1,0:T(8,128)S(1)}, f32[128,128]{1,0:T(8,128)S(1)}, u32[]{:S(2)}, u32[]{:S(2)}) collective-permute-start(f32[128,128]{1,0:T(8,128)S(1)} %get-tuple-element.51), channel_id=1, source_target_pairs={{0,7},{1,2},{2,1},{3,4},{4,3},{5,6},{6,5},{7,0},{8,15},{9,10},{10,... | collective-permute-start | bytes 196616 | tf_op jit(solution)/shard_map/ppermute | solution.py:677
  21.2 3.1 %radial_two.1 = (f32[2,384,2048]{2,1,0:T(8,128)S(1)}, bf16[2,256,2048]{2,1,0:T(8,128)(2,1)S(1)}, bf16[2,128,2048]{2,1,0:T(8,128)(2,1)S(1)}, f32[2,128,2048]{2,1,0:T(8,128)S(1)}) custom-call(f32[32,8,128]{2,1,0:T(8,128)S(1)} %get-tuple-element.48.geom_ref, f32[2,64,128]{2,1,0:T(8,128)S(1)} %copy-done.1, f32[2,128,384]{2,1,0:T(8,128)S(1)} %copy-done), custom_call_target="tpu_custom_call" | custom-call | flops 3000000000 | bytes 6000000 | tf_op jit(solution)/shard_map/radial_two/pallas_call | solution.py:706
  24.3 0.3 collective-permute-done.3.b_ref
  24.6 7.3 %layer_two.1 = (f32[4,128,128]{2,1,0:T(8,128)S(1)}, f32[136,128]{1,0:T(8,128)S(1)}, f32[128,128]{1,0:T(8,128)S(1)}, f32[480,128]{1,0:T(8,128)S(1)}, f32[40,128]{...) custom-call(s32[4]{0:T(128)S(1)} %pad_add_fusion.par_ref, ...), custom_call_target="tpu_custom_call" | custom-call | flops 5000000000 | bytes 10000000 | tf_op jit(solution)/shard_map/layer_two/pallas_call | solution.py:706
  31.9 0.2 collective-permute-start.4
  32.1 3.5 %collective-permute-start.8 = (f32[128,128]{1,0:T(8,128)S(1)}, f32[128,128]{1,0:T(8,128)S(1)}, u32[]{:S(2)}, u32[]{:S(2)}) collective-permute-start(f32[128,128]{1,0:T(8,128)S(1)} %get-tuple-element.63), channel_id=1, source_target_pairs={{0,7},{1,2},{2,1},{3,4},{4,3},{5,6},{6,5},{7,0},{8,15},{9,10},{10,... | collective-permute-start | bytes 196616 | tf_op jit(solution)/shard_map/ppermute | solution.py:677
  35.6 5.3 %radial_two_back.1 = (f32[32,8,128]{2,1,0:T(8,128)S(1)}, f32[928,128]{1,0:T(8,128)S(1)}) custom-call(f32[32,8,128]{2,1,0:T(8,128)S(1)} %get-tuple-element.48.geom_ref, f32[2,384,2048]{2,1,0:T(8,128)S(1)} %get-tuple-element.52.filters_ref, bf16[2,256,2048]{2,1,0:T(8,128)(2,1)S(1)} %get-tuple-element.54.hidden_ref, ...), custom_call_target="tpu_custom_call" | custom-call | flops 5000000000 | bytes 10000000 | tf_op jit(solution)/shard_map/radial_two_back/pallas_call | solution.py:706
  41.0 0.1 collective-permute-start.5
  41.1 1.0 %collective-permute-start.6 = (f32[8,128]{1,0:T(8,128)S(1)}, f32[8,128]{1,0:T(8,128)S(1)}, u32[]{:S(2)}, u32[]{:S(2)}) collective-permute-start(f32[8,128]{1,0:T(8,128)S(1)} %slice_add_fusion.3), channel_id=1, source_target_pairs={{0,4},{1,5},{2,6},{3,7},{4,0},{5,1},{6,2},{7,3},{8,12},{9,13},{10,... | collective-permute-start | bytes 12296 | tf_op jit(solution)/shard_map/ppermute | solution.py:681
  42.0 3.4 %collective-permute-start.7 = (f32[8,128]{1,0:T(8,128)S(1)}, f32[8,128]{1,0:T(8,128)S(1)}, u32[]{:S(2)}, u32[]{:S(2)}) collective-permute-start(f32[8,128]{1,0:T(8,128)S(1)} %slice_add_fusion.3), channel_id=1, source_target_pairs={{0,6},{1,7},{2,4},{3,5},{4,2},{5,3},{6,0},{7,1},{8,14},{9,15},{10,... | collective-permute-start | bytes 12296 | tf_op jit(solution)/shard_map/ppermute | solution.py:681
  45.4 7.4 %layer_one_back.1 = (f32[16,128]{1,0:T(8,128)S(1)}, f32[16,128]{1,0:T(8,128)S(1)}, f32[928,128]{1,0:T(8,128)S(1)}) custom-call(s32[4]{0:T(128)S(1)} %pad_add_fusion.par_ref, f32[32,8,128]{2,1,0:T(8,128)S(1)} %get-tuple-element.48.geom_ref, f32[32,8,128]{2,1,0:T(8,128)S(1)} %get-tuple-element.60.dgeom_ref, f32[4,128,128]{2,1,0:T(8,128)S(1)} %get-tuple-element.61.agg_ref, ...), custom_call_target="tpu_custom_call" | custom-call | flops 6000000000 | bytes 12000000 | tf_op jit(solution)/shard_map/layer_one_back/pallas_call | solution.py:706
  52.9 0.2 multiply_select_fusion
  53.1 0.1 collective-permute-start.9
  53.2 1.8 %collective-permute-done.9 = f32[928,128]{1,0:T(8,128)S(1)} collective-permute-done((f32[928,128]{1,0:T(8,128)S(1)}, f32[928,128]{1,0:T(8,128)S(1)}, u32[]{:S(2)}, u32[]{:S(2)}) %collective-permute-start.9) | collective-permute-done | bytes 475168 | tf_op jit(solution)/shard_map/ppermute | solution.py:681
  55.0 0.2 select_add_fusion
  55.3 0.1 collective-permute-start.10
  55.4 1.6 %collective-permute-start.11 = (f32[232,128]{1,0:T(8,128)S(1)}, f32[232,128]{1,0:T(8,128)S(1)}, u32[]{:S(2)}, u32[]{:S(2)}) collective-permute-start(f32[232,128]{1,0:T(8,128)S(1)} %get-tuple-element.96), channel_id=1, source_target_pairs={{0,16},{1,17},{2,18},{3,19},{4,20},{5,21},{6,22},{7,23},{8,24},{9,... | collective-permute-start | bytes 356360 | tf_op jit(solution)/shard_map/ppermute | solution.py:726
  56.9 1.9 %collective-permute-start.12 = (f32[232,128]{1,0:T(8,128)S(1)}, f32[232,128]{1,0:T(8,128)S(1)}, u32[]{:S(2)}, u32[]{:S(2)}) collective-permute-start(f32[232,128]{1,0:T(8,128)S(1)} %get-tuple-element.97), channel_id=1, source_target_pairs={{0,17},{1,16},{2,19},{3,18},{4,21},{5,20},{6,23},{7,22},{8,25},{9,... | collective-permute-start | bytes 356360 | tf_op jit(solution)/shard_map/ppermute | solution.py:726
  58.8 2.1 %collective-permute-done.10 = f32[248,128]{1,0:T(8,128)S(1)} collective-permute-done((f32[248,128]{1,0:T(8,128)S(1)}, f32[248,128]{1,0:T(8,128)S(1)}, u32[]{:S(2)}, u32[]{:S(2)}) %collective-permute-start.10) | collective-permute-done | bytes 127008 | tf_op jit(solution)/shard_map/ppermute | solution.py:726
  60.9 3.4 %collective-permute-done.12 = f32[232,128]{1,0:T(8,128)S(1)} collective-permute-done((f32[232,128]{1,0:T(8,128)S(1)}, f32[232,128]{1,0:T(8,128)S(1)}, u32[]{:S(2)}, u32[]{:S(2)}) %collective-permute-start.12) | collective-permute-done | bytes 118816 | tf_op jit(solution)/shard_map/ppermute | solution.py:726
  64.4 0.1 collective-permute-start.13
  64.5 5.2 %collective-permute-done.13 = f32[240,128]{1,0:T(8,128)S(1)} collective-permute-done((f32[240,128]{1,0:T(8,128)S(1)}, f32[240,128]{1,0:T(8,128)S(1)}, u32[]{:S(2)}, u32[]{:S(2)}) %collective-permute-start.13) | collective-permute-done | bytes 122912 | tf_op jit(solution)/shard_map/ppermute | solution.py:726
  69.7 0.1 collective-permute-start.14
  69.8 6.3 %collective-permute-done.14 = f32[248,128]{1,0:T(8,128)S(1)} collective-permute-done((f32[248,128]{1,0:T(8,128)S(1)}, f32[248,128]{1,0:T(8,128)S(1)}, u32[]{:S(2)}, u32[]{:S(2)}) %collective-permute-start.14) | collective-permute-done | bytes 127008 | tf_op jit(solution)/shard_map/ppermute | solution.py:726
  76.1 1.0 %collective-permute-start.15 = (f32[232,128]{1,0:T(8,128)S(1)}, f32[232,128]{1,0:T(8,128)S(1)}, u32[]{:S(2)}, u32[]{:S(2)}) collective-permute-start(f32[232,128]{1,0:T(8,128)S(1)} %slice_add_fusion), channel_id=1, source_target_pairs={{0,1},{1,0},{2,3},{3,2},{4,5},{5,4},{6,7},{7,6},{8,9},{9,8},{10,11... | collective-permute-start | bytes 356360 | tf_op jit(solution)/shard_map/ppermute | solution.py:726
  77.1 1.5 %collective-permute-start.16 = (f32[232,128]{1,0:T(8,128)S(1)}, f32[232,128]{1,0:T(8,128)S(1)}, u32[]{:S(2)}, u32[]{:S(2)}) collective-permute-start(f32[232,128]{1,0:T(8,128)S(1)} %slice_add_fusion), channel_id=1, source_target_pairs={{0,16},{1,17},{2,18},{3,19},{4,20},{5,21},{6,22},{7,23},{8,24},{9,... | collective-permute-start | bytes 356360 | tf_op jit(solution)/shard_map/ppermute | solution.py:726
  78.5 1.1 %collective-permute-start.17 = (f32[232,128]{1,0:T(8,128)S(1)}, f32[232,128]{1,0:T(8,128)S(1)}, u32[]{:S(2)}, u32[]{:S(2)}) collective-permute-start(f32[232,128]{1,0:T(8,128)S(1)} %slice_add_fusion), channel_id=1, source_target_pairs={{0,17},{1,16},{2,19},{3,18},{4,21},{5,20},{6,23},{7,22},{8,25},{9,... | collective-permute-start | bytes 356360 | tf_op jit(solution)/shard_map/ppermute | solution.py:726
  79.7 1.3 %collective-permute-done.15 = f32[232,128]{1,0:T(8,128)S(1)} collective-permute-done((f32[232,128]{1,0:T(8,128)S(1)}, f32[232,128]{1,0:T(8,128)S(1)}, u32[]{:S(2)}, u32[]{:S(2)}) %collective-permute-start.15) | collective-permute-done | bytes 118816 | tf_op jit(solution)/shard_map/ppermute | solution.py:726
  81.0 0.9 %collective-permute-done.16 = f32[232,128]{1,0:T(8,128)S(1)} collective-permute-done((f32[232,128]{1,0:T(8,128)S(1)}, f32[232,128]{1,0:T(8,128)S(1)}, u32[]{:S(2)}, u32[]{:S(2)}) %collective-permute-start.16) | collective-permute-done | bytes 118816 | tf_op jit(solution)/shard_map/ppermute | solution.py:726
  81.9 2.4 %collective-permute-done.17 = f32[232,128]{1,0:T(8,128)S(1)} collective-permute-done((f32[232,128]{1,0:T(8,128)S(1)}, f32[232,128]{1,0:T(8,128)S(1)}, u32[]{:S(2)}, u32[]{:S(2)}) %collective-permute-start.17) | collective-permute-done | bytes 118816 | tf_op jit(solution)/shard_map/ppermute | solution.py:726
  84.3 0.1 collective-permute-start.18
  84.4 1.8 %collective-permute-done.18.other_turned = f32[928,128]{1,0:T(8,128)S(1)} collective-permute-done((f32[928,128]{1,0:T(8,128)S(1)}, f32[928,128]{1,0:T(8,128)S(1)}, u32[]{:S(2)}, u32[]{:S(2)}) %collective-permute-start.18) | collective-permute-done | bytes 475168 | tf_op jit(solution)/shard_map/ppermute | solution.py:681
  86.2 1.7 %final.1 = (f32[1,1]{1,0:T(1,128)}, f32[3,128]{1,0:T(4,128)}, f32[1,3,3]{2,1,0:T(4,128)S(1)}, f32[96,128]{1,0:T(8,128)}, f32[2,64,128]{2,1,0:T(8,128)}, /*index=...) custom-call(s32[4]{0:T(128)S(1)} %pad_add_fusion.par_ref, ...), custom_call_target="tpu_custom_call" | custom-call | flops 100000000 | bytes 200000 | tf_op jit(solution)/shard_map/final/pallas_call | solution.py:706
  87.9 0.6 copy.29
  (44 shorter events, 0.3 us)
Async XLA Ops:
  1.3 0.7 copy-start.9
  2.0 0.7 copy-start.10
  2.7 10.0 %copy-start = (f32[2,128,384]{2,1,0:T(8,128)S(1)}, f32[2,128,384]{2,1,0:T(8,128)}, u32[]{:S(2)}) copy-start(f32[2,128,384]{2,1,0:T(8,128)} %rout_ref.7) | copy-start | bytes 1179652
  2.7 10.0 %copy-start.1 = (f32[2,64,128]{2,1,0:T(8,128)S(1)}, f32[2,64,128]{2,1,0:T(8,128)}, u32[]{:S(2)}) copy-start(f32[2,64,128]{2,1,0:T(8,128)} %rin_ref.7) | copy-start | bytes 196612
  2.7 10.0 %copy-start.2 = (f32[2,128,128]{2,1,0:T(8,128)S(1)}, f32[2,128,128]{2,1,0:T(8,128)}, u32[]{:S(2)}) copy-start(f32[2,128,128]{2,1,0:T(8,128)} %sm_ref.5) | copy-start | bytes 393220
  2.7 10.0 %copy-start.3 = (f32[2,128,128]{2,1,0:T(8,128)S(1)}, f32[2,128,128]{2,1,0:T(8,128)}, u32[]{:S(2)}) copy-start(f32[2,128,128]{2,1,0:T(8,128)} %vm_ref.5) | copy-start | bytes 393220
  2.7 10.0 %copy-start.4 = (f32[2,128,128]{2,1,0:T(8,128)S(1)}, f32[2,128,128]{2,1,0:T(8,128)}, u32[]{:S(2)}) copy-start(f32[2,128,128]{2,1,0:T(8,128)} %vg_ref.5) | copy-start | bytes 393220
  2.7 10.0 %copy-start.6 = (s32[3,32,128]{2,1,0:T(8,128)S(1)}, s32[3,32,128]{2,1,0:T(8,128)}, u32[]{:S(2)}) copy-start(s32[3,32,128]{2,1,0:T(8,128)} %shift_ref.1) | copy-start | bytes 147460
  2.7 10.0 %copy-start.7 = (f32[96,128]{1,0:T(8,128)S(1)}, f32[96,128]{1,0:T(8,128)}, u32[]{:S(2)}) copy-start(f32[96,128]{1,0:T(8,128)} %emb_ref.3) | copy-start | bytes 147460
  2.7 10.0 %copy-start.8 = (s32[32,128]{1,0:T(8,128)S(1)}, s32[32,128]{1,0:T(8,128)}, u32[]{:S(2)}) copy-start(s32[32,128]{1,0:T(8,128)} %nb_ref.1) | copy-start | bytes 49156
  2.7 10.0 %copy-start.11 = (s32[128]{0:T(128)S(1)}, s32[128]{0:T(128)}, u32[]{:S(2)}) copy-start(s32[128]{0:T(128)} %param.18) | copy-start | bytes 1540
  3.3 7.3 %collective-permute-start = (f32[8,128]{1,0:T(8,128)S(1)}, f32[8,128]{1,0:T(8,128)S(1)}, u32[]{:S(2)}, u32[]{:S(2)}) collective-permute-start(f32[8,128]{1,0:T(8,128)S(1)} %place.1.own_ref), channel_id=1, source_target_pairs={{0,1},{1,0},{2,3},{3,2},{4,5},{5,4},{6,7},{7,6},{8,9},{9,8},{10,11... | collective-permute-start | bytes 12296 | tf_op jit(solution)/shard_map/ppermute | solution.py:677
  6.4 6.3 %collective-permute-start.1 = (f32[8,128]{1,0:T(8,128)S(1)}, f32[8,128]{1,0:T(8,128)S(1)}, u32[]{:S(2)}, u32[]{:S(2)}) collective-permute-start(f32[8,128]{1,0:T(8,128)S(1)} %place.1.own_ref), channel_id=1, source_target_pairs={{0,7},{1,2},{2,1},{3,4},{4,3},{5,6},{6,5},{7,0},{8,15},{9,10},{10,... | collective-permute-start | bytes 12296 | tf_op jit(solution)/shard_map/ppermute | solution.py:677
  17.5 6.8 %collective-permute-start.2 = (f32[128,128]{1,0:T(8,128)S(1)}, f32[128,128]{1,0:T(8,128)S(1)}, u32[]{:S(2)}, u32[]{:S(2)}) collective-permute-start(f32[128,128]{1,0:T(8,128)S(1)} %get-tuple-element.50), channel_id=1, source_target_pairs={{0,1},{1,0},{2,3},{3,2},{4,5},{5,4},{6,7},{7,6},{8,9},{9,8},{10,11... | collective-permute-start | bytes 196616 | tf_op jit(solution)/shard_map/ppermute | solution.py:677
  17.6 7.0 %collective-permute-start.3 = (f32[128,128]{1,0:T(8,128)S(1)}, f32[128,128]{1,0:T(8,128)S(1)}, u32[]{:S(2)}, u32[]{:S(2)}) collective-permute-start(f32[128,128]{1,0:T(8,128)S(1)} %get-tuple-element.51), channel_id=1, source_target_pairs={{0,7},{1,2},{2,1},{3,4},{4,3},{5,6},{6,5},{7,0},{8,15},{9,10},{10,... | collective-permute-start | bytes 196616 | tf_op jit(solution)/shard_map/ppermute | solution.py:677
  21.2 3.4 %copy-start.5 = (f32[128,128]{1,0:T(8,128)S(1)}, f32[128,128]{1,0:T(8,128)}, u32[]{:S(2)}) copy-start(f32[128,128]{1,0:T(8,128)} %mid_ref.1) | copy-start | bytes 196612
  21.2 3.4 %copy-start.12 = (f32[128]{0:T(128)S(1)}, f32[128]{0:T(128)}, u32[]{:S(2)}) copy-start(f32[128]{0:T(128)} %param.29) | copy-start | bytes 1540
  31.9 9.1 %collective-permute-start.4 = (f32[136,128]{1,0:T(8,128)S(1)}, f32[136,128]{1,0:T(8,128)S(1)}, u32[]{:S(2)}, u32[]{:S(2)}) collective-permute-start(f32[136,128]{1,0:T(8,128)S(1)} %get-tuple-element.53), channel_id=1, source_target_pairs={{0,1},{1,0},{2,3},{3,2},{4,5},{5,4},{6,7},{7,6},{8,9},{9,8},{10,11... | collective-permute-start | bytes 208904 | tf_op jit(solution)/shard_map/ppermute | solution.py:677
  32.1 13.4 %collective-permute-start.8 = (f32[128,128]{1,0:T(8,128)S(1)}, f32[128,128]{1,0:T(8,128)S(1)}, u32[]{:S(2)}, u32[]{:S(2)}) collective-permute-start(f32[128,128]{1,0:T(8,128)S(1)} %get-tuple-element.63), channel_id=1, source_target_pairs={{0,7},{1,2},{2,1},{3,4},{4,3},{5,6},{6,5},{7,0},{8,15},{9,10},{10,... | collective-permute-start | bytes 196616 | tf_op jit(solution)/shard_map/ppermute | solution.py:677
  41.0 11.9 %collective-permute-start.5 = (f32[8,128]{1,0:T(8,128)S(1)}, f32[8,128]{1,0:T(8,128)S(1)}, u32[]{:S(2)}, u32[]{:S(2)}) collective-permute-start(f32[8,128]{1,0:T(8,128)S(1)} %slice_add_fusion.3), channel_id=1, source_target_pairs={{0,2},{1,3},{2,0},{3,1},{4,6},{5,7},{6,4},{7,5},{8,10},{9,11},{10,... | collective-permute-start | bytes 12296 | tf_op jit(solution)/shard_map/ppermute | solution.py:681
  41.1 11.8 %collective-permute-start.6 = (f32[8,128]{1,0:T(8,128)S(1)}, f32[8,128]{1,0:T(8,128)S(1)}, u32[]{:S(2)}, u32[]{:S(2)}) collective-permute-start(f32[8,128]{1,0:T(8,128)S(1)} %slice_add_fusion.3), channel_id=1, source_target_pairs={{0,4},{1,5},{2,6},{3,7},{4,0},{5,1},{6,2},{7,3},{8,12},{9,13},{10,... | collective-permute-start | bytes 12296 | tf_op jit(solution)/shard_map/ppermute | solution.py:681
  42.0 10.9 %collective-permute-start.7 = (f32[8,128]{1,0:T(8,128)S(1)}, f32[8,128]{1,0:T(8,128)S(1)}, u32[]{:S(2)}, u32[]{:S(2)}) collective-permute-start(f32[8,128]{1,0:T(8,128)S(1)} %slice_add_fusion.3), channel_id=1, source_target_pairs={{0,6},{1,7},{2,4},{3,5},{4,2},{5,3},{6,0},{7,1},{8,14},{9,15},{10,... | collective-permute-start | bytes 12296 | tf_op jit(solution)/shard_map/ppermute | solution.py:681
  53.1 1.9 %collective-permute-start.9 = (f32[928,128]{1,0:T(8,128)S(1)}, f32[928,128]{1,0:T(8,128)S(1)}, u32[]{:S(2)}, u32[]{:S(2)}) collective-permute-start(f32[928,128]{1,0:T(8,128)S(1)} %multiply_select_fusion), channel_id=1, source_target_pairs={{0,8},{8,0},{16,24},{24,16},{1,9},{9,1},{17,25},{25,17},{2,10},{10... | collective-permute-start | bytes 1425416 | tf_op jit(solution)/shard_map/ppermute | solution.py:681
  55.3 5.6 %collective-permute-start.10 = (f32[248,128]{1,0:T(8,128)S(1)}, f32[248,128]{1,0:T(8,128)S(1)}, u32[]{:S(2)}, u32[]{:S(2)}) collective-permute-start(f32[248,128]{1,0:T(8,128)S(1)} %pad_maximum_fusion.1), channel_id=1, source_target_pairs={{0,1},{1,0},{2,3},{3,2},{4,5},{5,4},{6,7},{7,6},{8,9},{9,8},{10,11... | collective-permute-start | bytes 380936 | tf_op jit(solution)/shard_map/ppermute | solution.py:726
  55.4 5.5 %collective-permute-start.11 = (f32[232,128]{1,0:T(8,128)S(1)}, f32[232,128]{1,0:T(8,128)S(1)}, u32[]{:S(2)}, u32[]{:S(2)}) collective-permute-start(f32[232,128]{1,0:T(8,128)S(1)} %get-tuple-element.96), channel_id=1, source_target_pairs={{0,16},{1,17},{2,18},{3,19},{4,20},{5,21},{6,22},{7,23},{8,24},{9,... | collective-permute-start | bytes 356360 | tf_op jit(solution)/shard_map/ppermute | solution.py:726
  56.9 7.4 %collective-permute-start.12 = (f32[232,128]{1,0:T(8,128)S(1)}, f32[232,128]{1,0:T(8,128)S(1)}, u32[]{:S(2)}, u32[]{:S(2)}) collective-permute-start(f32[232,128]{1,0:T(8,128)S(1)} %get-tuple-element.97), channel_id=1, source_target_pairs={{0,17},{1,16},{2,19},{3,18},{4,21},{5,20},{6,23},{7,22},{8,25},{9,... | collective-permute-start | bytes 356360 | tf_op jit(solution)/shard_map/ppermute | solution.py:726
  64.4 5.2 %collective-permute-start.13 = (f32[240,128]{1,0:T(8,128)S(1)}, f32[240,128]{1,0:T(8,128)S(1)}, u32[]{:S(2)}, u32[]{:S(2)}) collective-permute-start(f32[240,128]{1,0:T(8,128)S(1)} %pad_maximum_fusion.3), channel_id=1, source_target_pairs={{0,2},{1,3},{2,0},{3,1},{4,6},{5,7},{6,4},{7,5},{8,12},{9,13},{10,... | collective-permute-start | bytes 368648 | tf_op jit(solution)/shard_map/ppermute | solution.py:726
  69.7 6.4 %collective-permute-start.14 = (f32[248,128]{1,0:T(8,128)S(1)}, f32[248,128]{1,0:T(8,128)S(1)}, u32[]{:S(2)}, u32[]{:S(2)}) collective-permute-start(f32[248,128]{1,0:T(8,128)S(1)} %pad_maximum_fusion.2), channel_id=1, source_target_pairs={{0,4},{1,5},{2,6},{3,7},{4,0},{5,1},{6,2},{7,3},{8,10},{9,11},{10,... | collective-permute-start | bytes 380936 | tf_op jit(solution)/shard_map/ppermute | solution.py:726
  76.1 4.9 %collective-permute-start.15 = (f32[232,128]{1,0:T(8,128)S(1)}, f32[232,128]{1,0:T(8,128)S(1)}, u32[]{:S(2)}, u32[]{:S(2)}) collective-permute-start(f32[232,128]{1,0:T(8,128)S(1)} %slice_add_fusion), channel_id=1, source_target_pairs={{0,1},{1,0},{2,3},{3,2},{4,5},{5,4},{6,7},{7,6},{8,9},{9,8},{10,11... | collective-permute-start | bytes 356360 | tf_op jit(solution)/shard_map/ppermute | solution.py:726
  77.1 4.8 %collective-permute-start.16 = (f32[232,128]{1,0:T(8,128)S(1)}, f32[232,128]{1,0:T(8,128)S(1)}, u32[]{:S(2)}, u32[]{:S(2)}) collective-permute-start(f32[232,128]{1,0:T(8,128)S(1)} %slice_add_fusion), channel_id=1, source_target_pairs={{0,16},{1,17},{2,18},{3,19},{4,20},{5,21},{6,22},{7,23},{8,24},{9,... | collective-permute-start | bytes 356360 | tf_op jit(solution)/shard_map/ppermute | solution.py:726
  78.5 5.7 %collective-permute-start.17 = (f32[232,128]{1,0:T(8,128)S(1)}, f32[232,128]{1,0:T(8,128)S(1)}, u32[]{:S(2)}, u32[]{:S(2)}) collective-permute-start(f32[232,128]{1,0:T(8,128)S(1)} %slice_add_fusion), channel_id=1, source_target_pairs={{0,17},{1,16},{2,19},{3,18},{4,21},{5,20},{6,23},{7,22},{8,25},{9,... | collective-permute-start | bytes 356360 | tf_op jit(solution)/shard_map/ppermute | solution.py:726
  84.3 1.9 %collective-permute-start.18 = (f32[928,128]{1,0:T(8,128)S(1)}, f32[928,128]{1,0:T(8,128)S(1)}, u32[]{:S(2)}, u32[]{:S(2)}) collective-permute-start(f32[928,128]{1,0:T(8,128)S(1)} %pad_maximum_fusion.mine_turned), channel_id=1, source_target_pairs={{0,8},{8,0},{16,24},{24,16},{1,9},{9,1},{17,25},{25,17},{2,10},{10... | collective-permute-start | bytes 1425416 | tf_op jit(solution)/shard_map/ppermute | solution.py:681

commit v4 on v3

--- a/solution.py
+++ b/solution.py
@@ -171,7 +171,8 @@
         radial(edge_rows(geom, t), t, ri4, ro3, kept, basis_count)
         return carry
 
-    lax.fori_loop(0, geom.shape[0] // ROWS, step, 0)
+    for t in range(geom.shape[0] // ROWS):
+        step(t, 0)
 
 
 def forward_edges(geom, tab, acc, found_ref, filters_of, vectors):
@@ -201,7 +202,8 @@
             acc[h, n] += sums[n]
         return carry
 
-    lax.fori_loop(0, 2 * per_half, step, 0)
+    for t in range(2 * per_half):
+        step(t, 0)
 
 
 def aggregates(acc, scale):
@@ -326,23 +328,30 @@
     return hot_own, hot_beside
 
 
-def place_kernel(cell_ref, frac_ref, species_ref, own_ref):
-    own_ref[...] = jnp.zeros(own_ref.shape, F32)
-    for c in range(3):
-        own_ref[c : c + 1] = (
-            frac_ref[0:1] * cell_ref[0, 0, c] + frac_ref[1:2] * cell_ref[0, 1, c] + frac_ref[2:3] * cell_ref[0, 2, c]
-        )
-    own_ref[3:4] = species_ref[...].astype(F32)
+def positions(cell_ref, fractions):
+    rows = [
+        fractions[0:1] * cell_ref[0, 0, c] + fractions[1:2] * cell_ref[0, 1, c] + fractions[2:3] * cell_ref[0, 2, c]
+        for c in range(3)
+    ]
+    return jnp.concatenate(rows + [fractions[3:8]], axis=0)
+
+
+def prepare_kernel(rin_ref, rout_ref, *outs):
+    for layer, groups in enumerate(((0, 2), (0, 1, 2))):
+        ri4, ro3, rib, rob = outs[4 * layer : 4 * layer + 4]
+        rin, rout = rin_ref.at[pl.ds(layer, 1)], rout_ref.at[pl.ds(layer, 1)]
+        prepare_weights(rin, rout, ri4, ro3, groups)
+        prepare_back(rin, rout, rib, rob, groups)
 
 
 def first_kernel(
-    halo, par_ref, cell_ref, own_ref, a_ref, b_ref, nb_ref, count_ref, shift_ref, emb_ref, rin_ref, rout_ref,
+    halo, par_ref, cell_ref, own_ref, a_ref, b_ref, nb_ref, count_ref, shift_ref, emb_ref, ri4, ro3,
     sm_ref, vm_ref, vg_ref,
-    geom_ref, feat_ref, agg_ref, send_a, send_b, filters_ref, hidden_ref, basis_ref, slope_ref, found_ref,
-    tab, ri4, ro3, acc,
+    geom_ref, feat_ref, agg_ref, node_ref, send_a, send_b, filters_ref, hidden_ref, basis_ref, slope_ref, found_ref,
+    tab, acc,
 ):
     slots = nb_ref.shape[0]
-    basis_count = rin_ref.shape[1]
+    basis_count = ri4.shape[1] // 4
     pairs = slots // 2
     up, down = from_sides(par_ref, a_ref, b_ref)
     lane = lane_ids(pairs)
@@ -356,7 +365,7 @@
     nb = halves(nb_ref)
     shift = [halves(shift_ref, a) for a in range(3)]
     row_slot = 2 * lax.broadcasted_iota(jnp.int32, (pairs, LANES), 0) + jnp.where(low, 0, 1)
-    own = own_ref[...]
+    own, up, down = [positions(cell_ref, x) for x in (own_ref[...], up, down)]
     lane8 = lane_ids(own.shape[0])
     places = (jnp.where(lane8 < LANES - halo, own, down), jnp.where(lane8 >= halo, own, up))
     for h in range(2):
@@ -379,7 +388,6 @@
     hot_own, hot_beside = species_tables(own_ref, up, down, emb_ref, halo)
     s, beside = first_features(emb_ref, hot_own), first_features(emb_ref, hot_beside)
     store_tables(tab, [s], [beside], halo)
-    prepare_weights(rin_ref, rout_ref, ri4, ro3, (0, 2))
     kept = (filters_ref, hidden_ref, basis_ref, slope_ref)
     forward_edges(
         geom_ref, tab, acc, found_ref, lambda rows, t: radial(rows, t, ri4, ro3, kept, basis_count), False
@@ -387,6 +395,8 @@
     agg = aggregates(acc, slots**-0.5)
     w, size, u, gate = node_forward(agg, sm_ref[0], vm_ref[0], vg_ref[0])
     features = [s + u * sigmoid(u)] + [w[c] * gate for c in range(3)]
+    for n, x in enumerate(w + [size, u, gate]):
+        node_ref[n] = x
     for n in range(4):
         agg_ref[n] = agg[n]
         feat_ref[n] = features[n]
@@ -396,9 +406,8 @@
     send_b[...] = jnp.where(even, head, tail)
 
 
-def radial_kernel(geom_ref, rin_ref, rout_ref, filters_ref, hidden_ref, basis_ref, slope_ref, ri4, ro3):
-    prepare_weights(rin_ref, rout_ref, ri4, ro3, (0, 1, 2))
-    radial_edges(geom_ref, ri4, ro3, (filters_ref, hidden_ref, basis_ref, slope_ref), rin_ref.shape[1])
+def radial_kernel(geom_ref, ri4, ro3, filters_ref, hidden_ref, basis_ref, slope_ref):
+    radial_edges(geom_ref, ri4, ro3, (filters_ref, hidden_ref, basis_ref, slope_ref), ri4.shape[1] // 4)
 
 
 def second_kernel(
@@ -461,7 +470,8 @@
         dtab[h] += scatter(columns, one_hot_of(rows))
         return carry
 
-    lax.fori_loop(0, 2 * per_half, step, 0)
+    for t in range(2 * per_half):
+        step(t, 0)
     firsts = [dtab[0, q * LANES : (q + 1) * LANES] for q in range(4)]
     seconds = [dtab[1, q * LANES : (q + 1) * LANES] for q in range(4)]
     for q in range(4):
@@ -475,42 +485,38 @@
 
 
 def radial_back_kernel(
-    geom_ref, filters_ref, hidden_ref, basis_ref, slope_ref, found_ref, gacc, mixed_ref, rin_ref, rout_ref,
-    dgeom_ref, grad_ref,
-    rib, rob, dro, dri,
+    t, geom_ref, filters_ref, hidden_ref, basis_ref, slope_ref, found_ref, gacc, rib, rob, *rest
 ):
-    basis_count = rin_ref.shape[1]
-    groups = (0, 1, 2)
-    prepare_back(rin_ref, rout_ref, rib, rob, groups)
+    basis_count = rib.shape[0] // 2
+    last = len(rest) > 3
+    if last:
+        dro_first, dri_first, mixed_ref, dgeom_ref, grad_ref, dro, dri = rest
+        dro[...] = dro_first[...]
+        dri[...] = dri_first[...]
+    else:
+        dgeom_ref, dro, dri = rest
+        dro[...] = jnp.zeros(dro.shape, F32)
+        dri[...] = jnp.zeros(dri.shape, F32)
     kept = (filters_ref, hidden_ref, basis_ref, slope_ref)
-    per_half = geom_ref.shape[0] // 2 // ROWS
-    dro[...] = jnp.zeros(dro.shape, F32)
-    dri[...] = jnp.zeros(dri.shape, F32)
-
-    def step(t, carry):
-        rows = edge_rows(geom_ref, t)
-        gs, gv = step_derivatives(gacc, t // per_half)
-        d_dirs, d_dists = filter_terms(
-            rows, t, kept, found_ref.at[t], gs, gv, rib, rob, dro, dri, basis_count, True
-        )
-        for q in range(ROWS):
-            for c in range(3):
-                dgeom_ref[t * ROWS + q, c : c + 1, :] = d_dirs[q][c]
-            dgeom_ref[t * ROWS + q, 3:4, :] = d_dists[q]
-        return carry
-
-    lax.fori_loop(0, 2 * per_half, step, 0)
-    radial_grads(dro, dri, grad_ref, 0, basis_count, basis_count, len(groups))
-    grad_ref[basis_count + 3 * LANES :] = mixed_ref[...]
+    rows = edge_rows(geom_ref, t)
+    gs, gv = step_derivatives(gacc, t // (geom_ref.shape[0] // 2 // ROWS))
+    d_dirs, d_dists = filter_terms(rows, t, kept, found_ref.at[t], gs, gv, rib, rob, dro, dri, basis_count, True)
+    for q in range(ROWS):
+        for c in range(3):
+            dgeom_ref[q, c : c + 1, :] = d_dirs[q][c]
+        dgeom_ref[q, 3:4, :] = d_dists[q]
+    if last:
+        radial_grads(dro, dri, grad_ref, 0, basis_count, basis_count, 3)
+        grad_ref[basis_count + 3 * LANES :] = mixed_ref[...]
 
 
 def third_kernel(
-    halo, par_ref, geom_ref, dgeom_ref, agg_ref, cot_ref, a_ref, b_ref, own_ref, pa_ref, pb_ref, mid_tail,
-    filters_ref, hidden_ref, basis_ref, slope_ref, found_ref, emb_ref, rin_ref, rout_ref, sm_ref, vm_ref, vg_ref,
+    halo, par_ref, geom_ref, dgeom_one, dgeom_two, agg_ref, node_ref, cot_ref, a_ref, b_ref, own_ref, pa_ref, pb_ref, mid_tail,
+    filters_ref, hidden_ref, basis_ref, slope_ref, found_ref, emb_ref, rib, rob, sm_ref, vm_ref, vg_ref,
     force_ref, send_ref, grad_ref,
-    rib, rob, gacc, dro, dri, dtab, pull, virial,
+    gacc, dro, dri, dtab, pull, virial,
 ):
-    basis_count = rin_ref.shape[1]
+    basis_count = rib.shape[0] // 2
     slots = geom_ref.shape[0]
     scale = slots**-0.5
     lane = lane_ids(LANES)
@@ -525,14 +531,13 @@
     place_up, place_down = from_sides(par_ref, pa_ref, pb_ref)
     hot_own, hot_beside = species_tables(own_ref, place_up, place_down, emb_ref, halo)
     groups = (0, 2)
-    prepare_back(rin_ref, rout_ref, rib, rob, groups)
     count = emb_ref.shape[0]
 
     @pl.when(par_ref[0] >= 0)
     def _():
         agg = [agg_ref[n] for n in range(4)]
         sm, vm, vg = sm_ref[0], vm_ref[0], vg_ref[0]
-        w, size, u, gate = node_forward(agg, sm, vm, vg)
+        w, (size, u, gate) = [node_ref[c] for c in range(3)], [node_ref[n] for n in range(3, 6)]
         da, g_sm, g_vm, g_vg = node_backward(agg, w, size, u, gate, sm, vm, vg, cot[0], cot[1:], scale)
         for n in range(4):
             for h in range(2):
@@ -546,7 +551,7 @@
     virial[...] = jnp.zeros(virial.shape, F32)
 
     def finish(row, g, d_dir, d_dist):
-        more = dgeom_ref[row]
+        more = (dgeom_one, dgeom_two)[row // ROWS][row % ROWS]
         dist = g[3:4]
         toward = [g[c : c + 1] for c in range(3)]
         turn = [d_dir[c] + more[c : c + 1] for c in range(3)]
@@ -579,7 +584,8 @@
         dtab[h] += scatter(columns, one_hot_of(rows))
         return carry
 
-    lax.fori_loop(0, 2 * per_half, step, 0)
+    for t in range(2 * per_half):
+        step(t, 0)
     first, second = dtab[0, 0:LANES], dtab[1, 0:LANES]
     own_cot = cot[0] + jnp.where(lane < LANES - halo, first, 0.0) + jnp.where(lane >= halo, second, 0.0)
     side_cot = jnp.where(lane >= LANES - halo, first, 0.0) + jnp.where(lane < halo, second, 0.0)
@@ -659,7 +665,7 @@
             for a in range(3)
         ]
         stress = jnp.concatenate(lines, axis=0) / (jnp.zeros((3, LANES), F32) + det)
-        stress_ref[0] = stress[:, 0:3]
+        stress_ref[...] = stress[:, 0:3]
 
     @pl.when(par_ref[1] % 2 == 0)
     def _():
@@ -670,11 +676,17 @@
         write(mine, other)
 
 
-def sides(a, b, axis):
+def side_one(x, axis):
+    return lax.ppermute(x, axis, [(i, i ^ 1) for i in range(lax.axis_size(axis))])
+
+
+def side_two(x, axis):
     size = lax.axis_size(axis)
-    pairs_a = [(i, i ^ 1) for i in range(size)]
-    pairs_b = [(i, (i + 1) % size if i % 2 else (i - 1) % size) for i in range(size)]
-    return lax.ppermute(a, axis, pairs_a), lax.ppermute(b, axis, pairs_b)
+    return lax.ppermute(x, axis, [(i, (i + 1) % size if i % 2 else (i - 1) % size) for i in range(size)])
+
+
+def after(x, *others):
+    return lax.optimization_barrier((x,) + others)[0]
 
 
 def swap(x, axis, bit):
@@ -736,12 +748,9 @@
     basis_count = radial_in.shape[1]
     me = lax.axis_index("atom")
     group = lax.axis_index("dp")
-    species_row, counts_row, out_row = species[None], counts[None], readout_out[None]
-    own = call(
-        place_kernel, "place", f32(8, LANES), [smem(), whole(frac), whole(species_row)], vmem(), [], 10**10,
-        cell, frac, species_row,
-    )
-    side_a, side_b = sides(own, own, "atom")
+    counts_row, out_row = counts[None], readout_out[None]
+    own = jnp.concatenate([frac, species.astype(F32)[None], jnp.zeros((4, atom_count), F32)], axis=0)
+    side_a, side_b = side_one(own, "atom"), side_two(own, "atom")
     plane = group // 2 * 2 + me % 2
     slabs = lax.axis_size("atom")
     levels = (slabs - 1).bit_length() - 1
@@ -758,32 +767,46 @@
         halves = tuple(jax.ShapeDtypeStruct((steps, n, edges), BF16) for n in (2 * LANES, 2 * basis_count))
         return (f32(steps, groups * LANES, edges),) + halves + (f32(steps, LANES, edges),)
 
-    geom, feat, agg, feat_a, feat_b, *kept_one = call(
+    prepared = call(
+        prepare_kernel,
+        "prepare",
+        tuple(
+            jax.ShapeDtypeStruct(shape, BF16)
+            for n in (2, 3)
+            for shape in (
+                (LANES, 4 * basis_count), (n * LANES, 3 * LANES), (2 * basis_count, 2 * LANES), (2 * LANES, 2 * n * LANES)
+            )
+        ),
+        [vmem()] * 2,
+        [vmem()] * 8,
+        [],
+        10**10,
+        radial_in, radial_out,
+    )
+    geom, feat, agg, node, feat_a, feat_b, *kept_one = call(
         functools.partial(first_kernel, halo),
         "layer_one",
-        (f32(slots, 8, LANES), f32(4, LANES, LANES), f32(4, LANES, LANES), block, block) + kept(2)
+        (f32(slots, 8, LANES), f32(4, LANES, LANES), f32(4, LANES, LANES), f32(6, LANES, LANES), block, block) + kept(2)
         + (f32(steps, LANES, edges),),
-        [smem(), smem()] + [vmem()] * 7 + [layer_spec(x, 0) for x in layer],
-        [vmem()] * 10,
+        [smem(), smem()] + [vmem()] * 9 + [layer_spec(x, 0) for x in layer[2:]],
+        [vmem()] * 11,
         [
             pltpu.VMEM((2, LANES, 2 * LANES), BF16),
-            pltpu.VMEM((LANES, 4 * basis_count), BF16),
-            pltpu.VMEM((2 * LANES, 3 * LANES), BF16),
             pltpu.VMEM((2, 4, LANES, LANES), F32),
         ],
         3 * 10**9,
-        par, cell, own, side_a, side_b, neighbours, counts_row, shifts, embedding, *layer,
-    )
-    feat_a, feat_b = sides(feat_a, feat_b, "atom")
+        par, cell, own, side_a, side_b, neighbours, counts_row, shifts, embedding, *prepared[:2], *layer[2:],
+    )
+    feat_a, feat_b = side_one(feat_a, "atom"), side_two(feat_b, "atom")
     kept_two = call(
         radial_kernel,
         "radial_two",
         kept(3),
-        [vmem(), layer_spec(radial_in, 1), layer_spec(radial_out, 1)],
+        [vmem()] * 3,
         [vmem()] * 4,
-        [pltpu.VMEM((LANES, 4 * basis_count), BF16), pltpu.VMEM((3 * LANES, 3 * LANES), BF16)],
+        [],
         3 * 10**9,
-        geom, radial_in, radial_out,
+        geom, *prepared[4:6],
     )
     tail_rows = LANES - MID_ROWS
     mixed_rows = 3 * LANES + 8 + MID_ROWS
@@ -805,35 +828,42 @@
         par, geom, feat, feat_a, feat_b, kept_two[0], *layer[2:], readout_mid, out_row,
     )
     energy = cot_a[LANES:]
-    cot_a, cot_b = sides(cot_a, cot_b, "atom")
-    dgeom, grads_two = call(
-        radial_back_kernel,
+    cot_a = side_one(cot_a, "atom")
+    back_args = (geom, *kept_two, found_two, gacc, *prepared[6:8])
+    sums = (f32(3 * LANES, 2 * LANES), f32(LANES, 2 * basis_count))
+    dgeom_one, dro_first, dri_first = call(
+        functools.partial(radial_back_kernel, 0),
         "radial_two_back",
-        (f32(slots, 8, LANES), f32(G_ROWS, LANES)),
-        [vmem()] * 8 + [layer_spec(radial_in, 1), layer_spec(radial_out, 1)],
+        (f32(ROWS, 8, LANES),) + sums,
+        [vmem()] * 9,
+        [vmem()] * 3,
+        [],
+        3 * 10**9,
+        *back_args,
+    )
+    energy = energy + cot_a[LANES:]
+    moved = swap(energy, "atom", 2)
+    cot_b = side_two(after(cot_b, dri_first), "atom")
+    dgeom_two, grads_two = call(
+        functools.partial(radial_back_kernel, 1),
+        "radial_two_back_last",
+        (f32(ROWS, 8, LANES), f32(G_ROWS, LANES)),
+        [vmem()] * 12,
         [vmem()] * 2,
-        [
-            pltpu.VMEM((2 * basis_count, 2 * LANES), BF16),
-            pltpu.VMEM((2 * LANES, 6 * LANES), BF16),
-            pltpu.VMEM((3 * LANES, 2 * LANES), F32),
-            pltpu.VMEM((LANES, 2 * basis_count), F32),
-        ],
-        5 * 10**9,
-        geom, *kept_two, found_two, gacc, mixed, radial_in, radial_out,
-    )
-    energy = energy + cot_a[LANES:]
-    others = [swap(energy, "atom", k) for k in range(2, min(slabs, 8), 2)]
-    for other in others:
-        energy = energy + other
+        [pltpu.VMEM(x.shape, F32) for x in sums],
+        3 * 10**9,
+        *back_args, dro_first, after(dri_first, energy), mixed,
+    )
+    energy = after(energy + moved, dgeom_two)
+    if slabs > 4:
+        energy = energy + swap(energy, "atom", 4)
     force, force_sent, grads_one = call(
         functools.partial(third_kernel, halo),
         "layer_one_back",
         (f32(16, LANES), f32(16, LANES), f32(G_ROWS, LANES)),
-        [smem()] + [vmem()] * 16 + [layer_spec(x, 0) for x in layer],
+        [smem()] + [vmem()] * 20 + [layer_spec(x, 0) for x in layer[2:]],
         [vmem()] * 3,
         [
-            pltpu.VMEM((2 * basis_count, 2 * LANES), BF16),
-            pltpu.VMEM((2 * LANES, 4 * LANES), BF16),
             pltpu.VMEM((2, 4, LANES, LANES), F32),
             pltpu.VMEM((2 * LANES, 2 * LANES), F32),
             pltpu.VMEM((LANES, 2 * basis_count), F32),
@@ -842,8 +872,8 @@
             pltpu.VMEM((16, LANES), F32),
         ],
         6 * 10**9,
-        par, geom, dgeom, agg, cot, cot_a, cot_b, own, side_a, side_b, mid_tail, *kept_one, embedding,
-        *layer,
+        par, geom, dgeom_one, dgeom_two, agg, node, cot, cot_a, cot_b, own, side_a, side_b, mid_tail, *kept_one,
+        embedding, *prepared[2:4], *layer[2:],
     )
     for bit in bits[2:]:
         energy = energy + swap(energy, "atom", bit)
@@ -875,7 +905,7 @@
     x = jnp.concatenate([y] + [exchange(y, plane_move(k)) for k in (1, 2, 3)])
     other = swap(x, "dp", 1)
     weights = (embedding,) + layer + (readout_mid, out_row)
-    outs = (f32(1, 1), f32(3, atom_count), f32(1, 3, 3)) + tuple(f32(*x.shape) for x in weights)
+    outs = (f32(1, 1), f32(3, atom_count), f32(3, 3)) + tuple(f32(*x.shape) for x in weights)
     result = call(
         functools.partial(final_kernel, halo),
         "final",
@@ -886,7 +916,7 @@
         10**8,
         par, cell, energy, force, force_a, force_b, x, other,
     )
-    return (result[0].reshape(1),) + tuple(result[1:-1]) + (result[-1].reshape(LANES),)
+    return (result[0].reshape(1), result[1], result[2][None]) + tuple(result[3:-1]) + (result[-1].reshape(LANES),)
 
 
 def solution(mesh):

time: 88.7 us -> 85.2 us (0.961)
  starting transfers between devices: 25.8 us -> 23.6 us
  Pallas kernels: 30.1 us -> 28 us
  other arithmetic: 0.63 us -> 2.07 us
    ppermute x5 -> x4, starting transfers between devices: 4.59 us -> 0.55 us  [swap(): lax.ppermute(x, axis, [(i, i ^ bit) for i in range(lax.axis_size(axis))])]
    ppermute x8, starting transfers between devices: 7.23 us -> 9.99 us  [exchange(): return lax.ppermute(x, ('dp', 'atom'), route)]
    pallas_call x7 -> x8, Pallas kernels: 30.1 us -> 28 us  [call(): pl.pallas_call(kernel, grid=(1,), out_shape=outs, in_specs=in_specs, out_...]
    ppermute x6, waiting for transfers between devices: 2.31 us -> 1.31 us  [the longest x3 1.3 us: side_two(): lax.ppermute(x, axis, [(i, (i + 1) % size if i % 2 else (i - 1) % size) f...]
    ppermute x6, starting transfers between devices: 14 us -> 13.1 us  [the longest x3 9.84 us: side_two(): lax.ppermute(x, axis, [(i, (i + 1) % size if i % 2 else (i - 1) % size) f...]
    ppermute x5 -> x4, waiting for transfers between devices: 3.62 us -> 4.36 us  [swap(): lax.ppermute(x, axis, [(i, i ^ bit) for i in range(lax.axis_size(axis))])]
    unnamed x28 -> x26, local copies, waits for them, and re-layouts: 2.64 us -> 2.67 us
  transfers between devices with their start and end apart: 19 -> 18, of which waited for: 11 -> 13; matrix products, arithmetic and copies ran while one was open for 0% -> 0% of each run, Pallas kernels for 18% -> 18%
where the time goes in v4:
time: 85.2 us; the launch traced here: 84.9 us
  Pallas kernels  28 us (33%)
  waiting for transfers between devices  26.9 us (32%)
  starting transfers between devices  23.6 us (28%)
  local copies, waits for them, and re-layouts  2.8 us (3%)
  other arithmetic  2.07 us (2%)
  between operations  1.62 us (2%)
    pallas_call x8, Pallas kernels, call(): pl.pallas_call(kernel, grid=(1,), out_shape=outs, in_specs=in_specs, out_...  28 us
    ppermute x8, waiting for transfers between devices, exchange(): return lax.ppermute(x, ('dp', 'atom'), route)  21.2 us
    ppermute x8, starting transfers between devices, exchange(): return lax.ppermute(x, ('dp', 'atom'), route)  9.99 us
    ppermute x3, starting transfers between devices, side_two(): lax.ppermute(x, axis, [(i, (i + 1) % size if i % 2 else (i - 1) % size) f...  9.84 us
    ppermute x4, waiting for transfers between devices, swap(): lax.ppermute(x, axis, [(i, i ^ bit) for i in range(lax.axis_size(axis))])  4.36 us
    ppermute x3, starting transfers between devices, side_one(): lax.ppermute(x, axis, [(i, i ^ 1) for i in range(lax.axis_size(axis))])  3.26 us
    unnamed x26, local copies, waits for them, and re-layouts  2.67 us
  transfers between devices with their start and end apart: 18, of which 13 were waited for; matrix products, arithmetic and copies ran while one was open for 0% of the time, Pallas kernels for 18%

profile of v4, /device:TPU:0, one launch (start us, length us, event | category | flops | bytes accessed | tf_op | source)
XLA Modules:
  0.0 84.9 jit_solution(11500500443946776794)
XLA Ops:
  0.6 0.7 convert_bitcast_fusion
  1.3 0.1 pad.16.clone
  1.4 0.8 maximum_maximum_fusion.own_ref
  2.1 3.0 %collective-permute-start = (f32[8,128]{1,0:T(8,128)S(1)}, f32[8,128]{1,0:T(8,128)S(1)}, u32[]{:S(2)}, u32[]{:S(2)}) collective-permute-start(f32[8,128]{1,0:T(8,128)S(1)} %maximum_maximum_fusion.own_ref), channel_id=1, source_target_pairs={{0,1},{1,0},{2,3},{3,2},{4,5},{5,4},{6,7},{7,6},{8,9},{9,8},{10,11... | collective-permute-start | bytes 12296 | tf_op jit(solution)/shard_map/ppermute | solution.py:680
  5.1 3.5 %collective-permute-start.1 = (f32[8,128]{1,0:T(8,128)S(1)}, f32[8,128]{1,0:T(8,128)S(1)}, u32[]{:S(2)}, u32[]{:S(2)}) collective-permute-start(f32[8,128]{1,0:T(8,128)S(1)} %maximum_maximum_fusion.own_ref), channel_id=1, source_target_pairs={{0,7},{1,2},{2,1},{3,4},{4,3},{5,6},{6,5},{7,0},{8,15},{9,10},{10,... | collective-permute-start | bytes 12296 | tf_op jit(solution)/shard_map/ppermute | solution.py:685
  8.7 1.0 %copy-done = f32[2,128,384]{2,1,0:T(8,128)S(1)} copy-done((f32[2,128,384]{2,1,0:T(8,128)S(1)}, f32[2,128,384]{2,1,0:T(8,128)}, u32[]{:S(2)}) %copy-start) | copy-done | bytes 393240
  9.6 0.8 copy-done.4
  10.5 0.3 prepare.1
  10.9 0.1 pad_add_fusion.par_ref
  10.9 0.2 copy-done.11
  11.9 4.4 %layer_one.1 = (f32[32,8,128]{2,1,0:T(8,128)S(1)}, f32[4,128,128]{2,1,0:T(8,128)S(1)}, f32[4,128,128]{2,1,0:T(8,128)S(1)}, f32[6,128,128]{2,1,0:T(8,128)S(1)}, f...) custom-call(s32[4]{0:T(128)S(1)} %pad_add_fusion.par_ref, ...), custom_call_target="tpu_custom_call" | custom-call | flops 3000000000 | bytes 6000000 | tf_op jit(solution)/shard_map/layer_one/pallas_call | solution.py:718
  16.4 0.1 collective-permute-start.2
  16.4 3.2 %collective-permute-start.3 = (f32[128,128]{1,0:T(8,128)S(1)}, f32[128,128]{1,0:T(8,128)S(1)}, u32[]{:S(2)}, u32[]{:S(2)}) collective-permute-start(f32[128,128]{1,0:T(8,128)S(1)} %get-tuple-element.68), channel_id=1, source_target_pairs={{0,7},{1,2},{2,1},{3,4},{4,3},{5,6},{6,5},{7,0},{8,15},{9,10},{10,... | collective-permute-start | bytes 196616 | tf_op jit(solution)/shard_map/ppermute | solution.py:685
  19.6 2.7 %radial_two.1 = (f32[2,384,2048]{2,1,0:T(8,128)S(1)}, bf16[2,256,2048]{2,1,0:T(8,128)(2,1)S(1)}, bf16[2,128,2048]{2,1,0:T(8,128)(2,1)S(1)}, f32[2,128,2048]{2,1,0:T(8,128)S(1)}) custom-call(f32[32,8,128]{2,1,0:T(8,128)S(1)} %get-tuple-element.65.geom_ref, bf16[128,256]{1,0:T(8,128)(2,1)S(1)} %get-tuple-element.69.ri4, bf16[384,384]{1,0:T(8,128)(2,1)S(1)} %get-tuple-element.70.ro3), custom_call_target="tpu_custom_call" | custom-call | flops 3000000000 | bytes 6000000 | tf_op jit(solution)/shard_map/radial_two/pallas_call | solution.py:718
  22.4 1.1 %collective-permute-done.3.b_ref = f32[128,128]{1,0:T(8,128)S(1)} collective-permute-done((f32[128,128]{1,0:T(8,128)S(1)}, f32[128,128]{1,0:T(8,128)S(1)}, u32[]{:S(2)}, u32[]{:S(2)}) %collective-permute-start.3) | collective-permute-done | bytes 65568 | tf_op jit(solution)/shard_map/ppermute | solution.py:685
  23.5 6.8 %layer_two.1 = (f32[4,128,128]{2,1,0:T(8,128)S(1)}, f32[136,128]{1,0:T(8,128)S(1)}, f32[128,128]{1,0:T(8,128)S(1)}, f32[480,128]{1,0:T(8,128)S(1)}, f32[40,128]{...) custom-call(s32[4]{0:T(128)S(1)} %pad_add_fusion.par_ref, ...), custom_call_target="tpu_custom_call" | custom-call | flops 5000000000 | bytes 10000000 | tf_op jit(solution)/shard_map/layer_two/pallas_call | solution.py:718
  30.3 0.2 collective-permute-start.4
  30.5 2.6 %radial_two_back.1 = (f32[16,8,128]{2,1,0:T(8,128)S(1)}, f32[384,256]{1,0:T(8,128)S(1)}, f32[128,128]{1,0:T(8,128)S(1)}) custom-call(f32[32,8,128]{2,1,0:T(8,128)S(1)} %get-tuple-element.65.geom_ref, f32[2,384,2048]{2,1,0:T(8,128)S(1)} %get-tuple-element.71.filters_ref, bf16[2,256,2048]{2,1,0:T(8,128)(2,1)S(1)} %get-tuple-element.73.hidden_ref, ...), custom_call_target="tpu_custom_call" | custom-call | flops 3000000000 | bytes 6000000 | tf_op jit(solution)/shard_map/radial_two_back/pallas_call | solution.py:718
  33.1 3.1 %collective-permute-start.7 = (f32[128,128]{1,0:T(8,128)S(1)}, f32[128,128]{1,0:T(8,128)S(1)}, u32[]{:S(2)}, u32[]{:S(2)}) collective-permute-start(f32[128,128]{1,0:T(8,128)S(1)} %get-tuple-element.91), channel_id=1, source_target_pairs={{0,7},{1,2},{2,1},{3,4},{4,3},{5,6},{6,5},{7,0},{8,15},{9,10},{10,... | collective-permute-start | bytes 196616 | tf_op jit(solution)/shard_map/ppermute | solution.py:685
  36.2 0.2 collective-permute-start.5
  36.5 2.6 %radial_two_back_last.1 = (f32[16,8,128]{2,1,0:T(8,128)S(1)}, f32[928,128]{1,0:T(8,128)S(1)}) custom-call(f32[32,8,128]{2,1,0:T(8,128)S(1)} %get-tuple-element.65.geom_ref, f32[2,384,2048]{2,1,0:T(8,128)S(1)} %get-tuple-element.71.filters_ref, bf16[2,256,2048]{2,1,0:T(8,128)(2,1)S(1)} %get-tuple-element.73.hidden_ref, ...), custom_call_target="tpu_custom_call" | custom-call | flops 3000000000 | bytes 6000000 | tf_op jit(solution)/shard_map/radial_two_back_last/pallas_call | solution.py:718
  39.1 0.7 collective-permute-done.5
  39.8 0.2 collective-permute-start.6
  40.0 0.2 collective-permute-done.7.b_ref
  40.2 6.8 %layer_one_back.1 = (f32[16,128]{1,0:T(8,128)S(1)}, f32[16,128]{1,0:T(8,128)S(1)}, f32[928,128]{1,0:T(8,128)S(1)}) custom-call(s32[4]{0:T(128)S(1)} %pad_add_fusion.par_ref, f32[32,8,128]{2,1,0:T(8,128)S(1)} %get-tuple-element.65.geom_ref, f32[16,8,128]{2,1,0:T(8,128)S(1)} %get-tuple-element.86.dgeom_one, f32[16,8,128]{2,1,0:T(8,128)S(1)} %get-tuple-element.84.dgeom_two, ...), custom_call_target="tpu_custom_call" | custom-call | flops 6000000000 | bytes 12000000 | tf_op jit(solution)/shard_map/layer_one_back/pallas_call | solution.py:718
  47.1 0.2 multiply_select_fusion
  47.3 0.1 collective-permute-start.8
  47.4 1.8 %collective-permute-done.8 = f32[928,128]{1,0:T(8,128)S(1)} collective-permute-done((f32[928,128]{1,0:T(8,128)S(1)}, f32[928,128]{1,0:T(8,128)S(1)}, u32[]{:S(2)}, u32[]{:S(2)}) %collective-permute-start.8) | collective-permute-done | bytes 475168 | tf_op jit(solution)/shard_map/ppermute | solution.py:693
  49.2 0.2 select_add_fusion
  49.4 2.2 %collective-permute-start.9 = (f32[248,128]{1,0:T(8,128)S(1)}, f32[248,128]{1,0:T(8,128)S(1)}, u32[]{:S(2)}, u32[]{:S(2)}) collective-permute-start(f32[248,128]{1,0:T(8,128)S(1)} %pad_maximum_fusion.1), channel_id=1, source_target_pairs={{0,1},{1,0},{2,3},{3,2},{4,5},{5,4},{6,7},{7,6},{8,9},{9,8},{10,11... | collective-permute-start | bytes 380936 | tf_op jit(solution)/shard_map/ppermute | solution.py:738
  51.6 1.5 %collective-permute-start.10 = (f32[232,128]{1,0:T(8,128)S(1)}, f32[232,128]{1,0:T(8,128)S(1)}, u32[]{:S(2)}, u32[]{:S(2)}) collective-permute-start(f32[232,128]{1,0:T(8,128)S(1)} %get-tuple-element.126), channel_id=1, source_target_pairs={{0,16},{1,17},{2,18},{3,19},{4,20},{5,21},{6,22},{7,23},{8,24},{9,... | collective-permute-start | bytes 356360 | tf_op jit(solution)/shard_map/ppermute | solution.py:738
  53.2 2.2 %collective-permute-done.9 = f32[248,128]{1,0:T(8,128)S(1)} collective-permute-done((f32[248,128]{1,0:T(8,128)S(1)}, f32[248,128]{1,0:T(8,128)S(1)}, u32[]{:S(2)}, u32[]{:S(2)}) %collective-permute-start.9) | collective-permute-done | bytes 127008 | tf_op jit(solution)/shard_map/ppermute | solution.py:738
  55.3 2.4 %collective-permute-done.10 = f32[232,128]{1,0:T(8,128)S(1)} collective-permute-done((f32[232,128]{1,0:T(8,128)S(1)}, f32[232,128]{1,0:T(8,128)S(1)}, u32[]{:S(2)}, u32[]{:S(2)}) %collective-permute-start.10) | collective-permute-done | bytes 118816 | tf_op jit(solution)/shard_map/ppermute | solution.py:738
  57.7 1.2 %collective-permute-done.11 = f32[232,128]{1,0:T(8,128)S(1)} collective-permute-done((f32[232,128]{1,0:T(8,128)S(1)}, f32[232,128]{1,0:T(8,128)S(1)}, u32[]{:S(2)}, u32[]{:S(2)}) %collective-permute-start.11) | collective-permute-done | bytes 118816 | tf_op jit(solution)/shard_map/ppermute | solution.py:738
  59.0 1.2 %collective-permute-start.12 = (f32[240,128]{1,0:T(8,128)S(1)}, f32[240,128]{1,0:T(8,128)S(1)}, u32[]{:S(2)}, u32[]{:S(2)}) collective-permute-start(f32[240,128]{1,0:T(8,128)S(1)} %pad_maximum_fusion.3), channel_id=1, source_target_pairs={{0,2},{1,3},{2,0},{3,1},{4,6},{5,7},{6,4},{7,5},{8,12},{9,13},{10,... | collective-permute-start | bytes 368648 | tf_op jit(solution)/shard_map/ppermute | solution.py:738
  60.2 4.4 %collective-permute-done.12 = f32[240,128]{1,0:T(8,128)S(1)} collective-permute-done((f32[240,128]{1,0:T(8,128)S(1)}, f32[240,128]{1,0:T(8,128)S(1)}, u32[]{:S(2)}, u32[]{:S(2)}) %collective-permute-start.12) | collective-permute-done | bytes 122912 | tf_op jit(solution)/shard_map/ppermute | solution.py:738
  64.7 1.5 %collective-permute-start.13 = (f32[248,128]{1,0:T(8,128)S(1)}, f32[248,128]{1,0:T(8,128)S(1)}, u32[]{:S(2)}, u32[]{:S(2)}) collective-permute-start(f32[248,128]{1,0:T(8,128)S(1)} %pad_maximum_fusion.2), channel_id=1, source_target_pairs={{0,4},{1,5},{2,6},{3,7},{4,0},{5,1},{6,2},{7,3},{8,10},{9,11},{10,... | collective-permute-start | bytes 380936 | tf_op jit(solution)/shard_map/ppermute | solution.py:738
  66.2 5.7 %collective-permute-done.13 = f32[248,128]{1,0:T(8,128)S(1)} collective-permute-done((f32[248,128]{1,0:T(8,128)S(1)}, f32[248,128]{1,0:T(8,128)S(1)}, u32[]{:S(2)}, u32[]{:S(2)}) %collective-permute-start.13) | collective-permute-done | bytes 127008 | tf_op jit(solution)/shard_map/ppermute | solution.py:738
  71.9 1.6 %collective-permute-start.14 = (f32[232,128]{1,0:T(8,128)S(1)}, f32[232,128]{1,0:T(8,128)S(1)}, u32[]{:S(2)}, u32[]{:S(2)}) collective-permute-start(f32[232,128]{1,0:T(8,128)S(1)} %slice_add_fusion), channel_id=1, source_target_pairs={{0,1},{1,0},{2,3},{3,2},{4,5},{5,4},{6,7},{7,6},{8,9},{9,8},{10,11... | collective-permute-start | bytes 356360 | tf_op jit(solution)/shard_map/ppermute | solution.py:738
  73.5 1.5 %collective-permute-start.15 = (f32[232,128]{1,0:T(8,128)S(1)}, f32[232,128]{1,0:T(8,128)S(1)}, u32[]{:S(2)}, u32[]{:S(2)}) collective-permute-start(f32[232,128]{1,0:T(8,128)S(1)} %slice_add_fusion), channel_id=1, source_target_pairs={{0,16},{1,17},{2,18},{3,19},{4,20},{5,21},{6,22},{7,23},{8,24},{9,... | collective-permute-start | bytes 356360 | tf_op jit(solution)/shard_map/ppermute | solution.py:738
  75.0 0.5 collective-permute-start.16
  75.5 1.3 %collective-permute-done.14 = f32[232,128]{1,0:T(8,128)S(1)} collective-permute-done((f32[232,128]{1,0:T(8,128)S(1)}, f32[232,128]{1,0:T(8,128)S(1)}, u32[]{:S(2)}, u32[]{:S(2)}) %collective-permute-start.14) | collective-permute-done | bytes 118816 | tf_op jit(solution)/shard_map/ppermute | solution.py:738
  76.8 1.5 %collective-permute-done.15 = f32[232,128]{1,0:T(8,128)S(1)} collective-permute-done((f32[232,128]{1,0:T(8,128)S(1)}, f32[232,128]{1,0:T(8,128)S(1)}, u32[]{:S(2)}, u32[]{:S(2)}) %collective-permute-start.15) | collective-permute-done | bytes 118816 | tf_op jit(solution)/shard_map/ppermute | solution.py:738
  78.4 2.4 %collective-permute-done.16 = f32[232,128]{1,0:T(8,128)S(1)} collective-permute-done((f32[232,128]{1,0:T(8,128)S(1)}, f32[232,128]{1,0:T(8,128)S(1)}, u32[]{:S(2)}, u32[]{:S(2)}) %collective-permute-start.16) | collective-permute-done | bytes 118816 | tf_op jit(solution)/shard_map/ppermute | solution.py:738
  80.8 0.1 collective-permute-start.17
  80.9 1.8 %collective-permute-done.17.other_turned = f32[928,128]{1,0:T(8,128)S(1)} collective-permute-done((f32[928,128]{1,0:T(8,128)S(1)}, f32[928,128]{1,0:T(8,128)S(1)}, u32[]{:S(2)}, u32[]{:S(2)}) %collective-permute-start.17) | collective-permute-done | bytes 475168 | tf_op jit(solution)/shard_map/ppermute | solution.py:693
  82.7 1.7 %final.1 = (f32[1,1]{1,0:T(1,128)}, f32[3,128]{1,0:T(4,128)}, f32[3,3]{1,0:T(4,128)S(1)}, f32[96,128]{1,0:T(8,128)}, f32[2,64,128]{2,1,0:T(8,128)}, /*index=5*/f...) custom-call(s32[4]{0:T(128)S(1)} %pad_add_fusion.par_ref, ...), custom_call_target="tpu_custom_call" | custom-call | flops 100000000 | bytes 200000 | tf_op jit(solution)/shard_map/final/pallas_call | solution.py:718
  84.4 0.6 copy.28
  (46 shorter events, 0.3 us)
Async XLA Ops:
  2.1 9.7 %collective-permute-start = (f32[8,128]{1,0:T(8,128)S(1)}, f32[8,128]{1,0:T(8,128)S(1)}, u32[]{:S(2)}, u32[]{:S(2)}) collective-permute-start(f32[8,128]{1,0:T(8,128)S(1)} %maximum_maximum_fusion.own_ref), channel_id=1, source_target_pairs={{0,1},{1,0},{2,3},{3,2},{4,5},{5,4},{6,7},{7,6},{8,9},{9,8},{10,11... | collective-permute-start | bytes 12296 | tf_op jit(solution)/shard_map/ppermute | solution.py:680
  5.1 6.7 %collective-permute-start.1 = (f32[8,128]{1,0:T(8,128)S(1)}, f32[8,128]{1,0:T(8,128)S(1)}, u32[]{:S(2)}, u32[]{:S(2)}) collective-permute-start(f32[8,128]{1,0:T(8,128)S(1)} %maximum_maximum_fusion.own_ref), channel_id=1, source_target_pairs={{0,7},{1,2},{2,1},{3,4},{4,3},{5,6},{6,5},{7,0},{8,15},{9,10},{10,... | collective-permute-start | bytes 12296 | tf_op jit(solution)/shard_map/ppermute | solution.py:685
  8.7 1.0 %copy-start = (f32[2,128,384]{2,1,0:T(8,128)S(1)}, f32[2,128,384]{2,1,0:T(8,128)}, u32[]{:S(2)}) copy-start(f32[2,128,384]{2,1,0:T(8,128)} %rout_ref.1) | copy-start | bytes 1179652
  9.6 0.8 copy-start.4
  10.5 0.7 copy-start.11
  10.5 1.4 %copy-start.1 = (f32[2,128,128]{2,1,0:T(8,128)S(1)}, f32[2,128,128]{2,1,0:T(8,128)}, u32[]{:S(2)}) copy-start(f32[2,128,128]{2,1,0:T(8,128)} %sm_ref.5) | copy-start | bytes 393220
  10.5 1.4 %copy-start.2 = (f32[2,128,128]{2,1,0:T(8,128)S(1)}, f32[2,128,128]{2,1,0:T(8,128)}, u32[]{:S(2)}) copy-start(f32[2,128,128]{2,1,0:T(8,128)} %vm_ref.5) | copy-start | bytes 393220
  10.5 1.4 %copy-start.3 = (f32[2,128,128]{2,1,0:T(8,128)S(1)}, f32[2,128,128]{2,1,0:T(8,128)}, u32[]{:S(2)}) copy-start(f32[2,128,128]{2,1,0:T(8,128)} %vg_ref.5) | copy-start | bytes 393220
  10.5 1.4 %copy-start.6 = (s32[3,32,128]{2,1,0:T(8,128)S(1)}, s32[3,32,128]{2,1,0:T(8,128)}, u32[]{:S(2)}) copy-start(s32[3,32,128]{2,1,0:T(8,128)} %shift_ref.1) | copy-start | bytes 147460
  10.5 1.4 %copy-start.7 = (f32[96,128]{1,0:T(8,128)S(1)}, f32[96,128]{1,0:T(8,128)}, u32[]{:S(2)}) copy-start(f32[96,128]{1,0:T(8,128)} %emb_ref.3) | copy-start | bytes 147460
  10.5 1.4 %copy-start.8 = (s32[32,128]{1,0:T(8,128)S(1)}, s32[32,128]{1,0:T(8,128)}, u32[]{:S(2)}) copy-start(s32[32,128]{1,0:T(8,128)} %nb_ref.1) | copy-start | bytes 49156
  10.5 1.4 %copy-start.9 = (s32[128]{0:T(128)S(1)}, s32[128]{0:T(128)}, u32[]{:S(2)}) copy-start(s32[128]{0:T(128)} %param.18) | copy-start | bytes 1540
  16.4 6.0 %collective-permute-start.2 = (f32[128,128]{1,0:T(8,128)S(1)}, f32[128,128]{1,0:T(8,128)S(1)}, u32[]{:S(2)}, u32[]{:S(2)}) collective-permute-start(f32[128,128]{1,0:T(8,128)S(1)} %get-tuple-element.67), channel_id=1, source_target_pairs={{0,1},{1,0},{2,3},{3,2},{4,5},{5,4},{6,7},{7,6},{8,9},{9,8},{10,11... | collective-permute-start | bytes 196616 | tf_op jit(solution)/shard_map/ppermute | solution.py:680
  16.4 7.0 %collective-permute-start.3 = (f32[128,128]{1,0:T(8,128)S(1)}, f32[128,128]{1,0:T(8,128)S(1)}, u32[]{:S(2)}, u32[]{:S(2)}) collective-permute-start(f32[128,128]{1,0:T(8,128)S(1)} %get-tuple-element.68), channel_id=1, source_target_pairs={{0,7},{1,2},{2,1},{3,4},{4,3},{5,6},{6,5},{7,0},{8,15},{9,10},{10,... | collective-permute-start | bytes 196616 | tf_op jit(solution)/shard_map/ppermute | solution.py:685
  19.6 3.9 %copy-start.5 = (f32[128,128]{1,0:T(8,128)S(1)}, f32[128,128]{1,0:T(8,128)}, u32[]{:S(2)}) copy-start(f32[128,128]{1,0:T(8,128)} %mid_ref.1) | copy-start | bytes 196612
  19.6 3.9 %copy-start.10 = (f32[128]{0:T(128)S(1)}, f32[128]{0:T(128)}, u32[]{:S(2)}) copy-start(f32[128]{0:T(128)} %param.29) | copy-start | bytes 1540
  30.3 5.9 %collective-permute-start.4 = (f32[136,128]{1,0:T(8,128)S(1)}, f32[136,128]{1,0:T(8,128)S(1)}, u32[]{:S(2)}, u32[]{:S(2)}) collective-permute-start(f32[136,128]{1,0:T(8,128)S(1)} %get-tuple-element.72), channel_id=1, source_target_pairs={{0,1},{1,0},{2,3},{3,2},{4,5},{5,4},{6,7},{7,6},{8,9},{9,8},{10,11... | collective-permute-start | bytes 208904 | tf_op jit(solution)/shard_map/ppermute | solution.py:680
  33.1 7.1 %collective-permute-start.7 = (f32[128,128]{1,0:T(8,128)S(1)}, f32[128,128]{1,0:T(8,128)S(1)}, u32[]{:S(2)}, u32[]{:S(2)}) collective-permute-start(f32[128,128]{1,0:T(8,128)S(1)} %get-tuple-element.91), channel_id=1, source_target_pairs={{0,7},{1,2},{2,1},{3,4},{4,3},{5,6},{6,5},{7,0},{8,15},{9,10},{10,... | collective-permute-start | bytes 196616 | tf_op jit(solution)/shard_map/ppermute | solution.py:685
  36.2 3.6 %collective-permute-start.5 = (f32[8,128]{1,0:T(8,128)S(1)}, f32[8,128]{1,0:T(8,128)S(1)}, u32[]{:S(2)}, u32[]{:S(2)}) collective-permute-start(f32[8,128]{1,0:T(8,128)S(1)} %slice_add_fusion.3), channel_id=1, source_target_pairs={{0,2},{1,3},{2,0},{3,1},{4,6},{5,7},{6,4},{7,5},{8,10},{9,11},{10,... | collective-permute-start | bytes 12296 | tf_op jit(solution)/shard_map/ppermute | solution.py:693
  39.8 7.2 %collective-permute-start.6 = (f32[8,128]{1,0:T(8,128)S(1)}, f32[8,128]{1,0:T(8,128)S(1)}, u32[]{:S(2)}, u32[]{:S(2)}) collective-permute-start(f32[8,128]{1,0:T(8,128)S(1)} %add.73), channel_id=1, source_target_pairs={{0,4},{1,5},{2,6},{3,7},{4,0},{5,1},{6,2},{7,3},{8,12},{9,13},{10,... | collective-permute-start | bytes 12296 | tf_op jit(solution)/shard_map/ppermute | solution.py:693
  47.3 1.9 %collective-permute-start.8 = (f32[928,128]{1,0:T(8,128)S(1)}, f32[928,128]{1,0:T(8,128)S(1)}, u32[]{:S(2)}, u32[]{:S(2)}) collective-permute-start(f32[928,128]{1,0:T(8,128)S(1)} %multiply_select_fusion), channel_id=1, source_target_pairs={{0,8},{8,0},{16,24},{24,16},{1,9},{9,1},{17,25},{25,17},{2,10},{10... | collective-permute-start | bytes 1425416 | tf_op jit(solution)/shard_map/ppermute | solution.py:693
  49.4 5.9 %collective-permute-start.9 = (f32[248,128]{1,0:T(8,128)S(1)}, f32[248,128]{1,0:T(8,128)S(1)}, u32[]{:S(2)}, u32[]{:S(2)}) collective-permute-start(f32[248,128]{1,0:T(8,128)S(1)} %pad_maximum_fusion.1), channel_id=1, source_target_pairs={{0,1},{1,0},{2,3},{3,2},{4,5},{5,4},{6,7},{7,6},{8,9},{9,8},{10,11... | collective-permute-start | bytes 380936 | tf_op jit(solution)/shard_map/ppermute | solution.py:738
  51.6 6.1 %collective-permute-start.10 = (f32[232,128]{1,0:T(8,128)S(1)}, f32[232,128]{1,0:T(8,128)S(1)}, u32[]{:S(2)}, u32[]{:S(2)}) collective-permute-start(f32[232,128]{1,0:T(8,128)S(1)} %get-tuple-element.126), channel_id=1, source_target_pairs={{0,16},{1,17},{2,18},{3,19},{4,20},{5,21},{6,22},{7,23},{8,24},{9,... | collective-permute-start | bytes 356360 | tf_op jit(solution)/shard_map/ppermute | solution.py:738
  53.1 5.9 %collective-permute-start.11 = (f32[232,128]{1,0:T(8,128)S(1)}, f32[232,128]{1,0:T(8,128)S(1)}, u32[]{:S(2)}, u32[]{:S(2)}) collective-permute-start(f32[232,128]{1,0:T(8,128)S(1)} %get-tuple-element.127), channel_id=1, source_target_pairs={{0,17},{1,16},{2,19},{3,18},{4,21},{5,20},{6,23},{7,22},{8,25},{9,... | collective-permute-start | bytes 356360 | tf_op jit(solution)/shard_map/ppermute | solution.py:738
  59.0 5.6 %collective-permute-start.12 = (f32[240,128]{1,0:T(8,128)S(1)}, f32[240,128]{1,0:T(8,128)S(1)}, u32[]{:S(2)}, u32[]{:S(2)}) collective-permute-start(f32[240,128]{1,0:T(8,128)S(1)} %pad_maximum_fusion.3), channel_id=1, source_target_pairs={{0,2},{1,3},{2,0},{3,1},{4,6},{5,7},{6,4},{7,5},{8,12},{9,13},{10,... | collective-permute-start | bytes 368648 | tf_op jit(solution)/shard_map/ppermute | solution.py:738
  64.7 7.2 %collective-permute-start.13 = (f32[248,128]{1,0:T(8,128)S(1)}, f32[248,128]{1,0:T(8,128)S(1)}, u32[]{:S(2)}, u32[]{:S(2)}) collective-permute-start(f32[248,128]{1,0:T(8,128)S(1)} %pad_maximum_fusion.2), channel_id=1, source_target_pairs={{0,4},{1,5},{2,6},{3,7},{4,0},{5,1},{6,2},{7,3},{8,10},{9,11},{10,... | collective-permute-start | bytes 380936 | tf_op jit(solution)/shard_map/ppermute | solution.py:738
  71.9 4.9 %collective-permute-start.14 = (f32[232,128]{1,0:T(8,128)S(1)}, f32[232,128]{1,0:T(8,128)S(1)}, u32[]{:S(2)}, u32[]{:S(2)}) collective-permute-start(f32[232,128]{1,0:T(8,128)S(1)} %slice_add_fusion), channel_id=1, source_target_pairs={{0,1},{1,0},{2,3},{3,2},{4,5},{5,4},{6,7},{7,6},{8,9},{9,8},{10,11... | collective-permute-start | bytes 356360 | tf_op jit(solution)/shard_map/ppermute | solution.py:738
  73.5 4.8 %collective-permute-start.15 = (f32[232,128]{1,0:T(8,128)S(1)}, f32[232,128]{1,0:T(8,128)S(1)}, u32[]{:S(2)}, u32[]{:S(2)}) collective-permute-start(f32[232,128]{1,0:T(8,128)S(1)} %slice_add_fusion), channel_id=1, source_target_pairs={{0,16},{1,17},{2,18},{3,19},{4,20},{5,21},{6,22},{7,23},{8,24},{9,... | collective-permute-start | bytes 356360 | tf_op jit(solution)/shard_map/ppermute | solution.py:738
  75.0 5.7 %collective-permute-start.16 = (f32[232,128]{1,0:T(8,128)S(1)}, f32[232,128]{1,0:T(8,128)S(1)}, u32[]{:S(2)}, u32[]{:S(2)}) collective-permute-start(f32[232,128]{1,0:T(8,128)S(1)} %slice_add_fusion), channel_id=1, source_target_pairs={{0,17},{1,16},{2,19},{3,18},{4,21},{5,20},{6,23},{7,22},{8,25},{9,... | collective-permute-start | bytes 356360 | tf_op jit(solution)/shard_map/ppermute | solution.py:738
  80.8 1.9 %collective-permute-start.17 = (f32[928,128]{1,0:T(8,128)S(1)}, f32[928,128]{1,0:T(8,128)S(1)}, u32[]{:S(2)}, u32[]{:S(2)}) collective-permute-start(f32[928,128]{1,0:T(8,128)S(1)} %pad_maximum_fusion.mine_turned), channel_id=1, source_target_pairs={{0,8},{8,0},{16,24},{24,16},{1,9},{9,1},{17,25},{25,17},{2,10},{10... | collective-permute-start | bytes 1425416 | tf_op jit(solution)/shard_map/ppermute | solution.py:693

commit v5 on v4

--- a/solution.py
+++ b/solution.py
@@ -13,8 +13,8 @@
 HALF = 64
 ROWS = 16
 VMEM_LIMIT = 20 * 1024 * 1024
-G_ROWS = 928
-MID_ROWS = 88
+G_ROWS = 896
+MID_ROWS = 56
 
 
 def split(x):
@@ -274,7 +274,11 @@
         d_dirs.append([jnp.sum(push * gv[c], axis=0, keepdims=True) for c in range(3)])
     fh, fl = split(jnp.concatenate(d_filters, axis=1))
     both = hidden_ref[t]
-    dro[...] += mm_nt(jnp.concatenate([fh, fl], axis=1), jnp.concatenate([both, both], axis=1))
+    if vectors:
+        dro[...] += mm_nt(jnp.concatenate([fh, fl], axis=1), jnp.concatenate([both, both], axis=1))
+    else:
+        pair = mm_nt(both, fh)
+        dro[...] += pair[:LANES] + pair[LANES:] + mm_nt(both[:LANES], fl)
     spread = mm(rob[...], jnp.concatenate([fh, fl], axis=0))
     d_pre = (spread[:LANES] + spread[LANES:]) * slope_ref[t]
     ph, plo = split(d_pre)
@@ -288,14 +292,14 @@
     return d_dirs, [d_dist[:, q * LANES : (q + 1) * LANES] for q in range(len(rows))]
 
 
-def radial_grads(dro, dri, out, row_in, row_out, basis_count, groups):
+def radial_grads(dro, dri, out, row_in, row_out, basis_count, groups, turned):
     both = dri[...]
-    turned = both + pltpu.roll(both, HALF, 1)
-    out[row_in : row_in + basis_count] = turned.T[0:basis_count]
+    turned_in = both + pltpu.roll(both, HALF, 1)
+    out[row_in : row_in + basis_count] = turned_in.T[0:basis_count]
     for place in range(groups):
-        rows = slice(place * LANES, (place + 1) * LANES)
-        grad = dro[rows, 0:LANES] + dro[rows, LANES:]
-        out[row_out + place * LANES : row_out + (place + 1) * LANES] = grad.T
+        block = slice(place * LANES, (place + 1) * LANES)
+        grad = (dro[block, 0:LANES] + dro[block, LANES:]).T if turned else dro[:, block]
+        out[row_out + place * LANES : row_out + (place + 1) * LANES] = grad
 
 
 def species_hot(row, count):
@@ -506,7 +510,7 @@
             dgeom_ref[q, c : c + 1, :] = d_dirs[q][c]
         dgeom_ref[q, 3:4, :] = d_dists[q]
     if last:
-        radial_grads(dro, dri, grad_ref, 0, basis_count, basis_count, 3)
+        radial_grads(dro, dri, grad_ref, 0, basis_count, basis_count, 3, True)
         grad_ref[basis_count + 3 * LANES :] = mixed_ref[...]
 
 
@@ -530,7 +534,6 @@
         )
     place_up, place_down = from_sides(par_ref, pa_ref, pb_ref)
     hot_own, hot_beside = species_tables(own_ref, place_up, place_down, emb_ref, halo)
-    groups = (0, 2)
     count = emb_ref.shape[0]
 
     @pl.when(par_ref[0] >= 0)
@@ -595,12 +598,15 @@
         grad = grad + (mm_nt(hot, hi) + mm_nt(hot, lo))
     grad_ref[0:count] = grad
     row = count
-    radial_grads(dro, dri, grad_ref, row, row + basis_count, basis_count, len(groups))
+    radial_grads(dro, dri, grad_ref, row, row + basis_count, basis_count, 2, False)
     row += basis_count + 5 * LANES
     grad_ref[row:] = jnp.zeros((grad_ref.shape[0] - row, LANES), F32)
-    grad_ref[row + 64 : row + 64 + mid_tail.shape[0]] = mid_tail[...]
+    grad_ref[row + 8 : row + 8 + mid_tail.shape[0]] = mid_tail[...]
+    sublane = lax.broadcasted_iota(jnp.int32, (16, LANES), 0)
     total = jnp.broadcast_to(jnp.sum(virial[...], axis=1, keepdims=True), virial.shape)
-    grad_ref[pl.ds(pl.multiple_of(row + 16 * par_ref[1], 16), 16)] = total
+    nine = jnp.sum(jnp.where(lane_ids(16) == sublane, total, 0.0), axis=0, keepdims=True)
+    mine = (sublane[:8] - par_ref[1]) == 0
+    grad_ref[row : row + 8] = jnp.where(mine, nine, 0.0)
     lane16 = lane_ids(16)
     first, second = dtab[0, LANES:], dtab[1, LANES:]
     force_ref[...] = (
@@ -657,15 +663,13 @@
             line += LANES
         out_ref[...] = two[line : line + 1]
         mid_ref[0:MID_ROWS] = two[line + 8 : line + 8 + MID_ROWS]
-        mid_ref[MID_ROWS:] = one[row + 64 : row + 64 + LANES - MID_ROWS]
-        virial = one[pl.ds(pl.multiple_of(row + 16 * par_ref[1], 16), 16)]
-        place = lane_ids(1)
-        lines = [
-            jnp.where(place == 0, virial[3 * a : 3 * a + 1], jnp.where(place == 1, virial[3 * a + 1 : 3 * a + 2], virial[3 * a + 2 : 3 * a + 3]))
-            for a in range(3)
-        ]
-        stress = jnp.concatenate(lines, axis=0) / (jnp.zeros((3, LANES), F32) + det)
-        stress_ref[...] = stress[:, 0:3]
+        mid_ref[MID_ROWS:] = one[row + 8 : row + 8 + LANES - MID_ROWS]
+        wanted = (lax.broadcasted_iota(jnp.int32, (8, LANES), 0) - par_ref[1]) == 0
+        nine = jnp.sum(jnp.where(wanted, one[row : row + 8], 0.0), axis=0, keepdims=True)
+        stress = jnp.broadcast_to(nine, (8, LANES)) / (jnp.zeros((8, LANES), F32) + det)
+        lines = [stress] + [pltpu.roll(stress, LANES - 3 * a, 1) for a in (1, 2)]
+        for a in range(3):
+            stress_ref[a] = lines[a][0:1, 0:3]
 
     @pl.when(par_ref[1] % 2 == 0)
     def _():
@@ -749,7 +753,8 @@
     me = lax.axis_index("atom")
     group = lax.axis_index("dp")
     counts_row, out_row = counts[None], readout_out[None]
-    own = jnp.concatenate([frac, species.astype(F32)[None], jnp.zeros((4, atom_count), F32)], axis=0)
+    own_row = lax.broadcasted_iota(jnp.int32, (8, 1), 0)
+    own = jnp.pad(frac, ((0, 5), (0, 0))) + jnp.where(own_row == 3, species[None], 0).astype(F32)
     side_a, side_b = side_one(own, "atom"), side_two(own, "atom")
     plane = group // 2 * 2 + me % 2
     slabs = lax.axis_size("atom")
@@ -865,7 +870,7 @@
         [vmem()] * 3,
         [
             pltpu.VMEM((2, 4, LANES, LANES), F32),
-            pltpu.VMEM((2 * LANES, 2 * LANES), F32),
+            pltpu.VMEM((LANES, 2 * LANES), F32),
             pltpu.VMEM((LANES, 2 * basis_count), F32),
             pltpu.VMEM((2, LANES + 16, LANES), F32),
             pltpu.VMEM((2, 16, LANES), F32),
@@ -881,7 +886,7 @@
     loss_scale = 2.0 * (energy[0:1] / cell_atoms - energy_ref[0]) / cell_atoms
     virial_row = embedding.shape[0] + basis_count + 5 * LANES
     line = lax.broadcasted_iota(jnp.int32, (G_ROWS, 1), 0)
-    one = grads_one * jnp.where((line >= virial_row) & (line < virial_row + 64), 1.0, loss_scale)
+    one = grads_one * jnp.where((line >= virial_row) & (line < virial_row + 8), 1.0, loss_scale)
     two = grads_two * loss_scale
     core = group % 2 == 1
     x = jnp.where(core, one, two) + swap(jnp.where(core, two, one), "dp", 1)
@@ -905,7 +910,7 @@
     x = jnp.concatenate([y] + [exchange(y, plane_move(k)) for k in (1, 2, 3)])
     other = swap(x, "dp", 1)
     weights = (embedding,) + layer + (readout_mid, out_row)
-    outs = (f32(1, 1), f32(3, atom_count), f32(3, 3)) + tuple(f32(*x.shape) for x in weights)
+    outs = (f32(1, 1), f32(3, atom_count), f32(3, 1, 3)) + tuple(f32(*x.shape) for x in weights)
     result = call(
         functools.partial(final_kernel, halo),
         "final",
@@ -916,7 +921,7 @@
         10**8,
         par, cell, energy, force, force_a, force_b, x, other,
     )
-    return (result[0].reshape(1), result[1], result[2][None]) + tuple(result[3:-1]) + (result[-1].reshape(LANES),)
+    return (result[0].reshape(1), result[1], result[2].transpose(1, 0, 2)) + tuple(result[3:-1]) + (result[-1].reshape(LANES),)
 
 
 def solution(mesh):

time: 85.2 us -> 83.7 us (0.982)
    unnamed x26 -> x25, local copies, waits for them, and re-layouts: 2.67 us -> 2.11 us
where the time goes in v5:
time: 83.7 us; the launch traced here: 83.4 us
  Pallas kernels  27.9 us (33%)
  waiting for transfers between devices  26.5 us (32%)
  starting transfers between devices  23.7 us (28%)
  local copies, waits for them, and re-layouts  2.15 us (3%)
  between operations  1.8 us (2%)
  other arithmetic  1.39 us (2%)
    pallas_call x8, Pallas kernels, call(): pl.pallas_call(kernel, grid=(1,), out_shape=outs, in_specs=in_specs, out_...  27.9 us
    ppermute x8, waiting for transfers between devices, exchange(): return lax.ppermute(x, ('dp', 'atom'), route)  20.8 us
    ppermute x8, starting transfers between devices, exchange(): return lax.ppermute(x, ('dp', 'atom'), route)  10 us
    ppermute x3, starting transfers between devices, side_two(): lax.ppermute(x, axis, [(i, (i + 1) % size if i % 2 else (i - 1) % size) f...  9.85 us
    ppermute x4, waiting for transfers between devices, swap(): lax.ppermute(x, axis, [(i, i ^ bit) for i in range(lax.axis_size(axis))])  4.32 us
    ppermute x3, starting transfers between devices, side_one(): lax.ppermute(x, axis, [(i, i ^ 1) for i in range(lax.axis_size(axis))])  3.26 us
    unnamed x25, local copies, waits for them, and re-layouts  2.11 us
  transfers between devices with their start and end apart: 18, of which 13 were waited for; matrix products, arithmetic and copies ran while one was open for 0% of the time, Pallas kernels for 18%

profile of v5, /device:TPU:0, one launch (start us, length us, event | category | flops | bytes accessed | tf_op | source)
XLA Modules:
  0.0 83.4 jit_solution(544630847880711505)
XLA Ops:
  0.7 0.8 convert_add_fusion.own_ref
  1.4 3.0 %collective-permute-start = (f32[8,128]{1,0:T(8,128)S(1)}, f32[8,128]{1,0:T(8,128)S(1)}, u32[]{:S(2)}, u32[]{:S(2)}) collective-permute-start(f32[8,128]{1,0:T(8,128)S(1)} %convert_add_fusion.own_ref), channel_id=1, source_target_pairs={{0,1},{1,0},{2,3},{3,2},{4,5},{5,4},{6,7},{7,6},{8,9},{9,8},{10,11... | collective-permute-start | bytes 12296 | tf_op jit(solution)/shard_map/ppermute | solution.py:684
  4.4 3.5 %collective-permute-start.1 = (f32[8,128]{1,0:T(8,128)S(1)}, f32[8,128]{1,0:T(8,128)S(1)}, u32[]{:S(2)}, u32[]{:S(2)}) collective-permute-start(f32[8,128]{1,0:T(8,128)S(1)} %convert_add_fusion.own_ref), channel_id=1, source_target_pairs={{0,7},{1,2},{2,1},{3,4},{4,3},{5,6},{6,5},{7,0},{8,15},{9,10},{10,... | collective-permute-start | bytes 12296 | tf_op jit(solution)/shard_map/ppermute | solution.py:689
  7.9 1.0 %copy-done = f32[2,128,384]{2,1,0:T(8,128)S(1)} copy-done((f32[2,128,384]{2,1,0:T(8,128)S(1)}, f32[2,128,384]{2,1,0:T(8,128)}, u32[]{:S(2)}) %copy-start) | copy-done | bytes 393240
  8.9 0.8 %copy-done.4 = f32[2,64,128]{2,1,0:T(8,128)S(1)} copy-done((f32[2,64,128]{2,1,0:T(8,128)S(1)}, f32[2,64,128]{2,1,0:T(8,128)}, u32[]{:S(2)}) %copy-start.4) | copy-done | bytes 65560
  9.8 0.0 copy-start.7
  9.8 0.3 prepare.1
  10.1 0.1 pad_add_fusion.par_ref
  10.2 0.2 copy-done.11
  11.2 4.4 %layer_one.1 = (f32[32,8,128]{2,1,0:T(8,128)S(1)}, f32[4,128,128]{2,1,0:T(8,128)S(1)}, f32[4,128,128]{2,1,0:T(8,128)S(1)}, f32[6,128,128]{2,1,0:T(8,128)S(1)}, f...) custom-call(s32[4]{0:T(128)S(1)} %pad_add_fusion.par_ref, ...), custom_call_target="tpu_custom_call" | custom-call | flops 3000000000 | bytes 6000000 | tf_op jit(solution)/shard_map/layer_one/pallas_call | solution.py:722
  15.6 0.1 collective-permute-start.2
  15.7 3.2 %collective-permute-start.3 = (f32[128,128]{1,0:T(8,128)S(1)}, f32[128,128]{1,0:T(8,128)S(1)}, u32[]{:S(2)}, u32[]{:S(2)}) collective-permute-start(f32[128,128]{1,0:T(8,128)S(1)} %get-tuple-element.68), channel_id=1, source_target_pairs={{0,7},{1,2},{2,1},{3,4},{4,3},{5,6},{6,5},{7,0},{8,15},{9,10},{10,... | collective-permute-start | bytes 196616 | tf_op jit(solution)/shard_map/ppermute | solution.py:689
  18.9 2.7 %radial_two.1 = (f32[2,384,2048]{2,1,0:T(8,128)S(1)}, bf16[2,256,2048]{2,1,0:T(8,128)(2,1)S(1)}, bf16[2,128,2048]{2,1,0:T(8,128)(2,1)S(1)}, f32[2,128,2048]{2,1,0:T(8,128)S(1)}) custom-call(f32[32,8,128]{2,1,0:T(8,128)S(1)} %get-tuple-element.65.geom_ref, bf16[128,256]{1,0:T(8,128)(2,1)S(1)} %get-tuple-element.69.ri4, bf16[384,384]{1,0:T(8,128)(2,1)S(1)} %get-tuple-element.70.ro3), custom_call_target="tpu_custom_call" | custom-call | flops 3000000000 | bytes 6000000 | tf_op jit(solution)/shard_map/radial_two/pallas_call | solution.py:722
  21.6 1.1 %collective-permute-done.3.b_ref = f32[128,128]{1,0:T(8,128)S(1)} collective-permute-done((f32[128,128]{1,0:T(8,128)S(1)}, f32[128,128]{1,0:T(8,128)S(1)}, u32[]{:S(2)}, u32[]{:S(2)}) %collective-permute-start.3) | collective-permute-done | bytes 65568 | tf_op jit(solution)/shard_map/ppermute | solution.py:689
  22.8 6.8 %layer_two.1 = (f32[4,128,128]{2,1,0:T(8,128)S(1)}, f32[136,128]{1,0:T(8,128)S(1)}, f32[128,128]{1,0:T(8,128)S(1)}, f32[448,128]{1,0:T(8,128)S(1)}, f32[72,128]{...) custom-call(s32[4]{0:T(128)S(1)} %pad_add_fusion.par_ref, ...), custom_call_target="tpu_custom_call" | custom-call | flops 5000000000 | bytes 10000000 | tf_op jit(solution)/shard_map/layer_two/pallas_call | solution.py:722
  29.6 0.2 collective-permute-start.4
  29.8 2.6 %radial_two_back.1 = (f32[16,8,128]{2,1,0:T(8,128)S(1)}, f32[384,256]{1,0:T(8,128)S(1)}, f32[128,128]{1,0:T(8,128)S(1)}) custom-call(f32[32,8,128]{2,1,0:T(8,128)S(1)} %get-tuple-element.65.geom_ref, f32[2,384,2048]{2,1,0:T(8,128)S(1)} %get-tuple-element.71.filters_ref, bf16[2,256,2048]{2,1,0:T(8,128)(2,1)S(1)} %get-tuple-element.73.hidden_ref, ...), custom_call_target="tpu_custom_call" | custom-call | flops 3000000000 | bytes 6000000 | tf_op jit(solution)/shard_map/radial_two_back/pallas_call | solution.py:722
  32.3 3.2 %collective-permute-start.7 = (f32[128,128]{1,0:T(8,128)S(1)}, f32[128,128]{1,0:T(8,128)S(1)}, u32[]{:S(2)}, u32[]{:S(2)}) collective-permute-start(f32[128,128]{1,0:T(8,128)S(1)} %get-tuple-element.91), channel_id=1, source_target_pairs={{0,7},{1,2},{2,1},{3,4},{4,3},{5,6},{6,5},{7,0},{8,15},{9,10},{10,... | collective-permute-start | bytes 196616 | tf_op jit(solution)/shard_map/ppermute | solution.py:689
  35.5 0.2 collective-permute-start.5
  35.8 2.6 %radial_two_back_last.1 = (f32[16,8,128]{2,1,0:T(8,128)S(1)}, f32[896,128]{1,0:T(8,128)S(1)}) custom-call(f32[32,8,128]{2,1,0:T(8,128)S(1)} %get-tuple-element.65.geom_ref, f32[2,384,2048]{2,1,0:T(8,128)S(1)} %get-tuple-element.71.filters_ref, bf16[2,256,2048]{2,1,0:T(8,128)(2,1)S(1)} %get-tuple-element.73.hidden_ref, ...), custom_call_target="tpu_custom_call" | custom-call | flops 3000000000 | bytes 6000000 | tf_op jit(solution)/shard_map/radial_two_back_last/pallas_call | solution.py:722
  38.4 0.7 collective-permute-done.5
  39.1 0.2 collective-permute-start.6
  39.3 0.2 collective-permute-done.7.b_ref
  39.5 6.8 %layer_one_back.1 = (f32[16,128]{1,0:T(8,128)S(1)}, f32[16,128]{1,0:T(8,128)S(1)}, f32[896,128]{1,0:T(8,128)S(1)}) custom-call(s32[4]{0:T(128)S(1)} %pad_add_fusion.par_ref, f32[32,8,128]{2,1,0:T(8,128)S(1)} %get-tuple-element.65.geom_ref, f32[16,8,128]{2,1,0:T(8,128)S(1)} %get-tuple-element.86.dgeom_one, f32[16,8,128]{2,1,0:T(8,128)S(1)} %get-tuple-element.84.dgeom_two, ...), custom_call_target="tpu_custom_call" | custom-call | flops 6000000000 | bytes 12000000 | tf_op jit(solution)/shard_map/layer_one_back/pallas_call | solution.py:722
  46.3 0.0 collective-permute-done.6
  46.3 0.2 multiply_select_fusion
  46.5 0.1 collective-permute-start.8
  46.6 1.8 %collective-permute-done.8 = f32[896,128]{1,0:T(8,128)S(1)} collective-permute-done((f32[896,128]{1,0:T(8,128)S(1)}, f32[896,128]{1,0:T(8,128)S(1)}, u32[]{:S(2)}, u32[]{:S(2)}) %collective-permute-start.8) | collective-permute-done | bytes 458784 | tf_op jit(solution)/shard_map/ppermute | solution.py:697
  48.4 0.2 select_add_fusion
  48.7 2.2 %collective-permute-start.9 = (f32[240,128]{1,0:T(8,128)S(1)}, f32[240,128]{1,0:T(8,128)S(1)}, u32[]{:S(2)}, u32[]{:S(2)}) collective-permute-start(f32[240,128]{1,0:T(8,128)S(1)} %pad_maximum_fusion.1), channel_id=1, source_target_pairs={{0,1},{1,0},{2,3},{3,2},{4,5},{5,4},{6,7},{7,6},{8,9},{9,8},{10,11... | collective-permute-start | bytes 368648 | tf_op jit(solution)/shard_map/ppermute | solution.py:742
  50.9 1.5 %collective-permute-start.10 = (f32[224,128]{1,0:T(8,128)S(1)}, f32[224,128]{1,0:T(8,128)S(1)}, u32[]{:S(2)}, u32[]{:S(2)}) collective-permute-start(f32[224,128]{1,0:T(8,128)S(1)} %get-tuple-element.115), channel_id=1, source_target_pairs={{0,16},{1,17},{2,18},{3,19},{4,20},{5,21},{6,22},{7,23},{8,24},{9,... | collective-permute-start | bytes 344072 | tf_op jit(solution)/shard_map/ppermute | solution.py:742
  52.4 0.1 collective-permute-start.11
  52.4 2.1 %collective-permute-done.9 = f32[240,128]{1,0:T(8,128)S(1)} collective-permute-done((f32[240,128]{1,0:T(8,128)S(1)}, f32[240,128]{1,0:T(8,128)S(1)}, u32[]{:S(2)}, u32[]{:S(2)}) %collective-permute-start.9) | collective-permute-done | bytes 122912 | tf_op jit(solution)/shard_map/ppermute | solution.py:742
  54.5 2.4 %collective-permute-done.10 = f32[224,128]{1,0:T(8,128)S(1)} collective-permute-done((f32[224,128]{1,0:T(8,128)S(1)}, f32[224,128]{1,0:T(8,128)S(1)}, u32[]{:S(2)}, u32[]{:S(2)}) %collective-permute-start.10) | collective-permute-done | bytes 114720 | tf_op jit(solution)/shard_map/ppermute | solution.py:742
  56.9 1.2 %collective-permute-done.11 = f32[224,128]{1,0:T(8,128)S(1)} collective-permute-done((f32[224,128]{1,0:T(8,128)S(1)}, f32[224,128]{1,0:T(8,128)S(1)}, u32[]{:S(2)}, u32[]{:S(2)}) %collective-permute-start.11) | collective-permute-done | bytes 114720 | tf_op jit(solution)/shard_map/ppermute | solution.py:742
  58.1 1.2 %collective-permute-start.12 = (f32[232,128]{1,0:T(8,128)S(1)}, f32[232,128]{1,0:T(8,128)S(1)}, u32[]{:S(2)}, u32[]{:S(2)}) collective-permute-start(f32[232,128]{1,0:T(8,128)S(1)} %pad_maximum_fusion.3), channel_id=1, source_target_pairs={{0,2},{1,3},{2,0},{3,1},{4,6},{5,7},{6,4},{7,5},{8,12},{9,13},{10,... | collective-permute-start | bytes 356360 | tf_op jit(solution)/shard_map/ppermute | solution.py:742
  59.3 4.3 %collective-permute-done.12 = f32[232,128]{1,0:T(8,128)S(1)} collective-permute-done((f32[232,128]{1,0:T(8,128)S(1)}, f32[232,128]{1,0:T(8,128)S(1)}, u32[]{:S(2)}, u32[]{:S(2)}) %collective-permute-start.12) | collective-permute-done | bytes 118816 | tf_op jit(solution)/shard_map/ppermute | solution.py:742
  63.7 1.6 %collective-permute-start.13 = (f32[240,128]{1,0:T(8,128)S(1)}, f32[240,128]{1,0:T(8,128)S(1)}, u32[]{:S(2)}, u32[]{:S(2)}) collective-permute-start(f32[240,128]{1,0:T(8,128)S(1)} %pad_maximum_fusion.2), channel_id=1, source_target_pairs={{0,4},{1,5},{2,6},{3,7},{4,0},{5,1},{6,2},{7,3},{8,10},{9,11},{10,... | collective-permute-start | bytes 368648 | tf_op jit(solution)/shard_map/ppermute | solution.py:742
  65.2 5.6 %collective-permute-done.13 = f32[240,128]{1,0:T(8,128)S(1)} collective-permute-done((f32[240,128]{1,0:T(8,128)S(1)}, f32[240,128]{1,0:T(8,128)S(1)}, u32[]{:S(2)}, u32[]{:S(2)}) %collective-permute-start.13) | collective-permute-done | bytes 122912 | tf_op jit(solution)/shard_map/ppermute | solution.py:742
  70.8 1.6 %collective-permute-start.14 = (f32[224,128]{1,0:T(8,128)S(1)}, f32[224,128]{1,0:T(8,128)S(1)}, u32[]{:S(2)}, u32[]{:S(2)}) collective-permute-start(f32[224,128]{1,0:T(8,128)S(1)} %slice_add_fusion), channel_id=1, source_target_pairs={{0,1},{1,0},{2,3},{3,2},{4,5},{5,4},{6,7},{7,6},{8,9},{9,8},{10,11... | collective-permute-start | bytes 344072 | tf_op jit(solution)/shard_map/ppermute | solution.py:742
  72.5 1.5 %collective-permute-start.15 = (f32[224,128]{1,0:T(8,128)S(1)}, f32[224,128]{1,0:T(8,128)S(1)}, u32[]{:S(2)}, u32[]{:S(2)}) collective-permute-start(f32[224,128]{1,0:T(8,128)S(1)} %slice_add_fusion), channel_id=1, source_target_pairs={{0,16},{1,17},{2,18},{3,19},{4,20},{5,21},{6,22},{7,23},{8,24},{9,... | collective-permute-start | bytes 344072 | tf_op jit(solution)/shard_map/ppermute | solution.py:742
  74.0 0.4 collective-permute-start.16
  74.4 1.3 %collective-permute-done.14 = f32[224,128]{1,0:T(8,128)S(1)} collective-permute-done((f32[224,128]{1,0:T(8,128)S(1)}, f32[224,128]{1,0:T(8,128)S(1)}, u32[]{:S(2)}, u32[]{:S(2)}) %collective-permute-start.14) | collective-permute-done | bytes 114720 | tf_op jit(solution)/shard_map/ppermute | solution.py:742
  75.7 1.6 %collective-permute-done.15 = f32[224,128]{1,0:T(8,128)S(1)} collective-permute-done((f32[224,128]{1,0:T(8,128)S(1)}, f32[224,128]{1,0:T(8,128)S(1)}, u32[]{:S(2)}, u32[]{:S(2)}) %collective-permute-start.15) | collective-permute-done | bytes 114720 | tf_op jit(solution)/shard_map/ppermute | solution.py:742
  77.3 2.4 %collective-permute-done.16 = f32[224,128]{1,0:T(8,128)S(1)} collective-permute-done((f32[224,128]{1,0:T(8,128)S(1)}, f32[224,128]{1,0:T(8,128)S(1)}, u32[]{:S(2)}, u32[]{:S(2)}) %collective-permute-start.16) | collective-permute-done | bytes 114720 | tf_op jit(solution)/shard_map/ppermute | solution.py:742
  79.7 0.1 collective-permute-start.17
  79.8 1.8 %collective-permute-done.17.other_turned = f32[896,128]{1,0:T(8,128)S(1)} collective-permute-done((f32[896,128]{1,0:T(8,128)S(1)}, f32[896,128]{1,0:T(8,128)S(1)}, u32[]{:S(2)}, u32[]{:S(2)}) %collective-permute-start.17) | collective-permute-done | bytes 458784 | tf_op jit(solution)/shard_map/ppermute | solution.py:697
  81.6 1.7 %final.1 = (f32[1,1]{1,0:T(1,128)}, f32[3,128]{1,0:T(4,128)}, f32[3,1,3]{2,1,0:T(1,128)}, f32[96,128]{1,0:T(8,128)}, f32[2,64,128]{2,1,0:T(8,128)}, /*index=5*/f...) custom-call(s32[4]{0:T(128)S(1)} %pad_add_fusion.par_ref, ...), custom_call_target="tpu_custom_call" | custom-call | flops 100000000 | bytes 200000 | tf_op jit(solution)/shard_map/final/pallas_call | solution.py:722
  (43 shorter events, 0.3 us)
Async XLA Ops:
  1.4 9.7 %collective-permute-start = (f32[8,128]{1,0:T(8,128)S(1)}, f32[8,128]{1,0:T(8,128)S(1)}, u32[]{:S(2)}, u32[]{:S(2)}) collective-permute-start(f32[8,128]{1,0:T(8,128)S(1)} %convert_add_fusion.own_ref), channel_id=1, source_target_pairs={{0,1},{1,0},{2,3},{3,2},{4,5},{5,4},{6,7},{7,6},{8,9},{9,8},{10,11... | collective-permute-start | bytes 12296 | tf_op jit(solution)/shard_map/ppermute | solution.py:684
  4.4 6.7 %collective-permute-start.1 = (f32[8,128]{1,0:T(8,128)S(1)}, f32[8,128]{1,0:T(8,128)S(1)}, u32[]{:S(2)}, u32[]{:S(2)}) collective-permute-start(f32[8,128]{1,0:T(8,128)S(1)} %convert_add_fusion.own_ref), channel_id=1, source_target_pairs={{0,7},{1,2},{2,1},{3,4},{4,3},{5,6},{6,5},{7,0},{8,15},{9,10},{10,... | collective-permute-start | bytes 12296 | tf_op jit(solution)/shard_map/ppermute | solution.py:689
  7.9 1.0 %copy-start = (f32[2,128,384]{2,1,0:T(8,128)S(1)}, f32[2,128,384]{2,1,0:T(8,128)}, u32[]{:S(2)}) copy-start(f32[2,128,384]{2,1,0:T(8,128)} %rout_ref.1) | copy-start | bytes 1179652
  8.9 0.8 %copy-start.4 = (f32[2,64,128]{2,1,0:T(8,128)S(1)}, f32[2,64,128]{2,1,0:T(8,128)}, u32[]{:S(2)}) copy-start(f32[2,64,128]{2,1,0:T(8,128)} %rin_ref.1) | copy-start | bytes 196612
  9.8 0.7 copy-start.11
  9.8 1.4 %copy-start.1 = (f32[2,128,128]{2,1,0:T(8,128)S(1)}, f32[2,128,128]{2,1,0:T(8,128)}, u32[]{:S(2)}) copy-start(f32[2,128,128]{2,1,0:T(8,128)} %sm_ref.5) | copy-start | bytes 393220
  9.8 1.4 %copy-start.2 = (f32[2,128,128]{2,1,0:T(8,128)S(1)}, f32[2,128,128]{2,1,0:T(8,128)}, u32[]{:S(2)}) copy-start(f32[2,128,128]{2,1,0:T(8,128)} %vm_ref.5) | copy-start | bytes 393220
  9.8 1.4 %copy-start.3 = (f32[2,128,128]{2,1,0:T(8,128)S(1)}, f32[2,128,128]{2,1,0:T(8,128)}, u32[]{:S(2)}) copy-start(f32[2,128,128]{2,1,0:T(8,128)} %vg_ref.5) | copy-start | bytes 393220
  9.8 1.4 %copy-start.6 = (s32[3,32,128]{2,1,0:T(8,128)S(1)}, s32[3,32,128]{2,1,0:T(8,128)}, u32[]{:S(2)}) copy-start(s32[3,32,128]{2,1,0:T(8,128)} %shift_ref.1) | copy-start | bytes 147460
  9.8 1.4 %copy-start.7 = (f32[96,128]{1,0:T(8,128)S(1)}, f32[96,128]{1,0:T(8,128)}, u32[]{:S(2)}) copy-start(f32[96,128]{1,0:T(8,128)} %emb_ref.3) | copy-start | bytes 147460
  9.8 1.4 %copy-start.8 = (s32[32,128]{1,0:T(8,128)S(1)}, s32[32,128]{1,0:T(8,128)}, u32[]{:S(2)}) copy-start(s32[32,128]{1,0:T(8,128)} %nb_ref.1) | copy-start | bytes 49156
  9.8 1.4 %copy-start.9 = (s32[128]{0:T(128)S(1)}, s32[128]{0:T(128)}, u32[]{:S(2)}) copy-start(s32[128]{0:T(128)} %param.18) | copy-start | bytes 1540
  15.6 6.0 %collective-permute-start.2 = (f32[128,128]{1,0:T(8,128)S(1)}, f32[128,128]{1,0:T(8,128)S(1)}, u32[]{:S(2)}, u32[]{:S(2)}) collective-permute-start(f32[128,128]{1,0:T(8,128)S(1)} %get-tuple-element.67), channel_id=1, source_target_pairs={{0,1},{1,0},{2,3},{3,2},{4,5},{5,4},{6,7},{7,6},{8,9},{9,8},{10,11... | collective-permute-start | bytes 196616 | tf_op jit(solution)/shard_map/ppermute | solution.py:684
  15.7 7.0 %collective-permute-start.3 = (f32[128,128]{1,0:T(8,128)S(1)}, f32[128,128]{1,0:T(8,128)S(1)}, u32[]{:S(2)}, u32[]{:S(2)}) collective-permute-start(f32[128,128]{1,0:T(8,128)S(1)} %get-tuple-element.68), channel_id=1, source_target_pairs={{0,7},{1,2},{2,1},{3,4},{4,3},{5,6},{6,5},{7,0},{8,15},{9,10},{10,... | collective-permute-start | bytes 196616 | tf_op jit(solution)/shard_map/ppermute | solution.py:689
  18.9 3.9 %copy-start.5 = (f32[128,128]{1,0:T(8,128)S(1)}, f32[128,128]{1,0:T(8,128)}, u32[]{:S(2)}) copy-start(f32[128,128]{1,0:T(8,128)} %mid_ref.1) | copy-start | bytes 196612
  18.9 3.9 %copy-start.10 = (f32[128]{0:T(128)S(1)}, f32[128]{0:T(128)}, u32[]{:S(2)}) copy-start(f32[128]{0:T(128)} %param.29) | copy-start | bytes 1540
  29.6 5.9 %collective-permute-start.4 = (f32[136,128]{1,0:T(8,128)S(1)}, f32[136,128]{1,0:T(8,128)S(1)}, u32[]{:S(2)}, u32[]{:S(2)}) collective-permute-start(f32[136,128]{1,0:T(8,128)S(1)} %get-tuple-element.72), channel_id=1, source_target_pairs={{0,1},{1,0},{2,3},{3,2},{4,5},{5,4},{6,7},{7,6},{8,9},{9,8},{10,11... | collective-permute-start | bytes 208904 | tf_op jit(solution)/shard_map/ppermute | solution.py:684
  32.3 7.1 %collective-permute-start.7 = (f32[128,128]{1,0:T(8,128)S(1)}, f32[128,128]{1,0:T(8,128)S(1)}, u32[]{:S(2)}, u32[]{:S(2)}) collective-permute-start(f32[128,128]{1,0:T(8,128)S(1)} %get-tuple-element.91), channel_id=1, source_target_pairs={{0,7},{1,2},{2,1},{3,4},{4,3},{5,6},{6,5},{7,0},{8,15},{9,10},{10,... | collective-permute-start | bytes 196616 | tf_op jit(solution)/shard_map/ppermute | solution.py:689
  35.5 3.6 %collective-permute-start.5 = (f32[8,128]{1,0:T(8,128)S(1)}, f32[8,128]{1,0:T(8,128)S(1)}, u32[]{:S(2)}, u32[]{:S(2)}) collective-permute-start(f32[8,128]{1,0:T(8,128)S(1)} %slice_add_fusion.3), channel_id=1, source_target_pairs={{0,2},{1,3},{2,0},{3,1},{4,6},{5,7},{6,4},{7,5},{8,10},{9,11},{10,... | collective-permute-start | bytes 12296 | tf_op jit(solution)/shard_map/ppermute | solution.py:697
  39.1 7.2 %collective-permute-start.6 = (f32[8,128]{1,0:T(8,128)S(1)}, f32[8,128]{1,0:T(8,128)S(1)}, u32[]{:S(2)}, u32[]{:S(2)}) collective-permute-start(f32[8,128]{1,0:T(8,128)S(1)} %add.79), channel_id=1, source_target_pairs={{0,4},{1,5},{2,6},{3,7},{4,0},{5,1},{6,2},{7,3},{8,12},{9,13},{10,... | collective-permute-start | bytes 12296 | tf_op jit(solution)/shard_map/ppermute | solution.py:697
  46.5 1.9 %collective-permute-start.8 = (f32[896,128]{1,0:T(8,128)S(1)}, f32[896,128]{1,0:T(8,128)S(1)}, u32[]{:S(2)}, u32[]{:S(2)}) collective-permute-start(f32[896,128]{1,0:T(8,128)S(1)} %multiply_select_fusion), channel_id=1, source_target_pairs={{0,8},{8,0},{16,24},{24,16},{1,9},{9,1},{17,25},{25,17},{2,10},{10... | collective-permute-start | bytes 1376264 | tf_op jit(solution)/shard_map/ppermute | solution.py:697
  48.7 5.8 %collective-permute-start.9 = (f32[240,128]{1,0:T(8,128)S(1)}, f32[240,128]{1,0:T(8,128)S(1)}, u32[]{:S(2)}, u32[]{:S(2)}) collective-permute-start(f32[240,128]{1,0:T(8,128)S(1)} %pad_maximum_fusion.1), channel_id=1, source_target_pairs={{0,1},{1,0},{2,3},{3,2},{4,5},{5,4},{6,7},{7,6},{8,9},{9,8},{10,11... | collective-permute-start | bytes 368648 | tf_op jit(solution)/shard_map/ppermute | solution.py:742
  50.9 6.0 %collective-permute-start.10 = (f32[224,128]{1,0:T(8,128)S(1)}, f32[224,128]{1,0:T(8,128)S(1)}, u32[]{:S(2)}, u32[]{:S(2)}) collective-permute-start(f32[224,128]{1,0:T(8,128)S(1)} %get-tuple-element.115), channel_id=1, source_target_pairs={{0,16},{1,17},{2,18},{3,19},{4,20},{5,21},{6,22},{7,23},{8,24},{9,... | collective-permute-start | bytes 344072 | tf_op jit(solution)/shard_map/ppermute | solution.py:742
  52.4 5.7 %collective-permute-start.11 = (f32[224,128]{1,0:T(8,128)S(1)}, f32[224,128]{1,0:T(8,128)S(1)}, u32[]{:S(2)}, u32[]{:S(2)}) collective-permute-start(f32[224,128]{1,0:T(8,128)S(1)} %get-tuple-element.116), channel_id=1, source_target_pairs={{0,17},{1,16},{2,19},{3,18},{4,21},{5,20},{6,23},{7,22},{8,25},{9,... | collective-permute-start | bytes 344072 | tf_op jit(solution)/shard_map/ppermute | solution.py:742
  58.1 5.5 %collective-permute-start.12 = (f32[232,128]{1,0:T(8,128)S(1)}, f32[232,128]{1,0:T(8,128)S(1)}, u32[]{:S(2)}, u32[]{:S(2)}) collective-permute-start(f32[232,128]{1,0:T(8,128)S(1)} %pad_maximum_fusion.3), channel_id=1, source_target_pairs={{0,2},{1,3},{2,0},{3,1},{4,6},{5,7},{6,4},{7,5},{8,12},{9,13},{10,... | collective-permute-start | bytes 356360 | tf_op jit(solution)/shard_map/ppermute | solution.py:742
  63.7 7.2 %collective-permute-start.13 = (f32[240,128]{1,0:T(8,128)S(1)}, f32[240,128]{1,0:T(8,128)S(1)}, u32[]{:S(2)}, u32[]{:S(2)}) collective-permute-start(f32[240,128]{1,0:T(8,128)S(1)} %pad_maximum_fusion.2), channel_id=1, source_target_pairs={{0,4},{1,5},{2,6},{3,7},{4,0},{5,1},{6,2},{7,3},{8,10},{9,11},{10,... | collective-permute-start | bytes 368648 | tf_op jit(solution)/shard_map/ppermute | solution.py:742
  70.8 4.9 %collective-permute-start.14 = (f32[224,128]{1,0:T(8,128)S(1)}, f32[224,128]{1,0:T(8,128)S(1)}, u32[]{:S(2)}, u32[]{:S(2)}) collective-permute-start(f32[224,128]{1,0:T(8,128)S(1)} %slice_add_fusion), channel_id=1, source_target_pairs={{0,1},{1,0},{2,3},{3,2},{4,5},{5,4},{6,7},{7,6},{8,9},{9,8},{10,11... | collective-permute-start | bytes 344072 | tf_op jit(solution)/shard_map/ppermute | solution.py:742
  72.5 4.8 %collective-permute-start.15 = (f32[224,128]{1,0:T(8,128)S(1)}, f32[224,128]{1,0:T(8,128)S(1)}, u32[]{:S(2)}, u32[]{:S(2)}) collective-permute-start(f32[224,128]{1,0:T(8,128)S(1)} %slice_add_fusion), channel_id=1, source_target_pairs={{0,16},{1,17},{2,18},{3,19},{4,20},{5,21},{6,22},{7,23},{8,24},{9,... | collective-permute-start | bytes 344072 | tf_op jit(solution)/shard_map/ppermute | solution.py:742
  74.0 5.7 %collective-permute-start.16 = (f32[224,128]{1,0:T(8,128)S(1)}, f32[224,128]{1,0:T(8,128)S(1)}, u32[]{:S(2)}, u32[]{:S(2)}) collective-permute-start(f32[224,128]{1,0:T(8,128)S(1)} %slice_add_fusion), channel_id=1, source_target_pairs={{0,17},{1,16},{2,19},{3,18},{4,21},{5,20},{6,23},{7,22},{8,25},{9,... | collective-permute-start | bytes 344072 | tf_op jit(solution)/shard_map/ppermute | solution.py:742
  79.7 1.9 %collective-permute-start.17 = (f32[896,128]{1,0:T(8,128)S(1)}, f32[896,128]{1,0:T(8,128)S(1)}, u32[]{:S(2)}, u32[]{:S(2)}) collective-permute-start(f32[896,128]{1,0:T(8,128)S(1)} %pad_maximum_fusion.mine_turned), channel_id=1, source_target_pairs={{0,8},{8,0},{16,24},{24,16},{1,9},{9,1},{17,25},{25,17},{2,10},{10... | collective-permute-start | bytes 1376264 | tf_op jit(solution)/shard_map/ppermute | solution.py:697

commit v6 on v5

--- a/solution.py
+++ b/solution.py
@@ -334,7 +334,7 @@
 
 def positions(cell_ref, fractions):
     rows = [
-        fractions[0:1] * cell_ref[0, 0, c] + fractions[1:2] * cell_ref[0, 1, c] + fractions[2:3] * cell_ref[0, 2, c]
+        fractions[0:1] * cell_ref[0, 0, c] + fractions[1:2] * cell_ref[1, 0, c] + fractions[2:3] * cell_ref[2, 0, c]
         for c in range(3)
     ]
     return jnp.concatenate(rows + [fractions[3:8]], axis=0)
@@ -382,7 +382,7 @@
         for c in range(3):
             table = jnp.broadcast_to(places[h][c : c + 1], (pairs, LANES))
             far = jnp.take_along_axis(table, index, axis=1, mode="promise_in_bounds")
-            image = steps[0] * cell_ref[0, 0, c] + steps[1] * cell_ref[0, 1, c] + steps[2] * cell_ref[0, 2, c]
+            image = steps[0] * cell_ref[0, 0, c] + steps[1] * cell_ref[1, 0, c] + steps[2] * cell_ref[2, 0, c]
             r.append(far - near[c : c + 1] + image)
         dist = jnp.sqrt(r[0] * r[0] + r[1] * r[1] + r[2] * r[2] + 1.0)
         values = [x / dist for x in r] + [dist, mask, index.astype(F32)]
@@ -635,7 +635,7 @@
     force = force_ref[0:8] + jnp.where(lane >= LANES - halo, up, 0.0) + jnp.where(lane < halo, down, 0.0)
     forces_ref[...] = -force[0:3]
     count, basis_count = emb_ref.shape[0], rin_ref.shape[1]
-    m = [[cell_ref[0, a, c] for c in range(3)] for a in range(3)]
+    m = [[cell_ref[a, 0, c] for c in range(3)] for a in range(3)]
     det = (
         m[0][0] * (m[1][1] * m[2][2] - m[1][2] * m[2][1])
         - m[0][1] * (m[1][0] * m[2][2] - m[1][2] * m[2][0])
@@ -753,6 +753,7 @@
     me = lax.axis_index("atom")
     group = lax.axis_index("dp")
     counts_row, out_row = counts[None], readout_out[None]
+    lattice = cell.transpose(1, 0, 2)
     own_row = lax.broadcasted_iota(jnp.int32, (8, 1), 0)
     own = jnp.pad(frac, ((0, 5), (0, 0))) + jnp.where(own_row == 3, species[None], 0).astype(F32)
     side_a, side_b = side_one(own, "atom"), side_two(own, "atom")
@@ -800,7 +801,7 @@
             pltpu.VMEM((2, 4, LANES, LANES), F32),
         ],
         3 * 10**9,
-        par, cell, own, side_a, side_b, neighbours, counts_row, shifts, embedding, *prepared[:2], *layer[2:],
+        par, lattice, own, side_a, side_b, neighbours, counts_row, shifts, embedding, *prepared[:2], *layer[2:],
     )
     feat_a, feat_b = side_one(feat_a, "atom"), side_two(feat_b, "atom")
     kept_two = call(
@@ -898,16 +899,28 @@
     def plane_move(k):
         return lambda g, p: (g ^ (2 * (k >> 1)), p ^ (k & 1))
 
-    joined = exchange(jnp.concatenate([piece(1), force_sent]), plane_move(1))
-    second, third = exchange(piece(2), plane_move(2)), exchange(piece(3), plane_move(3))
-    force_a, force_b = joined[quarter : quarter + 8], joined[quarter + 8 :]
-    y = piece(0) + joined[:quarter] + second + third
+    link_a, link_b = jnp.where(core, 2, 1), jnp.where(core, 1, 2)
+
+    def move_a(g, p):
+        return plane_move(2 if g % 2 else 1)(g, p)
+
+    def move_b(g, p):
+        return plane_move(1 if g % 2 else 2)(g, p)
+
+    got_a = exchange(jnp.concatenate([piece(link_a), force_sent]), move_a)
+    got_b = exchange(jnp.concatenate([piece(link_b), force_sent]), move_b)
+    got_c = exchange(piece(3), plane_move(3))
+    joined = jnp.where(core, got_b, got_a)[quarter:]
+    force_a, force_b = joined[:8], joined[8:]
+    y = piece(0) + got_a[:quarter] + got_b[:quarter] + got_c
     for n in range(levels):
         one_bit, two_bit = bits[n], bits[(n + 1) % levels]
         joined = exchange(jnp.concatenate([y, force_b]), lambda g, p: (g, p ^ (two_bit if g % 2 else one_bit)))
         y = y + joined[:quarter]
         force_b = jnp.concatenate([force_b, joined[quarter:]])
-    x = jnp.concatenate([y] + [exchange(y, plane_move(k)) for k in (1, 2, 3)])
+    all_a, all_b = exchange(y, move_a), exchange(y, move_b)
+    all_c = exchange(y, plane_move(3))
+    x = jnp.concatenate([y, jnp.where(core, all_b, all_a), jnp.where(core, all_a, all_b), all_c])
     other = swap(x, "dp", 1)
     weights = (embedding,) + layer + (readout_mid, out_row)
     outs = (f32(1, 1), f32(3, atom_count), f32(3, 1, 3)) + tuple(f32(*x.shape) for x in weights)
@@ -919,7 +932,7 @@
         [smem()] + [whole(x) for x in outs[1:]],
         [pltpu.VMEM((G_ROWS, LANES), F32)] * 2,
         10**8,
-        par, cell, energy, force, force_a, force_b, x, other,
+        par, lattice, energy, force, force_a, force_b, x, other,
     )
     return (result[0].reshape(1), result[1], result[2].transpose(1, 0, 2)) + tuple(result[3:-1]) + (result[-1].reshape(LANES),)
 

time: 83.7 us -> 83 us (level)
    unnamed x25 -> x24, local copies, waits for them, and re-layouts: 2.11 us -> 1.88 us
  transfers between devices with their start and end apart: 18 -> 18, of which waited for: 13 -> 12; matrix products, arithmetic and copies ran while one was open for 0% -> 0% of each run, Pallas kernels for 18% -> 18%
where the time goes in v6:
time: 83 us; the launch traced here: 82.8 us
  Pallas kernels  27.9 us (34%)
  waiting for transfers between devices  25.8 us (31%)
  starting transfers between devices  23.8 us (29%)
  local copies, waits for them, and re-layouts  1.93 us (2%)
  between operations  1.83 us (2%)
  other arithmetic  1.43 us (2%)
    pallas_call x8, Pallas kernels, call(): pl.pallas_call(kernel, grid=(1,), out_shape=outs, in_specs=in_specs, out_...  27.9 us
    ppermute x8, waiting for transfers between devices, exchange(): return lax.ppermute(x, ('dp', 'atom'), route)  20.4 us
    ppermute x3, starting transfers between devices, side_two(): lax.ppermute(x, axis, [(i, (i + 1) % size if i % 2 else (i - 1) % size) f...  10.3 us
    ppermute x8, starting transfers between devices, exchange(): return lax.ppermute(x, ('dp', 'atom'), route)  9.96 us
    ppermute x4, waiting for transfers between devices, swap(): lax.ppermute(x, axis, [(i, i ^ bit) for i in range(lax.axis_size(axis))])  4.54 us
    ppermute x3, starting transfers between devices, side_one(): lax.ppermute(x, axis, [(i, i ^ 1) for i in range(lax.axis_size(axis))])  3.25 us
    unnamed x24, local copies, waits for them, and re-layouts  1.88 us
  transfers between devices with their start and end apart: 18, of which 12 were waited for; matrix products, arithmetic and copies ran while one was open for 0% of the time, Pallas kernels for 18%

profile of v6, /device:TPU:0, one launch (start us, length us, event | category | flops | bytes accessed | tf_op | source)
XLA Modules:
  0.0 82.8 jit_solution(15317652848172055965)
XLA Ops:
  0.7 0.8 convert_add_fusion.own_ref
  1.4 3.0 %collective-permute-start = (f32[8,128]{1,0:T(8,128)S(1)}, f32[8,128]{1,0:T(8,128)S(1)}, u32[]{:S(2)}, u32[]{:S(2)}) collective-permute-start(f32[8,128]{1,0:T(8,128)S(1)} %convert_add_fusion.own_ref), channel_id=1, source_target_pairs={{0,1},{1,0},{2,3},{3,2},{4,5},{5,4},{6,7},{7,6},{8,9},{9,8},{10,11... | collective-permute-start | bytes 12296 | tf_op jit(solution)/shard_map/ppermute | solution.py:684
  4.4 3.5 %collective-permute-start.1 = (f32[8,128]{1,0:T(8,128)S(1)}, f32[8,128]{1,0:T(8,128)S(1)}, u32[]{:S(2)}, u32[]{:S(2)}) collective-permute-start(f32[8,128]{1,0:T(8,128)S(1)} %convert_add_fusion.own_ref), channel_id=1, source_target_pairs={{0,7},{1,2},{2,1},{3,4},{4,3},{5,6},{6,5},{7,0},{8,15},{9,10},{10,... | collective-permute-start | bytes 12296 | tf_op jit(solution)/shard_map/ppermute | solution.py:689
  7.9 1.0 %copy-done.1 = f32[2,128,384]{2,1,0:T(8,128)S(1)} copy-done((f32[2,128,384]{2,1,0:T(8,128)S(1)}, f32[2,128,384]{2,1,0:T(8,128)}, u32[]{:S(2)}) %copy-start.1) | copy-done | bytes 393240
  8.9 0.8 %copy-done.5 = f32[2,64,128]{2,1,0:T(8,128)S(1)} copy-done((f32[2,64,128]{2,1,0:T(8,128)S(1)}, f32[2,64,128]{2,1,0:T(8,128)}, u32[]{:S(2)}) %copy-start.5) | copy-done | bytes 65560
  9.8 0.0 copy-start.7
  9.8 0.0 copy-start.8
  9.8 0.0 copy-start.9
  9.8 0.3 prepare.1
  10.1 0.1 pad_add_fusion.par_ref
  11.0 4.4 %layer_one.1 = (f32[32,8,128]{2,1,0:T(8,128)S(1)}, f32[4,128,128]{2,1,0:T(8,128)S(1)}, f32[4,128,128]{2,1,0:T(8,128)S(1)}, f32[6,128,128]{2,1,0:T(8,128)S(1)}, f...) custom-call(s32[4]{0:T(128)S(1)} %pad_add_fusion.par_ref, ...), custom_call_target="tpu_custom_call" | custom-call | flops 3000000000 | bytes 6000000 | tf_op jit(solution)/shard_map/layer_one/pallas_call | solution.py:722
  15.4 0.1 collective-permute-start.2
  15.5 3.4 %collective-permute-start.3 = (f32[128,128]{1,0:T(8,128)S(1)}, f32[128,128]{1,0:T(8,128)S(1)}, u32[]{:S(2)}, u32[]{:S(2)}) collective-permute-start(f32[128,128]{1,0:T(8,128)S(1)} %get-tuple-element.68), channel_id=1, source_target_pairs={{0,7},{1,2},{2,1},{3,4},{4,3},{5,6},{6,5},{7,0},{8,15},{9,10},{10,... | collective-permute-start | bytes 196616 | tf_op jit(solution)/shard_map/ppermute | solution.py:689
  18.9 2.7 %radial_two.1 = (f32[2,384,2048]{2,1,0:T(8,128)S(1)}, bf16[2,256,2048]{2,1,0:T(8,128)(2,1)S(1)}, bf16[2,128,2048]{2,1,0:T(8,128)(2,1)S(1)}, f32[2,128,2048]{2,1,0:T(8,128)S(1)}) custom-call(f32[32,8,128]{2,1,0:T(8,128)S(1)} %get-tuple-element.65.geom_ref, bf16[128,256]{1,0:T(8,128)(2,1)S(1)} %get-tuple-element.69.ri4, bf16[384,384]{1,0:T(8,128)(2,1)S(1)} %get-tuple-element.70.ro3), custom_call_target="tpu_custom_call" | custom-call | flops 3000000000 | bytes 6000000 | tf_op jit(solution)/shard_map/radial_two/pallas_call | solution.py:722
  21.6 0.9 %collective-permute-done.3.b_ref = f32[128,128]{1,0:T(8,128)S(1)} collective-permute-done((f32[128,128]{1,0:T(8,128)S(1)}, f32[128,128]{1,0:T(8,128)S(1)}, u32[]{:S(2)}, u32[]{:S(2)}) %collective-permute-start.3) | collective-permute-done | bytes 65568 | tf_op jit(solution)/shard_map/ppermute | solution.py:689
  22.5 6.8 %layer_two.1 = (f32[4,128,128]{2,1,0:T(8,128)S(1)}, f32[136,128]{1,0:T(8,128)S(1)}, f32[128,128]{1,0:T(8,128)S(1)}, f32[448,128]{1,0:T(8,128)S(1)}, f32[72,128]{...) custom-call(s32[4]{0:T(128)S(1)} %pad_add_fusion.par_ref, ...), custom_call_target="tpu_custom_call" | custom-call | flops 5000000000 | bytes 10000000 | tf_op jit(solution)/shard_map/layer_two/pallas_call | solution.py:722
  29.4 0.2 collective-permute-start.4
  29.6 2.6 %radial_two_back.1 = (f32[16,8,128]{2,1,0:T(8,128)S(1)}, f32[384,256]{1,0:T(8,128)S(1)}, f32[128,128]{1,0:T(8,128)S(1)}) custom-call(f32[32,8,128]{2,1,0:T(8,128)S(1)} %get-tuple-element.65.geom_ref, f32[2,384,2048]{2,1,0:T(8,128)S(1)} %get-tuple-element.71.filters_ref, bf16[2,256,2048]{2,1,0:T(8,128)(2,1)S(1)} %get-tuple-element.73.hidden_ref, ...), custom_call_target="tpu_custom_call" | custom-call | flops 3000000000 | bytes 6000000 | tf_op jit(solution)/shard_map/radial_two_back/pallas_call | solution.py:722
  32.1 3.4 %collective-permute-start.7 = (f32[128,128]{1,0:T(8,128)S(1)}, f32[128,128]{1,0:T(8,128)S(1)}, u32[]{:S(2)}, u32[]{:S(2)}) collective-permute-start(f32[128,128]{1,0:T(8,128)S(1)} %get-tuple-element.91), channel_id=1, source_target_pairs={{0,7},{1,2},{2,1},{3,4},{4,3},{5,6},{6,5},{7,0},{8,15},{9,10},{10,... | collective-permute-start | bytes 196616 | tf_op jit(solution)/shard_map/ppermute | solution.py:689
  35.5 0.0 collective-permute-start.5
  35.5 2.6 %radial_two_back_last.1 = (f32[16,8,128]{2,1,0:T(8,128)S(1)}, f32[896,128]{1,0:T(8,128)S(1)}) custom-call(f32[32,8,128]{2,1,0:T(8,128)S(1)} %get-tuple-element.65.geom_ref, f32[2,384,2048]{2,1,0:T(8,128)S(1)} %get-tuple-element.71.filters_ref, bf16[2,256,2048]{2,1,0:T(8,128)(2,1)S(1)} %get-tuple-element.73.hidden_ref, ...), custom_call_target="tpu_custom_call" | custom-call | flops 3000000000 | bytes 6000000 | tf_op jit(solution)/shard_map/radial_two_back_last/pallas_call | solution.py:722
  38.1 1.0 %collective-permute-done.5 = f32[8,128]{1,0:T(8,128)S(1)} collective-permute-done((f32[8,128]{1,0:T(8,128)S(1)}, f32[8,128]{1,0:T(8,128)S(1)}, u32[]{:S(2)}, u32[]{:S(2)}) %collective-permute-start.5) | collective-permute-done | bytes 4128 | tf_op jit(solution)/shard_map/ppermute | solution.py:697
  39.1 0.2 collective-permute-start.6
  39.3 6.8 %layer_one_back.1 = (f32[16,128]{1,0:T(8,128)S(1)}, f32[16,128]{1,0:T(8,128)S(1)}, f32[896,128]{1,0:T(8,128)S(1)}) custom-call(s32[4]{0:T(128)S(1)} %pad_add_fusion.par_ref, f32[32,8,128]{2,1,0:T(8,128)S(1)} %get-tuple-element.65.geom_ref, f32[16,8,128]{2,1,0:T(8,128)S(1)} %get-tuple-element.86.dgeom_one, f32[16,8,128]{2,1,0:T(8,128)S(1)} %get-tuple-element.84.dgeom_two, ...), custom_call_target="tpu_custom_call" | custom-call | flops 6000000000 | bytes 12000000 | tf_op jit(solution)/shard_map/layer_one_back/pallas_call | solution.py:722
  46.1 0.0 collective-permute-done.6
  46.2 0.2 multiply_select_fusion
  46.4 0.1 collective-permute-start.8
  46.5 1.8 %collective-permute-done.8 = f32[896,128]{1,0:T(8,128)S(1)} collective-permute-done((f32[896,128]{1,0:T(8,128)S(1)}, f32[896,128]{1,0:T(8,128)S(1)}, u32[]{:S(2)}, u32[]{:S(2)}) %collective-permute-start.8) | collective-permute-done | bytes 458784 | tf_op jit(solution)/shard_map/ppermute | solution.py:697
  48.2 0.2 select_add_fusion
  48.5 2.3 %collective-permute-start.10 = (f32[240,128]{1,0:T(8,128)S(1)}, f32[240,128]{1,0:T(8,128)S(1)}, u32[]{:S(2)}, u32[]{:S(2)}) collective-permute-start(f32[240,128]{1,0:T(8,128)S(1)} %get-tuple-element.122), channel_id=1, source_target_pairs={{0,1},{1,0},{2,3},{3,2},{4,5},{5,4},{6,7},{7,6},{8,24},{9,25},{10,... | collective-permute-start | bytes 368648 | tf_op jit(solution)/shard_map/ppermute | solution.py:742
  50.9 1.5 %collective-permute-start.9 = (f32[240,128]{1,0:T(8,128)S(1)}, f32[240,128]{1,0:T(8,128)S(1)}, u32[]{:S(2)}, u32[]{:S(2)}) collective-permute-start(f32[240,128]{1,0:T(8,128)S(1)} %get-tuple-element.123), channel_id=1, source_target_pairs={{0,16},{1,17},{2,18},{3,19},{4,20},{5,21},{6,22},{7,23},{8,9},{9,8... | collective-permute-start | bytes 368648 | tf_op jit(solution)/shard_map/ppermute | solution.py:742
  52.4 0.0 collective-permute-start.11
  52.4 2.6 %collective-permute-done.10 = f32[240,128]{1,0:T(8,128)S(1)} collective-permute-done((f32[240,128]{1,0:T(8,128)S(1)}, f32[240,128]{1,0:T(8,128)S(1)}, u32[]{:S(2)}, u32[]{:S(2)}) %collective-permute-start.10) | collective-permute-done | bytes 122912 | tf_op jit(solution)/shard_map/ppermute | solution.py:742
  55.0 1.7 %collective-permute-done.9 = f32[240,128]{1,0:T(8,128)S(1)} collective-permute-done((f32[240,128]{1,0:T(8,128)S(1)}, f32[240,128]{1,0:T(8,128)S(1)}, u32[]{:S(2)}, u32[]{:S(2)}) %collective-permute-start.9) | collective-permute-done | bytes 122912 | tf_op jit(solution)/shard_map/ppermute | solution.py:742
  56.8 1.3 %collective-permute-done.11 = f32[224,128]{1,0:T(8,128)S(1)} collective-permute-done((f32[224,128]{1,0:T(8,128)S(1)}, f32[224,128]{1,0:T(8,128)S(1)}, u32[]{:S(2)}, u32[]{:S(2)}) %collective-permute-start.11) | collective-permute-done | bytes 114720 | tf_op jit(solution)/shard_map/ppermute | solution.py:742
  58.2 1.2 %collective-permute-start.12 = (f32[232,128]{1,0:T(8,128)S(1)}, f32[232,128]{1,0:T(8,128)S(1)}, u32[]{:S(2)}, u32[]{:S(2)}) collective-permute-start(f32[232,128]{1,0:T(8,128)S(1)} %pad_maximum_fusion.4), channel_id=1, source_target_pairs={{0,2},{1,3},{2,0},{3,1},{4,6},{5,7},{6,4},{7,5},{8,12},{9,13},{10,... | collective-permute-start | bytes 356360 | tf_op jit(solution)/shard_map/ppermute | solution.py:742
  59.4 4.3 %collective-permute-done.12 = f32[232,128]{1,0:T(8,128)S(1)} collective-permute-done((f32[232,128]{1,0:T(8,128)S(1)}, f32[232,128]{1,0:T(8,128)S(1)}, u32[]{:S(2)}, u32[]{:S(2)}) %collective-permute-start.12) | collective-permute-done | bytes 118816 | tf_op jit(solution)/shard_map/ppermute | solution.py:742
  63.7 1.3 %collective-permute-start.13 = (f32[240,128]{1,0:T(8,128)S(1)}, f32[240,128]{1,0:T(8,128)S(1)}, u32[]{:S(2)}, u32[]{:S(2)}) collective-permute-start(f32[240,128]{1,0:T(8,128)S(1)} %pad_maximum_fusion.3), channel_id=1, source_target_pairs={{0,4},{1,5},{2,6},{3,7},{4,0},{5,1},{6,2},{7,3},{8,10},{9,11},{10,... | collective-permute-start | bytes 368648 | tf_op jit(solution)/shard_map/ppermute | solution.py:742
  65.1 5.8 %collective-permute-done.13 = f32[240,128]{1,0:T(8,128)S(1)} collective-permute-done((f32[240,128]{1,0:T(8,128)S(1)}, f32[240,128]{1,0:T(8,128)S(1)}, u32[]{:S(2)}, u32[]{:S(2)}) %collective-permute-start.13) | collective-permute-done | bytes 122912 | tf_op jit(solution)/shard_map/ppermute | solution.py:742
  70.9 1.5 %collective-permute-start.14 = (f32[224,128]{1,0:T(8,128)S(1)}, f32[224,128]{1,0:T(8,128)S(1)}, u32[]{:S(2)}, u32[]{:S(2)}) collective-permute-start(f32[224,128]{1,0:T(8,128)S(1)} %slice_add_fusion), channel_id=1, source_target_pairs={{0,16},{1,17},{2,18},{3,19},{4,20},{5,21},{6,22},{7,23},{8,9},{9,8... | collective-permute-start | bytes 344072 | tf_op jit(solution)/shard_map/ppermute | solution.py:742
  72.4 0.9 %collective-permute-start.15 = (f32[224,128]{1,0:T(8,128)S(1)}, f32[224,128]{1,0:T(8,128)S(1)}, u32[]{:S(2)}, u32[]{:S(2)}) collective-permute-start(f32[224,128]{1,0:T(8,128)S(1)} %slice_add_fusion), channel_id=1, source_target_pairs={{0,1},{1,0},{2,3},{3,2},{4,5},{5,4},{6,7},{7,6},{8,24},{9,25},{10,... | collective-permute-start | bytes 344072 | tf_op jit(solution)/shard_map/ppermute | solution.py:742
  73.3 1.1 %collective-permute-start.16 = (f32[224,128]{1,0:T(8,128)S(1)}, f32[224,128]{1,0:T(8,128)S(1)}, u32[]{:S(2)}, u32[]{:S(2)}) collective-permute-start(f32[224,128]{1,0:T(8,128)S(1)} %slice_add_fusion), channel_id=1, source_target_pairs={{0,17},{1,16},{2,19},{3,18},{4,21},{5,20},{6,23},{7,22},{8,25},{9,... | collective-permute-start | bytes 344072 | tf_op jit(solution)/shard_map/ppermute | solution.py:742
  74.5 1.3 %collective-permute-done.14 = f32[224,128]{1,0:T(8,128)S(1)} collective-permute-done((f32[224,128]{1,0:T(8,128)S(1)}, f32[224,128]{1,0:T(8,128)S(1)}, u32[]{:S(2)}, u32[]{:S(2)}) %collective-permute-start.14) | collective-permute-done | bytes 114720 | tf_op jit(solution)/shard_map/ppermute | solution.py:742
  75.8 1.4 %collective-permute-done.15 = f32[224,128]{1,0:T(8,128)S(1)} collective-permute-done((f32[224,128]{1,0:T(8,128)S(1)}, f32[224,128]{1,0:T(8,128)S(1)}, u32[]{:S(2)}, u32[]{:S(2)}) %collective-permute-start.15) | collective-permute-done | bytes 114720 | tf_op jit(solution)/shard_map/ppermute | solution.py:742
  77.2 1.8 %collective-permute-done.16 = f32[224,128]{1,0:T(8,128)S(1)} collective-permute-done((f32[224,128]{1,0:T(8,128)S(1)}, f32[224,128]{1,0:T(8,128)S(1)}, u32[]{:S(2)}, u32[]{:S(2)}) %collective-permute-start.16) | collective-permute-done | bytes 114720 | tf_op jit(solution)/shard_map/ppermute | solution.py:742
  79.1 0.1 collective-permute-start.17
  79.2 1.8 %collective-permute-done.17.other_turned = f32[896,128]{1,0:T(8,128)S(1)} collective-permute-done((f32[896,128]{1,0:T(8,128)S(1)}, f32[896,128]{1,0:T(8,128)S(1)}, u32[]{:S(2)}, u32[]{:S(2)}) %collective-permute-start.17) | collective-permute-done | bytes 458784 | tf_op jit(solution)/shard_map/ppermute | solution.py:697
  80.9 1.7 %final.1 = (f32[1,1]{1,0:T(1,128)}, f32[3,128]{1,0:T(4,128)}, f32[3,1,3]{2,1,0:T(1,128)}, f32[96,128]{1,0:T(8,128)}, f32[2,64,128]{2,1,0:T(8,128)}, /*index=5*/f...) custom-call(s32[4]{0:T(128)S(1)} %pad_add_fusion.par_ref, ...), custom_call_target="tpu_custom_call" | custom-call | flops 100000000 | bytes 200000 | tf_op jit(solution)/shard_map/final/pallas_call | solution.py:722
  (44 shorter events, 0.3 us)
Async XLA Ops:
  1.4 9.5 %collective-permute-start = (f32[8,128]{1,0:T(8,128)S(1)}, f32[8,128]{1,0:T(8,128)S(1)}, u32[]{:S(2)}, u32[]{:S(2)}) collective-permute-start(f32[8,128]{1,0:T(8,128)S(1)} %convert_add_fusion.own_ref), channel_id=1, source_target_pairs={{0,1},{1,0},{2,3},{3,2},{4,5},{5,4},{6,7},{7,6},{8,9},{9,8},{10,11... | collective-permute-start | bytes 12296 | tf_op jit(solution)/shard_map/ppermute | solution.py:684
  4.4 6.5 %collective-permute-start.1 = (f32[8,128]{1,0:T(8,128)S(1)}, f32[8,128]{1,0:T(8,128)S(1)}, u32[]{:S(2)}, u32[]{:S(2)}) collective-permute-start(f32[8,128]{1,0:T(8,128)S(1)} %convert_add_fusion.own_ref), channel_id=1, source_target_pairs={{0,7},{1,2},{2,1},{3,4},{4,3},{5,6},{6,5},{7,0},{8,15},{9,10},{10,... | collective-permute-start | bytes 12296 | tf_op jit(solution)/shard_map/ppermute | solution.py:689
  7.9 1.0 %copy-start.1 = (f32[2,128,384]{2,1,0:T(8,128)S(1)}, f32[2,128,384]{2,1,0:T(8,128)}, u32[]{:S(2)}) copy-start(f32[2,128,384]{2,1,0:T(8,128)} %rout_ref.1) | copy-start | bytes 1179652
  8.9 0.8 %copy-start.5 = (f32[2,64,128]{2,1,0:T(8,128)S(1)}, f32[2,64,128]{2,1,0:T(8,128)}, u32[]{:S(2)}) copy-start(f32[2,64,128]{2,1,0:T(8,128)} %rin_ref.1) | copy-start | bytes 196612
  9.8 1.1 %copy-start = (f32[1,3,3]{2,0,1:T(1,128)S(1)}, f32[1,3,3]{2,0,1:T(1,128)}, u32[]{:S(2)}) copy-start(f32[1,3,3]{2,0,1:T(1,128)} %param.20) | copy-start | bytes 112
  9.8 1.1 %copy-start.2 = (f32[2,128,128]{2,1,0:T(8,128)S(1)}, f32[2,128,128]{2,1,0:T(8,128)}, u32[]{:S(2)}) copy-start(f32[2,128,128]{2,1,0:T(8,128)} %sm_ref.5) | copy-start | bytes 393220
  9.8 1.1 %copy-start.3 = (f32[2,128,128]{2,1,0:T(8,128)S(1)}, f32[2,128,128]{2,1,0:T(8,128)}, u32[]{:S(2)}) copy-start(f32[2,128,128]{2,1,0:T(8,128)} %vm_ref.5) | copy-start | bytes 393220
  9.8 1.2 %copy-start.4 = (f32[2,128,128]{2,1,0:T(8,128)S(1)}, f32[2,128,128]{2,1,0:T(8,128)}, u32[]{:S(2)}) copy-start(f32[2,128,128]{2,1,0:T(8,128)} %vg_ref.5) | copy-start | bytes 393220
  9.8 1.2 %copy-start.7 = (s32[3,32,128]{2,1,0:T(8,128)S(1)}, s32[3,32,128]{2,1,0:T(8,128)}, u32[]{:S(2)}) copy-start(s32[3,32,128]{2,1,0:T(8,128)} %shift_ref.1) | copy-start | bytes 147460
  9.8 1.2 %copy-start.8 = (f32[96,128]{1,0:T(8,128)S(1)}, f32[96,128]{1,0:T(8,128)}, u32[]{:S(2)}) copy-start(f32[96,128]{1,0:T(8,128)} %emb_ref.3) | copy-start | bytes 147460
  9.8 1.2 %copy-start.9 = (s32[32,128]{1,0:T(8,128)S(1)}, s32[32,128]{1,0:T(8,128)}, u32[]{:S(2)}) copy-start(s32[32,128]{1,0:T(8,128)} %nb_ref.1) | copy-start | bytes 49156
  9.8 1.2 %copy-start.10 = (s32[128]{0:T(128)S(1)}, s32[128]{0:T(128)}, u32[]{:S(2)}) copy-start(s32[128]{0:T(128)} %param.18) | copy-start | bytes 1540
  15.4 6.2 %collective-permute-start.2 = (f32[128,128]{1,0:T(8,128)S(1)}, f32[128,128]{1,0:T(8,128)S(1)}, u32[]{:S(2)}, u32[]{:S(2)}) collective-permute-start(f32[128,128]{1,0:T(8,128)S(1)} %get-tuple-element.67), channel_id=1, source_target_pairs={{0,1},{1,0},{2,3},{3,2},{4,5},{5,4},{6,7},{7,6},{8,9},{9,8},{10,11... | collective-permute-start | bytes 196616 | tf_op jit(solution)/shard_map/ppermute | solution.py:684
  15.5 7.0 %collective-permute-start.3 = (f32[128,128]{1,0:T(8,128)S(1)}, f32[128,128]{1,0:T(8,128)S(1)}, u32[]{:S(2)}, u32[]{:S(2)}) collective-permute-start(f32[128,128]{1,0:T(8,128)S(1)} %get-tuple-element.68), channel_id=1, source_target_pairs={{0,7},{1,2},{2,1},{3,4},{4,3},{5,6},{6,5},{7,0},{8,15},{9,10},{10,... | collective-permute-start | bytes 196616 | tf_op jit(solution)/shard_map/ppermute | solution.py:689
  18.9 3.6 %copy-start.6 = (f32[128,128]{1,0:T(8,128)S(1)}, f32[128,128]{1,0:T(8,128)}, u32[]{:S(2)}) copy-start(f32[128,128]{1,0:T(8,128)} %mid_ref.1) | copy-start | bytes 196612
  18.9 3.6 %copy-start.11 = (f32[128]{0:T(128)S(1)}, f32[128]{0:T(128)}, u32[]{:S(2)}) copy-start(f32[128]{0:T(128)} %param.29) | copy-start | bytes 1540
  29.4 6.2 %collective-permute-start.4 = (f32[136,128]{1,0:T(8,128)S(1)}, f32[136,128]{1,0:T(8,128)S(1)}, u32[]{:S(2)}, u32[]{:S(2)}) collective-permute-start(f32[136,128]{1,0:T(8,128)S(1)} %get-tuple-element.72), channel_id=1, source_target_pairs={{0,1},{1,0},{2,3},{3,2},{4,5},{5,4},{6,7},{7,6},{8,9},{9,8},{10,11... | collective-permute-start | bytes 208904 | tf_op jit(solution)/shard_map/ppermute | solution.py:684
  32.1 7.2 %collective-permute-start.7 = (f32[128,128]{1,0:T(8,128)S(1)}, f32[128,128]{1,0:T(8,128)S(1)}, u32[]{:S(2)}, u32[]{:S(2)}) collective-permute-start(f32[128,128]{1,0:T(8,128)S(1)} %get-tuple-element.91), channel_id=1, source_target_pairs={{0,7},{1,2},{2,1},{3,4},{4,3},{5,6},{6,5},{7,0},{8,15},{9,10},{10,... | collective-permute-start | bytes 196616 | tf_op jit(solution)/shard_map/ppermute | solution.py:689
  35.5 3.6 %collective-permute-start.5 = (f32[8,128]{1,0:T(8,128)S(1)}, f32[8,128]{1,0:T(8,128)S(1)}, u32[]{:S(2)}, u32[]{:S(2)}) collective-permute-start(f32[8,128]{1,0:T(8,128)S(1)} %slice_add_fusion.4), channel_id=1, source_target_pairs={{0,2},{1,3},{2,0},{3,1},{4,6},{5,7},{6,4},{7,5},{8,10},{9,11},{10,... | collective-permute-start | bytes 12296 | tf_op jit(solution)/shard_map/ppermute | solution.py:697
  39.1 7.0 %collective-permute-start.6 = (f32[8,128]{1,0:T(8,128)S(1)}, f32[8,128]{1,0:T(8,128)S(1)}, u32[]{:S(2)}, u32[]{:S(2)}) collective-permute-start(f32[8,128]{1,0:T(8,128)S(1)} %add.79), channel_id=1, source_target_pairs={{0,4},{1,5},{2,6},{3,7},{4,0},{5,1},{6,2},{7,3},{8,12},{9,13},{10,... | collective-permute-start | bytes 12296 | tf_op jit(solution)/shard_map/ppermute | solution.py:697
  46.4 1.9 %collective-permute-start.8 = (f32[896,128]{1,0:T(8,128)S(1)}, f32[896,128]{1,0:T(8,128)S(1)}, u32[]{:S(2)}, u32[]{:S(2)}) collective-permute-start(f32[896,128]{1,0:T(8,128)S(1)} %multiply_select_fusion), channel_id=1, source_target_pairs={{0,8},{8,0},{16,24},{24,16},{1,9},{9,1},{17,25},{25,17},{2,10},{10... | collective-permute-start | bytes 1376264 | tf_op jit(solution)/shard_map/ppermute | solution.py:697
  48.5 6.5 %collective-permute-start.10 = (f32[240,128]{1,0:T(8,128)S(1)}, f32[240,128]{1,0:T(8,128)S(1)}, u32[]{:S(2)}, u32[]{:S(2)}) collective-permute-start(f32[240,128]{1,0:T(8,128)S(1)} %get-tuple-element.122), channel_id=1, source_target_pairs={{0,1},{1,0},{2,3},{3,2},{4,5},{5,4},{6,7},{7,6},{8,24},{9,25},{10,... | collective-permute-start | bytes 368648 | tf_op jit(solution)/shard_map/ppermute | solution.py:742
  50.9 5.9 %collective-permute-start.9 = (f32[240,128]{1,0:T(8,128)S(1)}, f32[240,128]{1,0:T(8,128)S(1)}, u32[]{:S(2)}, u32[]{:S(2)}) collective-permute-start(f32[240,128]{1,0:T(8,128)S(1)} %get-tuple-element.123), channel_id=1, source_target_pairs={{0,16},{1,17},{2,18},{3,19},{4,20},{5,21},{6,22},{7,23},{8,9},{9,8... | collective-permute-start | bytes 368648 | tf_op jit(solution)/shard_map/ppermute | solution.py:742
  52.4 5.7 %collective-permute-start.11 = (f32[224,128]{1,0:T(8,128)S(1)}, f32[224,128]{1,0:T(8,128)S(1)}, u32[]{:S(2)}, u32[]{:S(2)}) collective-permute-start(f32[224,128]{1,0:T(8,128)S(1)} %get-tuple-element.115), channel_id=1, source_target_pairs={{0,17},{1,16},{2,19},{3,18},{4,21},{5,20},{6,23},{7,22},{8,25},{9,... | collective-permute-start | bytes 344072 | tf_op jit(solution)/shard_map/ppermute | solution.py:742
  58.2 5.5 %collective-permute-start.12 = (f32[232,128]{1,0:T(8,128)S(1)}, f32[232,128]{1,0:T(8,128)S(1)}, u32[]{:S(2)}, u32[]{:S(2)}) collective-permute-start(f32[232,128]{1,0:T(8,128)S(1)} %pad_maximum_fusion.4), channel_id=1, source_target_pairs={{0,2},{1,3},{2,0},{3,1},{4,6},{5,7},{6,4},{7,5},{8,12},{9,13},{10,... | collective-permute-start | bytes 356360 | tf_op jit(solution)/shard_map/ppermute | solution.py:742
  63.7 7.2 %collective-permute-start.13 = (f32[240,128]{1,0:T(8,128)S(1)}, f32[240,128]{1,0:T(8,128)S(1)}, u32[]{:S(2)}, u32[]{:S(2)}) collective-permute-start(f32[240,128]{1,0:T(8,128)S(1)} %pad_maximum_fusion.3), channel_id=1, source_target_pairs={{0,4},{1,5},{2,6},{3,7},{4,0},{5,1},{6,2},{7,3},{8,10},{9,11},{10,... | collective-permute-start | bytes 368648 | tf_op jit(solution)/shard_map/ppermute | solution.py:742
  70.9 4.9 %collective-permute-start.14 = (f32[224,128]{1,0:T(8,128)S(1)}, f32[224,128]{1,0:T(8,128)S(1)}, u32[]{:S(2)}, u32[]{:S(2)}) collective-permute-start(f32[224,128]{1,0:T(8,128)S(1)} %slice_add_fusion), channel_id=1, source_target_pairs={{0,16},{1,17},{2,18},{3,19},{4,20},{5,21},{6,22},{7,23},{8,9},{9,8... | collective-permute-start | bytes 344072 | tf_op jit(solution)/shard_map/ppermute | solution.py:742
  72.4 4.8 %collective-permute-start.15 = (f32[224,128]{1,0:T(8,128)S(1)}, f32[224,128]{1,0:T(8,128)S(1)}, u32[]{:S(2)}, u32[]{:S(2)}) collective-permute-start(f32[224,128]{1,0:T(8,128)S(1)} %slice_add_fusion), channel_id=1, source_target_pairs={{0,1},{1,0},{2,3},{3,2},{4,5},{5,4},{6,7},{7,6},{8,24},{9,25},{10,... | collective-permute-start | bytes 344072 | tf_op jit(solution)/shard_map/ppermute | solution.py:742
  73.3 5.7 %collective-permute-start.16 = (f32[224,128]{1,0:T(8,128)S(1)}, f32[224,128]{1,0:T(8,128)S(1)}, u32[]{:S(2)}, u32[]{:S(2)}) collective-permute-start(f32[224,128]{1,0:T(8,128)S(1)} %slice_add_fusion), channel_id=1, source_target_pairs={{0,17},{1,16},{2,19},{3,18},{4,21},{5,20},{6,23},{7,22},{8,25},{9,... | collective-permute-start | bytes 344072 | tf_op jit(solution)/shard_map/ppermute | solution.py:742
  79.1 1.9 %collective-permute-start.17 = (f32[896,128]{1,0:T(8,128)S(1)}, f32[896,128]{1,0:T(8,128)S(1)}, u32[]{:S(2)}, u32[]{:S(2)}) collective-permute-start(f32[896,128]{1,0:T(8,128)S(1)} %pad_maximum_fusion.mine_turned), channel_id=1, source_target_pairs={{0,8},{8,0},{16,24},{24,16},{1,9},{9,1},{17,25},{25,17},{2,10},{10... | collective-permute-start | bytes 1376264 | tf_op jit(solution)/shard_map/ppermute | solution.py:697

commit v7 on v6

--- a/solution.py
+++ b/solution.py
@@ -763,7 +763,6 @@
     bits = [2 << n for n in range(levels)]
     opposite = jnp.where(me % 2 == 1, (me + 1) % slabs, (me + slabs - 1) % slabs)
     turned = (me ^ opposite ^ 1) >> 1
-    turned = jnp.where(group % 2 == 1, (turned >> 1) | ((turned & 1) << (levels - 1)), turned)
     par = jnp.stack([me % 2, group, plane, turned]).astype(jnp.int32)
     layer = (radial_in, radial_out, scalar_mix, vector_mix, vector_gate)
     block = f32(LANES, LANES)
@@ -914,8 +913,8 @@
     force_a, force_b = joined[:8], joined[8:]
     y = piece(0) + got_a[:quarter] + got_b[:quarter] + got_c
     for n in range(levels):
-        one_bit, two_bit = bits[n], bits[(n + 1) % levels]
-        joined = exchange(jnp.concatenate([y, force_b]), lambda g, p: (g, p ^ (two_bit if g % 2 else one_bit)))
+        one_bit = bits[n]
+        joined = exchange(jnp.concatenate([y, force_b]), lambda g, p: (g, p ^ one_bit))
         y = y + joined[:quarter]
         force_b = jnp.concatenate([force_b, joined[quarter:]])
     all_a, all_b = exchange(y, move_a), exchange(y, move_b)

time: 83 us -> 82.6 us (level)
  waiting for transfers between devices: 25.8 us -> 24.6 us
    ppermute x8, waiting for transfers between devices: 20.4 us -> 19.2 us  [exchange(): return lax.ppermute(x, ('dp', 'atom'), route)]
where the time goes in v7:
time: 82.6 us; the launch traced here: 82.4 us
  Pallas kernels  28.2 us (34%)
  waiting for transfers between devices  24.6 us (30%)
  starting transfers between devices  24.4 us (30%)
  local copies, waits for them, and re-layouts  1.93 us (2%)
  between operations  1.84 us (2%)
  other arithmetic  1.43 us (2%)
    pallas_call x8, Pallas kernels, call(): pl.pallas_call(kernel, grid=(1,), out_shape=outs, in_specs=in_specs, out_...  28.2 us
    ppermute x8, waiting for transfers between devices, exchange(): return lax.ppermute(x, ('dp', 'atom'), route)  19.2 us
    ppermute x8, starting transfers between devices, exchange(): return lax.ppermute(x, ('dp', 'atom'), route)  10.6 us
    ppermute x3, starting transfers between devices, side_two(): lax.ppermute(x, axis, [(i, (i + 1) % size if i % 2 else (i - 1) % size) f...  10.3 us
    ppermute x4, waiting for transfers between devices, swap(): lax.ppermute(x, axis, [(i, i ^ bit) for i in range(lax.axis_size(axis))])  4.54 us
    ppermute x3, starting transfers between devices, side_one(): lax.ppermute(x, axis, [(i, i ^ 1) for i in range(lax.axis_size(axis))])  3.25 us
    unnamed x24, local copies, waits for them, and re-layouts  1.88 us
  transfers between devices with their start and end apart: 18, of which 12 were waited for; matrix products, arithmetic and copies ran while one was open for 0% of the time, Pallas kernels for 18%

profile of v7, /device:TPU:0, one launch (start us, length us, event | category | flops | bytes accessed | tf_op | source)
XLA Modules:
  0.0 82.4 jit_solution(3313161709980634312)
XLA Ops:
  0.7 0.8 convert_add_fusion.own_ref
  1.4 3.0 %collective-permute-start = (f32[8,128]{1,0:T(8,128)S(1)}, f32[8,128]{1,0:T(8,128)S(1)}, u32[]{:S(2)}, u32[]{:S(2)}) collective-permute-start(f32[8,128]{1,0:T(8,128)S(1)} %convert_add_fusion.own_ref), channel_id=1, source_target_pairs={{0,1},{1,0},{2,3},{3,2},{4,5},{5,4},{6,7},{7,6},{8,9},{9,8},{10,11... | collective-permute-start | bytes 12296 | tf_op jit(solution)/shard_map/ppermute | solution.py:684
  4.4 3.5 %collective-permute-start.1 = (f32[8,128]{1,0:T(8,128)S(1)}, f32[8,128]{1,0:T(8,128)S(1)}, u32[]{:S(2)}, u32[]{:S(2)}) collective-permute-start(f32[8,128]{1,0:T(8,128)S(1)} %convert_add_fusion.own_ref), channel_id=1, source_target_pairs={{0,7},{1,2},{2,1},{3,4},{4,3},{5,6},{6,5},{7,0},{8,15},{9,10},{10,... | collective-permute-start | bytes 12296 | tf_op jit(solution)/shard_map/ppermute | solution.py:689
  7.9 1.0 %copy-done.1 = f32[2,128,384]{2,1,0:T(8,128)S(1)} copy-done((f32[2,128,384]{2,1,0:T(8,128)S(1)}, f32[2,128,384]{2,1,0:T(8,128)}, u32[]{:S(2)}) %copy-start.1) | copy-done | bytes 393240
  8.9 0.8 %copy-done.5 = f32[2,64,128]{2,1,0:T(8,128)S(1)} copy-done((f32[2,64,128]{2,1,0:T(8,128)S(1)}, f32[2,64,128]{2,1,0:T(8,128)}, u32[]{:S(2)}) %copy-start.5) | copy-done | bytes 65560
  9.8 0.0 copy-start.7
  9.8 0.0 copy-start.9
  9.8 0.0 copy-start.10
  9.8 0.3 prepare.1
  10.1 0.1 pad_add_fusion.par_ref
  11.0 4.5 %layer_one.1 = (f32[32,8,128]{2,1,0:T(8,128)S(1)}, f32[4,128,128]{2,1,0:T(8,128)S(1)}, f32[4,128,128]{2,1,0:T(8,128)S(1)}, f32[6,128,128]{2,1,0:T(8,128)S(1)}, f...) custom-call(s32[4]{0:T(128)S(1)} %pad_add_fusion.par_ref, ...), custom_call_target="tpu_custom_call" | custom-call | flops 3000000000 | bytes 6000000 | tf_op jit(solution)/shard_map/layer_one/pallas_call | solution.py:722
  15.5 0.1 collective-permute-start.2
  15.5 3.4 %collective-permute-start.3 = (f32[128,128]{1,0:T(8,128)S(1)}, f32[128,128]{1,0:T(8,128)S(1)}, u32[]{:S(2)}, u32[]{:S(2)}) collective-permute-start(f32[128,128]{1,0:T(8,128)S(1)} %get-tuple-element.68), channel_id=1, source_target_pairs={{0,7},{1,2},{2,1},{3,4},{4,3},{5,6},{6,5},{7,0},{8,15},{9,10},{10,... | collective-permute-start | bytes 196616 | tf_op jit(solution)/shard_map/ppermute | solution.py:689
  18.9 2.8 %radial_two.1 = (f32[2,384,2048]{2,1,0:T(8,128)S(1)}, bf16[2,256,2048]{2,1,0:T(8,128)(2,1)S(1)}, bf16[2,128,2048]{2,1,0:T(8,128)(2,1)S(1)}, f32[2,128,2048]{2,1,0:T(8,128)S(1)}) custom-call(f32[32,8,128]{2,1,0:T(8,128)S(1)} %get-tuple-element.65.geom_ref, bf16[128,256]{1,0:T(8,128)(2,1)S(1)} %get-tuple-element.69.ri4, bf16[384,384]{1,0:T(8,128)(2,1)S(1)} %get-tuple-element.70.ro3), custom_call_target="tpu_custom_call" | custom-call | flops 3000000000 | bytes 6000000 | tf_op jit(solution)/shard_map/radial_two/pallas_call | solution.py:722
  21.7 0.9 %collective-permute-done.3.b_ref = f32[128,128]{1,0:T(8,128)S(1)} collective-permute-done((f32[128,128]{1,0:T(8,128)S(1)}, f32[128,128]{1,0:T(8,128)S(1)}, u32[]{:S(2)}, u32[]{:S(2)}) %collective-permute-start.3) | collective-permute-done | bytes 65568 | tf_op jit(solution)/shard_map/ppermute | solution.py:689
  22.6 6.8 %layer_two.1 = (f32[4,128,128]{2,1,0:T(8,128)S(1)}, f32[136,128]{1,0:T(8,128)S(1)}, f32[128,128]{1,0:T(8,128)S(1)}, f32[448,128]{1,0:T(8,128)S(1)}, f32[72,128]{...) custom-call(s32[4]{0:T(128)S(1)} %pad_add_fusion.par_ref, ...), custom_call_target="tpu_custom_call" | custom-call | flops 5000000000 | bytes 10000000 | tf_op jit(solution)/shard_map/layer_two/pallas_call | solution.py:722
  29.4 0.2 collective-permute-start.4
  29.6 2.6 %radial_two_back.1 = (f32[16,8,128]{2,1,0:T(8,128)S(1)}, f32[384,256]{1,0:T(8,128)S(1)}, f32[128,128]{1,0:T(8,128)S(1)}) custom-call(f32[32,8,128]{2,1,0:T(8,128)S(1)} %get-tuple-element.65.geom_ref, f32[2,384,2048]{2,1,0:T(8,128)S(1)} %get-tuple-element.71.filters_ref, bf16[2,256,2048]{2,1,0:T(8,128)(2,1)S(1)} %get-tuple-element.73.hidden_ref, ...), custom_call_target="tpu_custom_call" | custom-call | flops 3000000000 | bytes 6000000 | tf_op jit(solution)/shard_map/radial_two_back/pallas_call | solution.py:722
  32.1 3.4 %collective-permute-start.7 = (f32[128,128]{1,0:T(8,128)S(1)}, f32[128,128]{1,0:T(8,128)S(1)}, u32[]{:S(2)}, u32[]{:S(2)}) collective-permute-start(f32[128,128]{1,0:T(8,128)S(1)} %get-tuple-element.91), channel_id=1, source_target_pairs={{0,7},{1,2},{2,1},{3,4},{4,3},{5,6},{6,5},{7,0},{8,15},{9,10},{10,... | collective-permute-start | bytes 196616 | tf_op jit(solution)/shard_map/ppermute | solution.py:689
  35.5 0.0 collective-permute-start.5
  35.6 2.6 %radial_two_back_last.1 = (f32[16,8,128]{2,1,0:T(8,128)S(1)}, f32[896,128]{1,0:T(8,128)S(1)}) custom-call(f32[32,8,128]{2,1,0:T(8,128)S(1)} %get-tuple-element.65.geom_ref, f32[2,384,2048]{2,1,0:T(8,128)S(1)} %get-tuple-element.71.filters_ref, bf16[2,256,2048]{2,1,0:T(8,128)(2,1)S(1)} %get-tuple-element.73.hidden_ref, ...), custom_call_target="tpu_custom_call" | custom-call | flops 3000000000 | bytes 6000000 | tf_op jit(solution)/shard_map/radial_two_back_last/pallas_call | solution.py:722
  38.2 1.0 %collective-permute-done.5 = f32[8,128]{1,0:T(8,128)S(1)} collective-permute-done((f32[8,128]{1,0:T(8,128)S(1)}, f32[8,128]{1,0:T(8,128)S(1)}, u32[]{:S(2)}, u32[]{:S(2)}) %collective-permute-start.5) | collective-permute-done | bytes 4128 | tf_op jit(solution)/shard_map/ppermute | solution.py:697
  39.1 0.2 collective-permute-start.6
  39.3 7.0 %layer_one_back.1 = (f32[16,128]{1,0:T(8,128)S(1)}, f32[16,128]{1,0:T(8,128)S(1)}, f32[896,128]{1,0:T(8,128)S(1)}) custom-call(s32[4]{0:T(128)S(1)} %pad_add_fusion.par_ref, f32[32,8,128]{2,1,0:T(8,128)S(1)} %get-tuple-element.65.geom_ref, f32[16,8,128]{2,1,0:T(8,128)S(1)} %get-tuple-element.86.dgeom_one, f32[16,8,128]{2,1,0:T(8,128)S(1)} %get-tuple-element.84.dgeom_two, ...), custom_call_target="tpu_custom_call" | custom-call | flops 6000000000 | bytes 12000000 | tf_op jit(solution)/shard_map/layer_one_back/pallas_call | solution.py:722
  46.3 0.0 collective-permute-done.6
  46.4 0.2 multiply_select_fusion
  46.6 0.1 collective-permute-start.8
  46.7 1.8 %collective-permute-done.8 = f32[896,128]{1,0:T(8,128)S(1)} collective-permute-done((f32[896,128]{1,0:T(8,128)S(1)}, f32[896,128]{1,0:T(8,128)S(1)}, u32[]{:S(2)}, u32[]{:S(2)}) %collective-permute-start.8) | collective-permute-done | bytes 458784 | tf_op jit(solution)/shard_map/ppermute | solution.py:697
  48.4 0.2 select_add_fusion
  48.7 2.3 %collective-permute-start.10 = (f32[240,128]{1,0:T(8,128)S(1)}, f32[240,128]{1,0:T(8,128)S(1)}, u32[]{:S(2)}, u32[]{:S(2)}) collective-permute-start(f32[240,128]{1,0:T(8,128)S(1)} %get-tuple-element.122), channel_id=1, source_target_pairs={{0,1},{1,0},{2,3},{3,2},{4,5},{5,4},{6,7},{7,6},{8,24},{9,25},{10,... | collective-permute-start | bytes 368648 | tf_op jit(solution)/shard_map/ppermute | solution.py:742
  51.1 1.5 %collective-permute-start.9 = (f32[240,128]{1,0:T(8,128)S(1)}, f32[240,128]{1,0:T(8,128)S(1)}, u32[]{:S(2)}, u32[]{:S(2)}) collective-permute-start(f32[240,128]{1,0:T(8,128)S(1)} %get-tuple-element.123), channel_id=1, source_target_pairs={{0,16},{1,17},{2,18},{3,19},{4,20},{5,21},{6,22},{7,23},{8,9},{9,8... | collective-permute-start | bytes 368648 | tf_op jit(solution)/shard_map/ppermute | solution.py:742
  52.6 0.0 collective-permute-start.11
  52.6 2.6 %collective-permute-done.10 = f32[240,128]{1,0:T(8,128)S(1)} collective-permute-done((f32[240,128]{1,0:T(8,128)S(1)}, f32[240,128]{1,0:T(8,128)S(1)}, u32[]{:S(2)}, u32[]{:S(2)}) %collective-permute-start.10) | collective-permute-done | bytes 122912 | tf_op jit(solution)/shard_map/ppermute | solution.py:742
  55.2 1.7 %collective-permute-done.9 = f32[240,128]{1,0:T(8,128)S(1)} collective-permute-done((f32[240,128]{1,0:T(8,128)S(1)}, f32[240,128]{1,0:T(8,128)S(1)}, u32[]{:S(2)}, u32[]{:S(2)}) %collective-permute-start.9) | collective-permute-done | bytes 122912 | tf_op jit(solution)/shard_map/ppermute | solution.py:742
  57.0 1.3 %collective-permute-done.11 = f32[224,128]{1,0:T(8,128)S(1)} collective-permute-done((f32[224,128]{1,0:T(8,128)S(1)}, f32[224,128]{1,0:T(8,128)S(1)}, u32[]{:S(2)}, u32[]{:S(2)}) %collective-permute-start.11) | collective-permute-done | bytes 114720 | tf_op jit(solution)/shard_map/ppermute | solution.py:742
  58.4 1.2 %collective-permute-start.12 = (f32[232,128]{1,0:T(8,128)S(1)}, f32[232,128]{1,0:T(8,128)S(1)}, u32[]{:S(2)}, u32[]{:S(2)}) collective-permute-start(f32[232,128]{1,0:T(8,128)S(1)} %pad_maximum_fusion.4), channel_id=1, source_target_pairs={{0,2},{1,3},{2,0},{3,1},{4,6},{5,7},{6,4},{7,5},{8,10},{9,11},{10,... | collective-permute-start | bytes 356360 | tf_op jit(solution)/shard_map/ppermute | solution.py:742
  59.6 3.7 %collective-permute-done.12 = f32[232,128]{1,0:T(8,128)S(1)} collective-permute-done((f32[232,128]{1,0:T(8,128)S(1)}, f32[232,128]{1,0:T(8,128)S(1)}, u32[]{:S(2)}, u32[]{:S(2)}) %collective-permute-start.12) | collective-permute-done | bytes 118816 | tf_op jit(solution)/shard_map/ppermute | solution.py:742
  63.3 2.0 %collective-permute-start.13 = (f32[240,128]{1,0:T(8,128)S(1)}, f32[240,128]{1,0:T(8,128)S(1)}, u32[]{:S(2)}, u32[]{:S(2)}) collective-permute-start(f32[240,128]{1,0:T(8,128)S(1)} %pad_maximum_fusion.3), channel_id=1, source_target_pairs={{0,4},{1,5},{2,6},{3,7},{4,0},{5,1},{6,2},{7,3},{8,12},{9,13},{10,... | collective-permute-start | bytes 368648 | tf_op jit(solution)/shard_map/ppermute | solution.py:742
  65.3 5.2 %collective-permute-done.13 = f32[240,128]{1,0:T(8,128)S(1)} collective-permute-done((f32[240,128]{1,0:T(8,128)S(1)}, f32[240,128]{1,0:T(8,128)S(1)}, u32[]{:S(2)}, u32[]{:S(2)}) %collective-permute-start.13) | collective-permute-done | bytes 122912 | tf_op jit(solution)/shard_map/ppermute | solution.py:742
  70.5 1.6 %collective-permute-start.14 = (f32[224,128]{1,0:T(8,128)S(1)}, f32[224,128]{1,0:T(8,128)S(1)}, u32[]{:S(2)}, u32[]{:S(2)}) collective-permute-start(f32[224,128]{1,0:T(8,128)S(1)} %slice_add_fusion), channel_id=1, source_target_pairs={{0,16},{1,17},{2,18},{3,19},{4,20},{5,21},{6,22},{7,23},{8,9},{9,8... | collective-permute-start | bytes 344072 | tf_op jit(solution)/shard_map/ppermute | solution.py:742
  72.1 0.9 %collective-permute-start.15 = (f32[224,128]{1,0:T(8,128)S(1)}, f32[224,128]{1,0:T(8,128)S(1)}, u32[]{:S(2)}, u32[]{:S(2)}) collective-permute-start(f32[224,128]{1,0:T(8,128)S(1)} %slice_add_fusion), channel_id=1, source_target_pairs={{0,1},{1,0},{2,3},{3,2},{4,5},{5,4},{6,7},{7,6},{8,24},{9,25},{10,... | collective-permute-start | bytes 344072 | tf_op jit(solution)/shard_map/ppermute | solution.py:742
  72.9 1.1 %collective-permute-start.16 = (f32[224,128]{1,0:T(8,128)S(1)}, f32[224,128]{1,0:T(8,128)S(1)}, u32[]{:S(2)}, u32[]{:S(2)}) collective-permute-start(f32[224,128]{1,0:T(8,128)S(1)} %slice_add_fusion), channel_id=1, source_target_pairs={{0,17},{1,16},{2,19},{3,18},{4,21},{5,20},{6,23},{7,22},{8,25},{9,... | collective-permute-start | bytes 344072 | tf_op jit(solution)/shard_map/ppermute | solution.py:742
  74.1 1.3 %collective-permute-done.14 = f32[224,128]{1,0:T(8,128)S(1)} collective-permute-done((f32[224,128]{1,0:T(8,128)S(1)}, f32[224,128]{1,0:T(8,128)S(1)}, u32[]{:S(2)}, u32[]{:S(2)}) %collective-permute-start.14) | collective-permute-done | bytes 114720 | tf_op jit(solution)/shard_map/ppermute | solution.py:742
  75.4 1.5 %collective-permute-done.15 = f32[224,128]{1,0:T(8,128)S(1)} collective-permute-done((f32[224,128]{1,0:T(8,128)S(1)}, f32[224,128]{1,0:T(8,128)S(1)}, u32[]{:S(2)}, u32[]{:S(2)}) %collective-permute-start.15) | collective-permute-done | bytes 114720 | tf_op jit(solution)/shard_map/ppermute | solution.py:742
  76.9 1.7 %collective-permute-done.16 = f32[224,128]{1,0:T(8,128)S(1)} collective-permute-done((f32[224,128]{1,0:T(8,128)S(1)}, f32[224,128]{1,0:T(8,128)S(1)}, u32[]{:S(2)}, u32[]{:S(2)}) %collective-permute-start.16) | collective-permute-done | bytes 114720 | tf_op jit(solution)/shard_map/ppermute | solution.py:742
  78.7 0.1 collective-permute-start.17
  78.8 1.8 %collective-permute-done.17.other_turned = f32[896,128]{1,0:T(8,128)S(1)} collective-permute-done((f32[896,128]{1,0:T(8,128)S(1)}, f32[896,128]{1,0:T(8,128)S(1)}, u32[]{:S(2)}, u32[]{:S(2)}) %collective-permute-start.17) | collective-permute-done | bytes 458784 | tf_op jit(solution)/shard_map/ppermute | solution.py:697
  80.5 1.7 %final.1 = (f32[1,1]{1,0:T(1,128)}, f32[3,128]{1,0:T(4,128)}, f32[3,1,3]{2,1,0:T(1,128)}, f32[96,128]{1,0:T(8,128)}, f32[2,64,128]{2,1,0:T(8,128)}, /*index=5*/f...) custom-call(s32[4]{0:T(128)S(1)} %pad_add_fusion.par_ref, ...), custom_call_target="tpu_custom_call" | custom-call | flops 100000000 | bytes 200000 | tf_op jit(solution)/shard_map/final/pallas_call | solution.py:722
  (44 shorter events, 0.3 us)
Async XLA Ops:
  1.4 9.5 %collective-permute-start = (f32[8,128]{1,0:T(8,128)S(1)}, f32[8,128]{1,0:T(8,128)S(1)}, u32[]{:S(2)}, u32[]{:S(2)}) collective-permute-start(f32[8,128]{1,0:T(8,128)S(1)} %convert_add_fusion.own_ref), channel_id=1, source_target_pairs={{0,1},{1,0},{2,3},{3,2},{4,5},{5,4},{6,7},{7,6},{8,9},{9,8},{10,11... | collective-permute-start | bytes 12296 | tf_op jit(solution)/shard_map/ppermute | solution.py:684
  4.4 6.5 %collective-permute-start.1 = (f32[8,128]{1,0:T(8,128)S(1)}, f32[8,128]{1,0:T(8,128)S(1)}, u32[]{:S(2)}, u32[]{:S(2)}) collective-permute-start(f32[8,128]{1,0:T(8,128)S(1)} %convert_add_fusion.own_ref), channel_id=1, source_target_pairs={{0,7},{1,2},{2,1},{3,4},{4,3},{5,6},{6,5},{7,0},{8,15},{9,10},{10,... | collective-permute-start | bytes 12296 | tf_op jit(solution)/shard_map/ppermute | solution.py:689
  7.9 1.0 %copy-start.1 = (f32[2,128,384]{2,1,0:T(8,128)S(1)}, f32[2,128,384]{2,1,0:T(8,128)}, u32[]{:S(2)}) copy-start(f32[2,128,384]{2,1,0:T(8,128)} %rout_ref.1) | copy-start | bytes 1179652
  8.9 0.8 %copy-start.5 = (f32[2,64,128]{2,1,0:T(8,128)S(1)}, f32[2,64,128]{2,1,0:T(8,128)}, u32[]{:S(2)}) copy-start(f32[2,64,128]{2,1,0:T(8,128)} %rin_ref.1) | copy-start | bytes 196612
  9.8 1.1 %copy-start = (f32[1,3,3]{2,0,1:T(1,128)S(1)}, f32[1,3,3]{2,0,1:T(1,128)}, u32[]{:S(2)}) copy-start(f32[1,3,3]{2,0,1:T(1,128)} %param.20) | copy-start | bytes 112
  9.8 1.1 %copy-start.2 = (f32[2,128,128]{2,1,0:T(8,128)S(1)}, f32[2,128,128]{2,1,0:T(8,128)}, u32[]{:S(2)}) copy-start(f32[2,128,128]{2,1,0:T(8,128)} %sm_ref.5) | copy-start | bytes 393220
  9.8 1.1 %copy-start.3 = (f32[2,128,128]{2,1,0:T(8,128)S(1)}, f32[2,128,128]{2,1,0:T(8,128)}, u32[]{:S(2)}) copy-start(f32[2,128,128]{2,1,0:T(8,128)} %vm_ref.5) | copy-start | bytes 393220
  9.8 1.2 %copy-start.4 = (f32[2,128,128]{2,1,0:T(8,128)S(1)}, f32[2,128,128]{2,1,0:T(8,128)}, u32[]{:S(2)}) copy-start(f32[2,128,128]{2,1,0:T(8,128)} %vg_ref.5) | copy-start | bytes 393220
  9.8 1.2 %copy-start.7 = (s32[3,32,128]{2,1,0:T(8,128)S(1)}, s32[3,32,128]{2,1,0:T(8,128)}, u32[]{:S(2)}) copy-start(s32[3,32,128]{2,1,0:T(8,128)} %shift_ref.1) | copy-start | bytes 147460
  9.8 1.2 %copy-start.8 = (f32[96,128]{1,0:T(8,128)S(1)}, f32[96,128]{1,0:T(8,128)}, u32[]{:S(2)}) copy-start(f32[96,128]{1,0:T(8,128)} %emb_ref.3) | copy-start | bytes 147460
  9.8 1.2 %copy-start.9 = (s32[32,128]{1,0:T(8,128)S(1)}, s32[32,128]{1,0:T(8,128)}, u32[]{:S(2)}) copy-start(s32[32,128]{1,0:T(8,128)} %nb_ref.1) | copy-start | bytes 49156
  9.8 1.2 %copy-start.10 = (s32[128]{0:T(128)S(1)}, s32[128]{0:T(128)}, u32[]{:S(2)}) copy-start(s32[128]{0:T(128)} %param.18) | copy-start | bytes 1540
  15.5 6.2 %collective-permute-start.2 = (f32[128,128]{1,0:T(8,128)S(1)}, f32[128,128]{1,0:T(8,128)S(1)}, u32[]{:S(2)}, u32[]{:S(2)}) collective-permute-start(f32[128,128]{1,0:T(8,128)S(1)} %get-tuple-element.67), channel_id=1, source_target_pairs={{0,1},{1,0},{2,3},{3,2},{4,5},{5,4},{6,7},{7,6},{8,9},{9,8},{10,11... | collective-permute-start | bytes 196616 | tf_op jit(solution)/shard_map/ppermute | solution.py:684
  15.5 7.0 %collective-permute-start.3 = (f32[128,128]{1,0:T(8,128)S(1)}, f32[128,128]{1,0:T(8,128)S(1)}, u32[]{:S(2)}, u32[]{:S(2)}) collective-permute-start(f32[128,128]{1,0:T(8,128)S(1)} %get-tuple-element.68), channel_id=1, source_target_pairs={{0,7},{1,2},{2,1},{3,4},{4,3},{5,6},{6,5},{7,0},{8,15},{9,10},{10,... | collective-permute-start | bytes 196616 | tf_op jit(solution)/shard_map/ppermute | solution.py:689
  18.9 3.7 %copy-start.6 = (f32[128,128]{1,0:T(8,128)S(1)}, f32[128,128]{1,0:T(8,128)}, u32[]{:S(2)}) copy-start(f32[128,128]{1,0:T(8,128)} %mid_ref.1) | copy-start | bytes 196612
  18.9 3.7 %copy-start.11 = (f32[128]{0:T(128)S(1)}, f32[128]{0:T(128)}, u32[]{:S(2)}) copy-start(f32[128]{0:T(128)} %param.29) | copy-start | bytes 1540
  29.4 6.2 %collective-permute-start.4 = (f32[136,128]{1,0:T(8,128)S(1)}, f32[136,128]{1,0:T(8,128)S(1)}, u32[]{:S(2)}, u32[]{:S(2)}) collective-permute-start(f32[136,128]{1,0:T(8,128)S(1)} %get-tuple-element.72), channel_id=1, source_target_pairs={{0,1},{1,0},{2,3},{3,2},{4,5},{5,4},{6,7},{7,6},{8,9},{9,8},{10,11... | collective-permute-start | bytes 208904 | tf_op jit(solution)/shard_map/ppermute | solution.py:684
  32.1 7.2 %collective-permute-start.7 = (f32[128,128]{1,0:T(8,128)S(1)}, f32[128,128]{1,0:T(8,128)S(1)}, u32[]{:S(2)}, u32[]{:S(2)}) collective-permute-start(f32[128,128]{1,0:T(8,128)S(1)} %get-tuple-element.91), channel_id=1, source_target_pairs={{0,7},{1,2},{2,1},{3,4},{4,3},{5,6},{6,5},{7,0},{8,15},{9,10},{10,... | collective-permute-start | bytes 196616 | tf_op jit(solution)/shard_map/ppermute | solution.py:689
  35.5 3.6 %collective-permute-start.5 = (f32[8,128]{1,0:T(8,128)S(1)}, f32[8,128]{1,0:T(8,128)S(1)}, u32[]{:S(2)}, u32[]{:S(2)}) collective-permute-start(f32[8,128]{1,0:T(8,128)S(1)} %slice_add_fusion.4), channel_id=1, source_target_pairs={{0,2},{1,3},{2,0},{3,1},{4,6},{5,7},{6,4},{7,5},{8,10},{9,11},{10,... | collective-permute-start | bytes 12296 | tf_op jit(solution)/shard_map/ppermute | solution.py:697
  39.1 7.2 %collective-permute-start.6 = (f32[8,128]{1,0:T(8,128)S(1)}, f32[8,128]{1,0:T(8,128)S(1)}, u32[]{:S(2)}, u32[]{:S(2)}) collective-permute-start(f32[8,128]{1,0:T(8,128)S(1)} %add.77), channel_id=1, source_target_pairs={{0,4},{1,5},{2,6},{3,7},{4,0},{5,1},{6,2},{7,3},{8,12},{9,13},{10,... | collective-permute-start | bytes 12296 | tf_op jit(solution)/shard_map/ppermute | solution.py:697
  46.6 1.9 %collective-permute-start.8 = (f32[896,128]{1,0:T(8,128)S(1)}, f32[896,128]{1,0:T(8,128)S(1)}, u32[]{:S(2)}, u32[]{:S(2)}) collective-permute-start(f32[896,128]{1,0:T(8,128)S(1)} %multiply_select_fusion), channel_id=1, source_target_pairs={{0,8},{8,0},{16,24},{24,16},{1,9},{9,1},{17,25},{25,17},{2,10},{10... | collective-permute-start | bytes 1376264 | tf_op jit(solution)/shard_map/ppermute | solution.py:697
  48.7 6.5 %collective-permute-start.10 = (f32[240,128]{1,0:T(8,128)S(1)}, f32[240,128]{1,0:T(8,128)S(1)}, u32[]{:S(2)}, u32[]{:S(2)}) collective-permute-start(f32[240,128]{1,0:T(8,128)S(1)} %get-tuple-element.122), channel_id=1, source_target_pairs={{0,1},{1,0},{2,3},{3,2},{4,5},{5,4},{6,7},{7,6},{8,24},{9,25},{10,... | collective-permute-start | bytes 368648 | tf_op jit(solution)/shard_map/ppermute | solution.py:742
  51.1 5.9 %collective-permute-start.9 = (f32[240,128]{1,0:T(8,128)S(1)}, f32[240,128]{1,0:T(8,128)S(1)}, u32[]{:S(2)}, u32[]{:S(2)}) collective-permute-start(f32[240,128]{1,0:T(8,128)S(1)} %get-tuple-element.123), channel_id=1, source_target_pairs={{0,16},{1,17},{2,18},{3,19},{4,20},{5,21},{6,22},{7,23},{8,9},{9,8... | collective-permute-start | bytes 368648 | tf_op jit(solution)/shard_map/ppermute | solution.py:742
  52.6 5.7 %collective-permute-start.11 = (f32[224,128]{1,0:T(8,128)S(1)}, f32[224,128]{1,0:T(8,128)S(1)}, u32[]{:S(2)}, u32[]{:S(2)}) collective-permute-start(f32[224,128]{1,0:T(8,128)S(1)} %get-tuple-element.115), channel_id=1, source_target_pairs={{0,17},{1,16},{2,19},{3,18},{4,21},{5,20},{6,23},{7,22},{8,25},{9,... | collective-permute-start | bytes 344072 | tf_op jit(solution)/shard_map/ppermute | solution.py:742
  58.4 4.9 %collective-permute-start.12 = (f32[232,128]{1,0:T(8,128)S(1)}, f32[232,128]{1,0:T(8,128)S(1)}, u32[]{:S(2)}, u32[]{:S(2)}) collective-permute-start(f32[232,128]{1,0:T(8,128)S(1)} %pad_maximum_fusion.4), channel_id=1, source_target_pairs={{0,2},{1,3},{2,0},{3,1},{4,6},{5,7},{6,4},{7,5},{8,10},{9,11},{10,... | collective-permute-start | bytes 356360 | tf_op jit(solution)/shard_map/ppermute | solution.py:742
  63.3 7.2 %collective-permute-start.13 = (f32[240,128]{1,0:T(8,128)S(1)}, f32[240,128]{1,0:T(8,128)S(1)}, u32[]{:S(2)}, u32[]{:S(2)}) collective-permute-start(f32[240,128]{1,0:T(8,128)S(1)} %pad_maximum_fusion.3), channel_id=1, source_target_pairs={{0,4},{1,5},{2,6},{3,7},{4,0},{5,1},{6,2},{7,3},{8,12},{9,13},{10,... | collective-permute-start | bytes 368648 | tf_op jit(solution)/shard_map/ppermute | solution.py:742
  70.5 4.9 %collective-permute-start.14 = (f32[224,128]{1,0:T(8,128)S(1)}, f32[224,128]{1,0:T(8,128)S(1)}, u32[]{:S(2)}, u32[]{:S(2)}) collective-permute-start(f32[224,128]{1,0:T(8,128)S(1)} %slice_add_fusion), channel_id=1, source_target_pairs={{0,16},{1,17},{2,18},{3,19},{4,20},{5,21},{6,22},{7,23},{8,9},{9,8... | collective-permute-start | bytes 344072 | tf_op jit(solution)/shard_map/ppermute | solution.py:742
  72.1 4.8 %collective-permute-start.15 = (f32[224,128]{1,0:T(8,128)S(1)}, f32[224,128]{1,0:T(8,128)S(1)}, u32[]{:S(2)}, u32[]{:S(2)}) collective-permute-start(f32[224,128]{1,0:T(8,128)S(1)} %slice_add_fusion), channel_id=1, source_target_pairs={{0,1},{1,0},{2,3},{3,2},{4,5},{5,4},{6,7},{7,6},{8,24},{9,25},{10,... | collective-permute-start | bytes 344072 | tf_op jit(solution)/shard_map/ppermute | solution.py:742
  72.9 5.7 %collective-permute-start.16 = (f32[224,128]{1,0:T(8,128)S(1)}, f32[224,128]{1,0:T(8,128)S(1)}, u32[]{:S(2)}, u32[]{:S(2)}) collective-permute-start(f32[224,128]{1,0:T(8,128)S(1)} %slice_add_fusion), channel_id=1, source_target_pairs={{0,17},{1,16},{2,19},{3,18},{4,21},{5,20},{6,23},{7,22},{8,25},{9,... | collective-permute-start | bytes 344072 | tf_op jit(solution)/shard_map/ppermute | solution.py:742
  78.7 1.9 %collective-permute-start.17 = (f32[896,128]{1,0:T(8,128)S(1)}, f32[896,128]{1,0:T(8,128)S(1)}, u32[]{:S(2)}, u32[]{:S(2)}) collective-permute-start(f32[896,128]{1,0:T(8,128)S(1)} %pad_maximum_fusion.mine_turned), channel_id=1, source_target_pairs={{0,8},{8,0},{16,24},{24,16},{1,9},{9,1},{17,25},{25,17},{2,10},{10... | collective-permute-start | bytes 1376264 | tf_op jit(solution)/shard_map/ppermute | solution.py:697
